TPU v7x, 128 devices: a whole 4x4x4 slice. The times are simulated.
128 devices in a mesh: pair: 8 (over x, z_lo), row: 4 (over z_hi, core), col: 4 (over y).
Axes of the slice: x: 4, y: 4, z: 4 (z_hi: 2, z_lo: 2; z = z_hi * 2 + z_lo), core: 2. Of those that a mesh axis runs over, the one named last changes fastest.
Arguments:
- valence_index: int32 [4096], P(('pair', 'row', 'col')), may hold values from 0 to 63, as said below
- conduction_index: int32 [4096], P(('pair', 'row', 'col')), may hold values from 0 to 63
- valence_waves: bfloat16 [64, 2, 32768], replicated, may hold values from -6 to 6
- conduction_waves: bfloat16 [64, 2, 32768], replicated, may hold values from -6 to 6
- valence_energy: float32 [64], replicated, may hold values from -1 to -0.05
- conduction_energy: float32 [64], replicated, may hold values from 0.05 to 1
- frequency: float32 [1], replicated, may hold values from 0.2 to 1
- sphere_map: int32 [8192], replicated, may hold values from 0 to 32767, as said below
Outputs:
- chi_zero: float32 [8192, 2, 8192], P(('pair', 'row'), None, 'col')
Inputs may be any that keep to these rules, and one draw needn't show every extreme that they name: The pairs (valence_index[p], conduction_index[p]) are all different. `sphere_map`: all entries are different.
All inputs are finite; a program needn't handle non-finite values.
Results may differ from a plain program's by a relative error of at most 0.011.
Values may be sent and summed in bfloat16 or wider, within the bound.
No kernel may reach another device: no remote copies, remote signals or barrier semaphores. Data moves between devices by JAX's collectives and lax.ppermute only.
A program may use at most 192 MiB of HBM per device.

v0:
```python
import math

import jax
import jax.numpy as jnp
from jax import lax
from jax.sharding import PartitionSpec as P

GRID = 32


def transform(field):
    extent = field.shape[2]
    indices = lax.iota(jnp.int32, extent)
    phase = indices[:, None] * indices[None, :] % extent
    angle = phase.astype(jnp.float32) * (2.0 * math.pi / extent)
    cosines = jnp.cos(angle)
    sines = jnp.sin(angle)
    table = jnp.stack([jnp.stack([cosines, sines], 0), jnp.stack([-sines, cosines], 0)], 0)
    for pattern in ("nixyz,oikx->nokyz", "nixyz,oiky->noxkz", "nixyz,oikz->noxyk"):
        field = jnp.einsum(pattern, field, table, precision=lax.Precision.HIGHEST)
    return field


def pair_densities(valence_index, conduction_index, valence_waves, conduction_waves, sphere_map):
    valence = jnp.take(valence_waves, valence_index, axis=0).astype(jnp.float32)
    conduction = jnp.take(conduction_waves, conduction_index, axis=0).astype(jnp.float32)
    real_part = valence[:, 0] * conduction[:, 0] + valence[:, 1] * conduction[:, 1]
    imag_part = valence[:, 0] * conduction[:, 1] - valence[:, 1] * conduction[:, 0]
    local_pairs = real_part.shape[0]
    field = jnp.stack([real_part, imag_part], 1).reshape(local_pairs, 2, GRID, GRID, GRID)
    field = transform(field).reshape(local_pairs, 2, -1)
    scaling = 1.0 / math.sqrt(GRID**3)
    picked = jnp.take(field, sphere_map, axis=2)
    return (picked * scaling).astype(jnp.bfloat16)


def select_energy(indices, table):
    hits = indices[:, None] == lax.iota(jnp.int32, table.shape[0])[None, :]
    return jnp.sum(jnp.where(hits, table[None, :], 0.0), axis=1)


def stacked(panel):
    negated = jnp.stack([panel[:, 1], -panel[:, 0]], 1)
    return jnp.stack([panel, negated], 0)


def contract(left_slice, right_panel):
    return jnp.einsum("opkr,pkc->roc", left_slice, right_panel, preferred_element_type=jnp.float32)


def local(
    valence_index,
    conduction_index,
    valence_waves,
    conduction_waves,
    valence_energy,
    conduction_energy,
    frequency,
    sphere_map,
):
    local_pairs = valence_index.shape[0]
    pair_devices = lax.axis_size("pair")
    row_devices = lax.axis_size("row")
    col_devices = lax.axis_size("col")
    pair_total = local_pairs * pair_devices * row_devices * col_devices
    density = pair_densities(
        valence_index, conduction_index, valence_waves, conduction_waves, sphere_map
    )
    sphere = density.shape[2]
    energy_gap = select_energy(conduction_index, conduction_energy) - select_energy(
        valence_index, valence_energy
    )
    weights = (
        4.0 * energy_gap / (energy_gap * energy_gap + frequency[0] * frequency[0]) / pair_total
    )
    weighted = (weights[:, None, None] * density.astype(jnp.float32)).astype(jnp.bfloat16)
    widened = lax.all_gather(weighted, "col", axis=0, tiled=True)
    blocks = widened.reshape(
        widened.shape[0], 2, pair_devices, row_devices, sphere // (pair_devices * row_devices)
    )
    row_panel = lax.all_to_all(blocks, "row", split_axis=3, concat_axis=0, tiled=True)
    col_blocks = density.reshape(local_pairs, 2, col_devices, sphere // col_devices)
    col_part = lax.all_to_all(col_blocks, "col", split_axis=2, concat_axis=0, tiled=True)
    col_panel = lax.all_gather(col_part, "row", axis=0, tiled=True)
    col_panel = col_panel.reshape(col_panel.shape[0], 2, sphere // col_devices)
    left_panel = stacked(row_panel.reshape(row_panel.shape[0], 2, -1))
    return lax.psum_scatter(
        contract(left_panel, col_panel), "pair", scatter_dimension=0, tiled=True
    )


def solution(mesh):
    placed = (P(("pair", "row", "col")), P(("pair", "row", "col")), P(), P(), P(), P(), P(), P())
    return jax.shard_map(
        local,
        mesh=mesh,
        in_specs=placed,
        out_specs=P(("pair", "row"), None, "col"),
        check_vma=False,
    )
```

profile of v0, /device:TPU:8, one launch (start us, length us, event | category | flops | bytes accessed | tf_op | source)
XLA Modules:
  0.0 1369.2 jit_solution(4766179192785460582)
XLA Ops:
  10.9 13.5 gather_fusion.1
  24.4 13.5 gather_fusion.2
  38.0 9.3 fusion.14
  47.2 32.4 %add_reduce_fusion = (f32[32,32768]{1,0:T(8,128)}, f32[32,32768]{1,0:T(8,128)}) fusion(f32[32,2,32768]{2,1,0:T(2,128)S(1)} %get-tuple-element.13, f32[32,2,32768]{2,1,0:T(2,128)S(1)} %get-tuple-element.12), kind=kLoop, calls=%fused_computation.24 | loop fusion | flops 6291456 | bytes 25165824 | tf_op jit(solution)/shard_map/add | solution.py:27
  79.7 9.8 stack.43
  89.5 18.7 %copy.62 = f32[32,1,32,32,32]{4,2,1,3,0:T(8,128)} copy(f32[32,1,32,32,32]{4,3,2,0,1:T(8,128)} %stack.43) | data formatting | bytes 8388608 | tf_op jit(solution)/shard_map/stack | solution.py:30
  108.1 9.8 stack.44
  118.0 18.4 %copy.63 = f32[32,1,32,32,32]{4,2,1,3,0:T(8,128)} copy(f32[32,1,32,32,32]{4,3,2,0,1:T(8,128)} %stack.44) | data formatting | bytes 8388608 | tf_op jit(solution)/shard_map/stack | solution.py:30
  136.4 37.2 %fusion.10 = f32[32,2,32,32,32,1]{4,2,3,0,1,5:T(8,128)} fusion(f32[32,1,32,32,32]{4,2,1,3,0:T(8,128)} %copy.63, f32[32,1,32,32,32]{4,2,1,3,0:T(8,128)} %copy.62, f32[1,2,32,32]{3,2,1,0:T(8,128)S(1)} %get-tuple-element.11, f32[1,2,32,32]{3,2,1,0:T(8,128)S(1)} %get-tuple-element.10), kind=kOutput, calls=%fused_computation.12 | convolution fusion | flops 1612713984 | bytes 16793600 | tf_op jit(solution)/shard_map/nixyz,oikx->nokyz/dot_general | solution.py:20
  173.7 67.7 %fusion.5 = f32[2,32,32,32,32,1]{4,1,5,0,3,2:T(8,128)} fusion(f32[32,2,32,32,32,1]{4,2,3,0,1,5:T(8,128)} %fusion.10, f32[1,2,32,32]{3,2,1,0:T(8,128)S(1)} %get-tuple-element.11, f32[1,2,32,32]{3,2,1,0:T(8,128)S(1)} %get-tuple-element.10), kind=kOutput, calls=%fused_computation.9 | convolution fusion | flops 1610616832 | bytes 16793600 | tf_op jit(solution)/shard_map/nixyz,oiky->noxkz/dot_general | solution.py:20
  241.4 86.9 %fusion.7 = f32[32,2,32,32,32]{3,4,2,0,1:T(8,128)} fusion(f32[2,32,32,32,32,1]{4,1,5,0,3,2:T(8,128)} %fusion.5, f32[1,2,32,32]{3,2,1,0:T(8,128)S(1)} %get-tuple-element.11, f32[1,2,32,32]{3,2,1,0:T(8,128)S(1)} %get-tuple-element.10), kind=kOutput, calls=%fused_computation.11 | convolution fusion | flops 1610616832 | bytes 16793600 | tf_op jit(solution)/shard_map/nixyz,oikz->noxyk/dot_general | solution.py:20
  328.3 56.5 %copy.87 = f32[32,2,32,32,32]{0,1,4,3,2:T(2,128)} copy(f32[32,2,32,32,32]{3,4,2,0,1:T(8,128)} %fusion.7) | data formatting | bytes 16777216 | tf_op jit(solution)/shard_map/reshape | solution.py:31
  384.8 126.2 %gather_fusion = f32[8192,32,2]{1,2,0:T(2,128)} fusion(f32[32,2,32768]{0,1,2:T(2,128)} %bitcast.91, s32[8192]{0:T(1024)S(1)} %fusion.24), kind=kCustom, calls=%fused_computation.2 | custom fusion | bytes 4227072 | tf_op jit(solution)/shard_map/jit(_take)/gather | solution.py:33
  511.1 9.5 copy.67
  524.3 21.9 %all_to_all.33 = bf16[32,2,4,2048]{3,0,1,2:T(8,128)(2,1)S(1)} all-to-all(bf16[32,2,4,2048]{3,0,1,2:T(8,128)(2,1)S(1)} %copy.69), channel_id=1, replica_groups=mesh['pair'=8,'row'=4,'col'=4] {'col'}, dimensions={2} | all-to-all | bytes 2097152 | tf_op jit(solution)/shard_map/all_to_all | solution.py:83
  547.7 28.5 %all-gather.5.cloned.1.call-done = bf16[128,2,8192]{2,1,0:T(2,128)(2,1)} async-done(((bf16[32,2,8192]{2,1,0:T(2,128)(2,1)}), bf16[128,2,8192]{2,1,0:T(2,128)(2,1)}) %all-gather.5.cloned.1.call-update) | async-done | bytes 4194320 | tf_op jit(solution)/shard_map/all_gather | solution.py:77
  576.1 11.2 copy.73
  590.1 71.7 %all_to_all.34 = bf16[128,2,8,4,256]{0,4,2,1,3:T(8,128)(2,1)} all-to-all(bf16[128,2,8,4,256]{0,4,2,1,3:T(8,128)(2,1)S(1)} %copy.74), channel_id=1, replica_groups=mesh['pair'=8,'row'=4,'col'=4] {'row'}, dimensions={3} | all-to-all | bytes 8388608 | tf_op jit(solution)/shard_map/all_to_all | solution.py:81
  661.8 7.8 copy.75
  669.7 7.4 reshape.127
  677.0 7.4 stack_reshape.3
  689.3 25.1 %convolution_bitcast_fusion = f32[2048,2,2048]{0,2,1:T(8,128)} fusion(bf16[1,512,2,2048]{3,1,2,0:T(8,128)(2,1)} %maximum_bitcast_fusion.4, bf16[1,512,2,2048]{3,1,2,0:T(8,128)(2,1)} %stack_reshape.3, bf16[512,2,1,2048]{0,3,1,2:T(8,128)(2,1)} %all-gather.3.cloned.1.call-done), kind=kOutput, calls=%fused_computation.13 | convolution fusion | flops 17196646400 | bytes 46137344 | tf_op jit(solution)/shard_map/opkr,pkc->roc/dot_general | solution.py:48
  714.4 640.5 %reduce-scatter.2.cloned.1.call-done = f32[256,2,2048]{0,2,1:T(8,128)} async-done(((f32[2048,2,2048]{0,2,1:T(8,128)}), f32[256,2,2048]{0,2,1:T(8,128)}) %reduce-scatter.2.cloned.1.call-update) | async-done | bytes 4194320 | tf_op jit(solution)/shard_map/reduce_scatter | solution.py:87
  1354.9 7.3 copy.77
  (38 shorter events, 16.6 us)
Async XLA Ops:
  6.5 569.6 %all-gather.5.cloned.1.call-start = ((), (), s32[]{:S(2)}) async-start(), calls=%async_computation.4 | async-start | bytes 5242880 | tf_op jit(solution)/shard_map/all_gather | solution.py:77
  511.1 10.2 copy-start
  511.1 10.2 copy-start.1
  511.1 10.2 copy-start.2
  511.1 10.2 copy-start.3
  523.8 165.5 %all-gather.3.cloned.1.call-start = ((), (), s32[]{:S(2)}) async-start(), calls=%async_computation.3 | async-start | bytes 5242880 | tf_op jit(solution)/shard_map/all_gather | solution.py:84
  547.6 807.3 %reduce-scatter.2.cloned.1.call-start = ((), (), s32[]{:S(2)}) async-start(), calls=%async_computation.5 | async-start | bytes 37748736 | tf_op jit(solution)/shard_map/reduce_scatter | solution.py:87
Sparse Core Ops, SparseCore 0:
  524.0 52.1 all-gather.4
  577.8 57.8 all-gather.2
  714.6 640.2 reduce-scatter.1
where the time goes:
time: 1380 us; the launch traced here: 1370 us
  waiting for transfers between devices  669 us (48%)
  local copies, waits for them, and re-layouts  324 us (23%)
  matrix products  217 us (16%)
  blocking collectives  93.6 us (7%)
  other arithmetic  51.7 us (4%)
  between operations  14.3 us (1%)
    reduce_scatter x1, waiting for transfers between devices, local(): lax.psum_scatter(contract(left_panel, col_panel), 'pair', scatter_dimensi...  640 us
    dot_general x3, matrix products, transform(): field = jnp.einsum(pattern, field, table, precision=lax.Precision.HIGHEST)  192 us
    gather x2, local copies, waits for them, and re-layouts, pair_densities(): picked = jnp.take(field, sphere_map, axis=2)  136 us
    all_to_all x1, blocking collectives, local(): lax.all_to_all(blocks, 'row', split_axis=3, concat_axis=0, tiled=True)  71.7 us
    another operation x4, local copies, waits for them, and re-layouts, pair_densities(): jnp.stack([real_part, imag_part], 1)  56.7 us
    reshape x1, local copies, waits for them, and re-layouts, pair_densities(): field = transform(field).reshape(local_pairs, 2, -1)  56.5 us
    add x1, other arithmetic, pair_densities(): valence[:, 0] * conduction[:, 0] + valence[:, 1] * conduction[:, 1]  32.4 us
    all_gather x1, waiting for transfers between devices, local(): widened = lax.all_gather(weighted, 'col', axis=0, tiled=True)  28.5 us
  transfers between devices with their start and end apart: 3, of which 2 were waited for; matrix products, arithmetic and copies ran while one was open for 3% of the time, Pallas kernels for 0%

commit v1 on v0

v1 whole, which is shorter than its diff:
```python
import numpy as np
import jax, jax.numpy as jnp
from jax import lax
from jax.experimental import pallas as pl
from jax.sharding import Mesh, PartitionSpec as P
from jax.experimental.pallas import tpu as pltpu


def tables():
    x = np.arange(32); e = np.arange(8); b = np.arange(4)
    ka, kx = np.meshgrid(e, x, indexing="ij")
    xx, yh = np.meshgrid(x, e, indexing="ij")
    ph = (kx.reshape(-1,1)*xx.reshape(1,-1) + 4*ka.reshape(-1,1)*yh.reshape(1,-1)) % 32
    c, s = np.cos(2*np.pi*ph/32), np.sin(2*np.pi*ph/32)
    first = np.block([[c, s], [-s, c]])
    second = []
    kb, kz = np.meshgrid(b, x, indexing="ij")
    yl, z = np.meshgrid(b, x, indexing="ij")
    for a in range(8):
        ky = a + 8*kb.reshape(-1,1)
        ph = (kz.reshape(-1,1)*z.reshape(1,-1) + ky*yl.reshape(1,-1)) % 32
        second.append(np.concatenate([np.cos(2*np.pi*ph/32), np.sin(2*np.pi*ph/32)], 1))
    return first.astype(jnp.bfloat16), np.stack(second).astype(jnp.bfloat16)

def density_kernel(pos, place, val, con, first, second, scale, *rest):
    outs, (xs, yr, yi, zt, held) = rest[:8], rest[8:]
    v = pl.program_id(0)
    vr = val[v, 0].astype(jnp.float32)
    vi = val[v, 1].astype(jnp.float32)
    for pair in range(4):
        for k in range(2):
            cr = con[2*pair+k, 0].astype(jnp.float32)
            ci = con[2*pair+k, 1].astype(jnp.float32)
            xs[0:256, k*128:(k+1)*128] = (vr*cr + vi*ci).astype(jnp.bfloat16)
            xs[256:512, k*128:(k+1)*128] = (vr*ci - vi*cr).astype(jnp.bfloat16)
        y = jnp.dot(first[...], xs[...], preferred_element_type=jnp.float32)
        for k in range(2):
            p = v*8 + 2*pair + k
            yr[pl.ds(p, 256, stride=64), :] = y[0:256, k*128:(k+1)*128]
            yi[pl.ds(p, 256, stride=64), :] = y[256:512, k*128:(k+1)*128]

    @pl.when(v == 7)
    def _():
        def side(r):
            ar = yr[pl.ds(pl.multiple_of(r*64, 64), 64), :].astype(jnp.bfloat16)
            ai = yi[pl.ds(pl.multiple_of(r*64, 64), 64), :].astype(jnp.bfloat16)
            return [jnp.concatenate([ar, ai], 1), jnp.concatenate([ai, -ar], 1)]
        @pl.loop(0, 128, unroll=4)
        def _(q):
            r = q*2
            right = jnp.concatenate(side(r) + side(r+1), 0)
            z = lax.dot_general(second[r // 32], right, (((1,), (1,)), ((), ())), preferred_element_type=jnp.float32)
            zt[pl.ds(pl.multiple_of(r*128, 128), 128), :] = z[:, 0:128]
            zt[pl.ds(pl.multiple_of(r*128+128, 128), 128), :] = z[:, 128:256]
        w = scale[...]
        @pl.loop(0, 256, unroll=2)
        def _(q):
            rows = [zt[pl.ds(pos[q*16+j], 1), :] for j in range(16)]
            t = jnp.concatenate(rows, 0) * w
            held[pl.ds(pl.multiple_of(q*16, 16), 16), :] = t.astype(jnp.bfloat16)
        for s in range(4):
            a = pl.multiple_of(lax.rem(place[0]+s, 4)*1024, 1024)
            outs[s][...] = held[pl.ds(a, 1024), :]
            b = pl.multiple_of(lax.rem(place[1]+s, 4)*1024, 1024)
            outs[4+s][...] = held[pl.ds(b, 1024), :]

def densities(pos, place, val, con, scale):
    first, second = tables()
    full = lambda shape: pl.BlockSpec(shape, lambda i, *_: (0,)*len(shape))
    return pl.pallas_call(
        density_kernel,
        grid_spec=pltpu.PrefetchScalarGridSpec(
            num_scalar_prefetch=2, grid=(8,),
            in_specs=[full((8,2,256,128)), full((8,2,256,128)), full((512,512)), full((8,128,256)), full((1,128))],
            out_specs=[full((1024,128))]*8,
            scratch_shapes=[pltpu.VMEM((512,256), jnp.bfloat16), pltpu.VMEM((16384,128), jnp.float32),
                pltpu.VMEM((16384,128), jnp.float32), pltpu.VMEM((32768,128), jnp.float32), pltpu.VMEM((4096,128), jnp.bfloat16)],
        ),
        out_shape=[jax.ShapeDtypeStruct((1024,128), jnp.bfloat16)]*8,
        compiler_params=pltpu.CompilerParams(vmem_limit_bytes=56*2**20),
        name="densities",
    )(pos, place, val, con, jnp.asarray(first), jnp.asarray(second), scale)


def product_kernel(core, *refs):
    rows, own, other = refs[0:4], refs[4:8], refs[8:12]
    out, left, right = refs[12:]
    step = pl.program_id(0)

    @pl.when(step == 0)
    def _():
        for t in range(4):
            for s in range(4):
                k = (t*4 + s)*128
                left[:, k:k+128] = rows[t][s]

    lane = lax.broadcasted_iota(jnp.int32, (1, 128), 1)
    sign = jnp.where(lane < 64, -1.0, 1.0)

    def fill(cols):
        for t in range(4):
            for s in range(4):
                k = (t*4 + s)*128
                piece = cols[s][t]
                right[0:256, k:k+128] = piece
                turned = pltpu.roll(piece.astype(jnp.float32), 64, 1) * sign
                right[256:512, k:k+128] = turned.astype(jnp.bfloat16)

    half = lax.rem(step, 2)

    @pl.when(half == 0)
    def _():
        fill(own)

    @pl.when(half == 1)
    def _():
        fill(other)

    tile = lax.dot_general(left[...], right[...], (((1,), (1,)), ((), ())), preferred_element_type=jnp.float32)
    tile = tile.astype(jnp.bfloat16)
    for j in range(4):
        place = (j % 2)*2 + j//2
        for o in range(2):
            out[place, o] = tile[j*256:(j+1)*256, o*256:(o+1)*256]


def product(core, rows, own, other, first, count):
    full = pl.BlockSpec((4, 1024, 128), lambda n, core: (0, 0, 0))
    part = pl.BlockSpec((4, 256, 128), lambda n, core: (0, first + n//2, 0))
    return pl.pallas_call(
        product_kernel,
        grid_spec=pltpu.PrefetchScalarGridSpec(
            num_scalar_prefetch=1, grid=(2*count,),
            in_specs=[full]*4 + [part]*8,
            out_specs=pl.BlockSpec(
                (4, 2, 256, 256),
                lambda n, core: (0, 0, 0, 2*(n//2) + core[0] + n % 2 - 2*core[0]*(n % 2))),
            scratch_shapes=[pltpu.VMEM((1024, 2048), jnp.bfloat16), pltpu.VMEM((512, 2048), jnp.bfloat16)],
        ),
        out_shape=jax.ShapeDtypeStruct((4, 2, 256, 512*count), jnp.bfloat16),
        compiler_params=pltpu.CompilerParams(vmem_limit_bytes=48*2**20),
        cost_estimate=pl.CostEstimate(flops=2*1024*512*2048*2*count, bytes_accessed=16*2**20, transcendentals=0),
        name="product",
    )(core, *rows, *own, *other)


def ring(shift):
    return [(i, (i + shift) % 4) for i in range(4)]


CHUNKS = 4


def local(valence_index, conduction_index, valence_waves, conduction_waves,
          valence_energy, conduction_energy, frequency, sphere_map):
    x, y = lax.axis_index("x"), lax.axis_index("y")
    zl, zh, core = lax.axis_index("zl"), lax.axis_index("zh"), lax.axis_index("core")
    vb, cb = (y*2 + zl)*8, (x*2 + zh)*8
    val = lax.dynamic_slice(valence_waves, (vb, 0, 0), (8, 2, 32768)).reshape(8, 2, 256, 128)
    con = lax.dynamic_slice(conduction_waves, (cb, 0, 0), (8, 2, 32768)).reshape(8, 2, 256, 128)
    gap = lax.dynamic_slice(conduction_energy, (cb,), (8,))[None, :] - lax.dynamic_slice(valence_energy, (vb,), (8,))[:, None]
    weight = 4.0 * gap / (gap*gap + frequency[0]*frequency[0]) / 4096
    scale = jnp.sqrt(weight / 32768.0).reshape(1, 64)
    scale = jnp.concatenate([scale, scale], 1)
    point = lax.dynamic_index_in_dim(sphere_map.reshape(16, 2, 256), core, 1, keepdims=False).reshape(4096)
    ky = (point >> 5) & 31
    pos = ((ky & 7)*32 + (point >> 10))*128 + (ky >> 3)*32 + (point & 31)
    parts = densities(pos, jnp.stack([x, y]).astype(jnp.int32), val, con, scale)
    row = [parts[0]] + [None]*3
    col = [parts[4]] + [None]*3
    for s in (2, 1, 3):
        row[s] = lax.ppermute(parts[s], "x", ring(s))
        col[s] = lax.ppermute(parts[4 + s], "y", ring(s))
    rows = [jnp.stack(row)] + [None]*3
    own = [jnp.stack(col)] + [None]*3
    for s in (1, 3, 2):
        rows[s] = lax.ppermute(rows[0], "y", ring(s))
        own[s] = lax.ppermute(own[0], "x", ring(s))
    other = [lax.ppermute(a, "core", [(0, 1), (1, 0)]) for a in own]
    which = core.astype(jnp.int32)[None]
    done = []
    for q in range(CHUNKS):
        count = 4 // CHUNKS
        tile = product(which, rows, own, other, q*count, count)
        tile = tile.reshape(4, 512, 512*count)
        total = lax.psum_scatter(tile, ("zh", "zl"), scatter_dimension=0, tiled=True)
        done.append(total.reshape(2, 256, 512*count))
    whole = jnp.concatenate(done, 2)
    return jnp.transpose(whole, (1, 0, 2)).astype(jnp.float32)


def solution(mesh):
    shaped = Mesh(mesh.devices.reshape(4, 2, 2, 2, 4), ("x", "zl", "zh", "core", "y"))
    split = P(("x", "zl", "zh", "core", "y"))
    return jax.shard_map(
        local,
        mesh=shaped,
        in_specs=(split, split, P(), P(), P(), P(), P(), P()),
        out_specs=P(("x", "zl", "zh", "core"), None, "y"),
        check_vma=False,
    )
```

time: 1380 us -> 299 us (0.22)
  waiting for transfers between devices: 669 us -> 158 us
  local copies, waits for them, and re-layouts: 324 us -> 23.7 us
  matrix products: 217 us -> 0 us
  blocking collectives: 93.6 us -> 0 us
  Pallas kernels: 0 us -> 73.5 us
  other arithmetic: 51.7 us -> 5.57 us
  starting transfers between devices: 0.09 us -> 22 us
    reduce_scatter x1 -> x4, waiting for transfers between devices: 640 us -> 91.2 us  [local(): lax.psum_scatter(tile, ('zh', 'zl'), scatter_dimension=0, tiled=True)]
    dot_general x4 -> x0, matrix products: 217 us -> none  [the longest x3 192 us: transform(): field = jnp.einsum(pattern, field, table, precision=lax.Precision.HIGHEST)]
    gather x4 -> x0, local copies, waits for them, and re-layouts: 163 us -> none  [the longest x2 136 us: pair_densities(): picked = jnp.take(field, sphere_map, axis=2)]
    all_to_all x2 -> x0, blocking collectives: 93.6 us -> none  [the longest x1 71.7 us: local(): lax.all_to_all(blocks, 'row', split_axis=3, concat_axis=0, tiled=True)]
    pallas_call x0 -> x5, Pallas kernels: none -> 73.5 us  [the longest x4 38.6 us: product(): pl.pallas_call(product_kernel, grid_spec=pltpu.PrefetchScalarGridSpec(num...]
    ppermute x0 -> x16, waiting for transfers between devices: none -> 67 us  [the longest x3 39.2 us: local(): own[s] = lax.ppermute(own[0], 'x', ring(s))]
    another operation x5 -> x0, local copies, waits for them, and re-layouts: 64.1 us -> none  [the longest x4 56.7 us: pair_densities(): jnp.stack([real_part, imag_part], 1)]
    reshape x3, local copies, waits for them, and re-layouts: 66.7 us -> 3.25 us  [the longest x1 1.62 us: local(): lax.dynamic_slice(conduction_waves, (cb, 0, 0), (8, 2, 32768))]
  transfers between devices with their start and end apart: 3 -> 20, of which waited for: 2 -> 10; matrix products, arithmetic and copies ran while one was open for 3% -> 1% of each run, Pallas kernels for 0% -> 10%
where the time goes in v1:
time: 299 us; the launch traced here: 297 us
  waiting for transfers between devices  158 us (53%)
  Pallas kernels  73.5 us (25%)
  local copies, waits for them, and re-layouts  23.7 us (8%)
  starting transfers between devices  22 us (7%)
  between operations  14 us (5%)
  other arithmetic  5.57 us (2%)
    reduce_scatter x4, waiting for transfers between devices, local(): lax.psum_scatter(tile, ('zh', 'zl'), scatter_dimension=0, tiled=True)  91.2 us
    ppermute x3, waiting for transfers between devices, local(): own[s] = lax.ppermute(own[0], 'x', ring(s))  39.2 us
    pallas_call x4, Pallas kernels, product(): pl.pallas_call(product_kernel, grid_spec=pltpu.PrefetchScalarGridSpec(num...  38.6 us
    pallas_call x1, Pallas kernels, densities(): pl.pallas_call(density_kernel, grid_spec=pltpu.PrefetchScalarGridSpec(num...  34.9 us
    ppermute x3, waiting for transfers between devices, local(): rows[s] = lax.ppermute(rows[0], 'y', ring(s))  23.6 us
    unnamed x33, local copies, waits for them, and re-layouts  9.7 us
    ppermute x3, starting transfers between devices, local(): row[s] = lax.ppermute(parts[s], 'x', ring(s))  6.97 us
  transfers between devices with their start and end apart: 20, of which 10 were waited for; matrix products, arithmetic and copies ran while one was open for 1% of the time, Pallas kernels for 10%

profile of v1, /device:TPU:8, one launch (start us, length us, event | category | flops | bytes accessed | tf_op | source)
XLA Modules:
  0.0 296.9 jit_solution(2553613432109716018)
XLA Ops:
  9.5 2.0 constant_dynamic-slice_fusion
  11.4 1.6 reshape.103.con
  13.1 1.9 constant_dynamic-slice_fusion.1
  15.0 1.6 reshape.102.val
  17.9 34.9 %densities.1 = (bf16[1024,128]{1,0:T(8,128)(2,1)}, bf16[1024,128]{1,0:T(8,128)(2,1)}, bf16[1024,128]{1,0:T(8,128)(2,1)}, bf16[1024,128]{1,0:T(8,128)(2,1)}, bf16...) custom-call(s32[4096]{0:T(1024)} %bitcast.42, ...), custom_call_target="tpu_custom_call" | custom-call | tf_op jit(solution)/shard_map/densities/pallas_call | solution.py:70
  52.8 2.3 collective-permute-start.7
  58.6 2.7 collective-permute-start.1
  61.4 2.4 collective-permute-done.7
  63.8 2.7 collective-permute-start.2
  66.5 1.7 collective-permute-done.8
  71.0 2.7 collective-permute-start.10
  77.7 18.0 %collective-permute-done.9.refs_5_ = bf16[4,1024,128]{2,1,0:T(8,128)(2,1)S(1)} collective-permute-done((bf16[4,1024,128]{2,1,0:T(8,128)(2,1)S(1)}, bf16[4,1024,128]{2,1,0:T(8,128)(2,1)S(1)}, u32[]{:S(2)}, u32[]{:S(2)}) %collective-permute-start.9) | collective-permute-done | bytes 1048608 | tf_op jit(solution)/shard_map/ppermute | solution.py:178
  95.8 2.2 collective-permute-start.4
  97.9 21.2 %collective-permute-done.10.refs_6_ = bf16[4,1024,128]{2,1,0:T(8,128)(2,1)S(1)} collective-permute-done((bf16[4,1024,128]{2,1,0:T(8,128)(2,1)S(1)}, bf16[4,1024,128]{2,1,0:T(8,128)(2,1)S(1)}, u32[]{:S(2)}, u32[]{:S(2)}) %collective-permute-start.10) | collective-permute-done | bytes 1048608 | tf_op jit(solution)/shard_map/ppermute | solution.py:178
  121.3 22.4 %collective-permute-done.5.refs_3_ = bf16[4,1024,128]{2,1,0:T(8,128)(2,1)S(1)} collective-permute-done((bf16[4,1024,128]{2,1,0:T(8,128)(2,1)S(1)}, bf16[4,1024,128]{2,1,0:T(8,128)(2,1)S(1)}, u32[]{:S(2)}, u32[]{:S(2)}) %collective-permute-start.5) | collective-permute-done | bytes 1048608 | tf_op jit(solution)/shard_map/ppermute | solution.py:177
  145.5 9.7 %product.4 = bf16[4,2,256,512]{3,2,1,0:T(8,128)(2,1)} custom-call(s32[1]{0:T(128)} %bitcast.core, bf16[4,1024,128]{2,1,0:T(8,128)(2,1)S(1)} %pad_maximum_fusion.refs_0_, bf16[4,1024,128]{2,1,0:T(8,128)(2,1)S(1)} %collective-permute-done.3.refs_1_, bf16[4,1024,128]{2,1,0:T(8,128)(2,1)S(1)} %collective-permute-done.4.refs_2_, ...), custom_call_target="tpu_custom_call" | custom-call | flops 4294967296 | bytes 16777216 | tf_op jit(solution)/shard_map/product/pallas_call | solution.py:130
  157.7 9.6 %product.5 = bf16[4,2,256,512]{3,2,1,0:T(8,128)(2,1)} custom-call(s32[1]{0:T(128)} %bitcast.core, bf16[4,1024,128]{2,1,0:T(8,128)(2,1)S(1)} %pad_maximum_fusion.refs_0_, bf16[4,1024,128]{2,1,0:T(8,128)(2,1)S(1)} %collective-permute-done.3.refs_1_, bf16[4,1024,128]{2,1,0:T(8,128)(2,1)S(1)} %copy-done.1, bf16[4,1024,128]{2,1,0:T(8,128)(2,1)S(1)} %copy-done.5, ...), custom_call_target="tpu_custom_call" | custom-call | flops 4294967296 | bytes 16777216 | tf_op jit(solution)/shard_map/product/pallas_call | solution.py:130
  169.8 9.7 %product.6 = bf16[4,2,256,512]{3,2,1,0:T(8,128)(2,1)} custom-call(s32[1]{0:T(128)} %bitcast.core, bf16[4,1024,128]{2,1,0:T(8,128)(2,1)S(1)} %pad_maximum_fusion.refs_0_, bf16[4,1024,128]{2,1,0:T(8,128)(2,1)S(1)} %collective-permute-done.3.refs_1_, bf16[4,1024,128]{2,1,0:T(8,128)(2,1)S(1)} %copy-done.2, bf16[4,1024,128]{2,1,0:T(8,128)(2,1)S(1)} %copy-done.6, ...), custom_call_target="tpu_custom_call" | custom-call | flops 4294967296 | bytes 16777216 | tf_op jit(solution)/shard_map/product/pallas_call | solution.py:130
  182.3 9.6 %product.7 = bf16[4,2,256,512]{3,2,1,0:T(8,128)(2,1)} custom-call(s32[1]{0:T(128)} %bitcast.core, bf16[4,1024,128]{2,1,0:T(8,128)(2,1)S(1)} %pad_maximum_fusion.refs_0_, bf16[4,1024,128]{2,1,0:T(8,128)(2,1)S(1)} %collective-permute-done.3.refs_1_, bf16[4,1024,128]{2,1,0:T(8,128)(2,1)S(1)} %copy-done.3, bf16[4,1024,128]{2,1,0:T(8,128)(2,1)S(1)} %copy-done.7, ...), custom_call_target="tpu_custom_call" | custom-call | flops 4294967296 | bytes 16777216 | tf_op jit(solution)/shard_map/product/pallas_call | solution.py:130
  191.9 27.4 %reduce-scatter.7.cloned.1.call-done = bf16[1,512,512]{2,1,0:T(8,128)(2,1)} async-done(((bf16[4,512,512]{2,1,0:T(8,128)(2,1)}), bf16[1,512,512]{2,1,0:T(8,128)(2,1)}) %reduce-scatter.7.cloned.1.call-update) | async-done | bytes 524304 | tf_op jit(solution)/shard_map/reduce_scatter | solution.py:186
  219.3 31.9 %reduce-scatter.9.cloned.1.call-done = bf16[1,512,512]{2,1,0:T(8,128)(2,1)} async-done(((bf16[4,512,512]{2,1,0:T(8,128)(2,1)}), bf16[1,512,512]{2,1,0:T(8,128)(2,1)}) %reduce-scatter.9.cloned.1.call-update) | async-done | bytes 524304 | tf_op jit(solution)/shard_map/reduce_scatter | solution.py:186
  251.2 31.9 %reduce-scatter.11.cloned.1.call-done = bf16[1,512,512]{2,1,0:T(8,128)(2,1)} async-done(((bf16[4,512,512]{2,1,0:T(8,128)(2,1)}), bf16[1,512,512]{2,1,0:T(8,128)(2,1)}) %reduce-scatter.11.cloned.1.call-update) | async-done | bytes 524304 | tf_op jit(solution)/shard_map/reduce_scatter | solution.py:186
  283.1 2.1 convert_bitcast_fusion
  285.2 5.3 %copy.12 = f32[256,2,2048]{2,1,0:T(2,128)} copy(f32[256,2,2048]{2,0,1:T(8,128)S(1)} %convert_bitcast_fusion) | data formatting | bytes 8388608 | tf_op jit(solution)/shard_map/convert_element_type | solution.py:189
  (75 shorter events, 25.6 us)
Async XLA Ops:
  6.5 185.4 %reduce-scatter.5.cloned.1.call-start = ((), (), s32[]{:S(2)}) async-start(), calls=%async_computation.4 | async-start | bytes 2621440 | tf_op jit(solution)/shard_map/reduce_scatter | solution.py:186
  52.8 11.0 %collective-permute-start.7 = (bf16[1024,128]{1,0:T(8,128)(2,1)}, bf16[1024,128]{1,0:T(8,128)(2,1)S(1)}, u32[]{:S(2)}, u32[]{:S(2)}) collective-permute-start(bf16[1024,128]{1,0:T(8,128)(2,1)} %get-tuple-element.19), channel_id=1, source_target_pairs={{0,2},{1,3},{2,0},{3,1},{4,6},{5,7},{6,4},{7,5},{8,10},{9,11},{10,... | collective-permute-start | bytes 786440 | tf_op jit(solution)/shard_map/ppermute | solution.py:173
  55.1 13.1 %collective-permute-start.8 = (bf16[1024,128]{1,0:T(8,128)(2,1)}, bf16[1024,128]{1,0:T(8,128)(2,1)S(1)}, u32[]{:S(2)}, u32[]{:S(2)}) collective-permute-start(bf16[1024,128]{1,0:T(8,128)(2,1)} %get-tuple-element.20), channel_id=1, source_target_pairs={{0,3},{1,0},{2,1},{3,2},{4,7},{5,4},{6,5},{7,6},{8,11},{9,8},{10,9... | collective-permute-start | bytes 786440 | tf_op jit(solution)/shard_map/ppermute | solution.py:173
  56.5 11.9 %collective-permute-start.6 = (bf16[1024,128]{1,0:T(8,128)(2,1)}, bf16[1024,128]{1,0:T(8,128)(2,1)S(1)}, u32[]{:S(2)}, u32[]{:S(2)}) collective-permute-start(bf16[1024,128]{1,0:T(8,128)(2,1)} %get-tuple-element.18), channel_id=1, source_target_pairs={{0,1},{1,2},{2,3},{3,0},{4,5},{5,6},{6,7},{7,4},{8,9},{9,10},{10,1... | collective-permute-start | bytes 786440 | tf_op jit(solution)/shard_map/ppermute | solution.py:173
  57.1 16.6 %collective-permute-start = (bf16[1024,128]{1,0:T(8,128)(2,1)}, bf16[1024,128]{1,0:T(8,128)(2,1)S(1)}, u32[]{:S(2)}, u32[]{:S(2)}) collective-permute-start(bf16[1024,128]{1,0:T(8,128)(2,1)} %get-tuple-element.14), channel_id=1, source_target_pairs={{0,32},{32,64},{64,96},{96,0},{1,33},{33,65},{65,97},{97,1},{2,34}... | collective-permute-start | bytes 786440 | tf_op jit(solution)/shard_map/ppermute | solution.py:172
  58.6 16.5 %collective-permute-start.1 = (bf16[1024,128]{1,0:T(8,128)(2,1)}, bf16[1024,128]{1,0:T(8,128)(2,1)S(1)}, u32[]{:S(2)}, u32[]{:S(2)}) collective-permute-start(bf16[1024,128]{1,0:T(8,128)(2,1)} %get-tuple-element.15), channel_id=1, source_target_pairs={{0,64},{32,96},{64,0},{96,32},{1,65},{33,97},{65,1},{97,33},{2,66}... | collective-permute-start | bytes 786440 | tf_op jit(solution)/shard_map/ppermute | solution.py:172
  63.8 11.4 %collective-permute-start.2 = (bf16[1024,128]{1,0:T(8,128)(2,1)}, bf16[1024,128]{1,0:T(8,128)(2,1)S(1)}, u32[]{:S(2)}, u32[]{:S(2)}) collective-permute-start(bf16[1024,128]{1,0:T(8,128)(2,1)} %get-tuple-element.16), channel_id=1, source_target_pairs={{0,96},{32,0},{64,32},{96,64},{1,97},{33,1},{65,33},{97,65},{2,98}... | collective-permute-start | bytes 786440 | tf_op jit(solution)/shard_map/ppermute | solution.py:172
  69.4 26.3 %collective-permute-start.9 = (bf16[4,1024,128]{2,1,0:T(8,128)(2,1)S(1)}, bf16[4,1024,128]{2,1,0:T(8,128)(2,1)S(1)}, u32[]{:S(2)}, u32[]{:S(2)}) collective-permute-start(bf16[4,1024,128]{2,1,0:T(8,128)(2,1)S(1)} %pad_maximum_fusion.1.refs_4_), channel_id=1, source_target_pairs={{0,32},{32,64},{64,96},{96,0},{1,33},{33,65},{65,97},{97,1},{2,34}... | collective-permute-start | bytes 3145736 | tf_op jit(solution)/shard_map/ppermute | solution.py:178
  71.0 48.1 %collective-permute-start.10 = (bf16[4,1024,128]{2,1,0:T(8,128)(2,1)S(1)}, bf16[4,1024,128]{2,1,0:T(8,128)(2,1)S(1)}, u32[]{:S(2)}, u32[]{:S(2)}) collective-permute-start(bf16[4,1024,128]{2,1,0:T(8,128)(2,1)S(1)} %pad_maximum_fusion.1.refs_4_), channel_id=1, source_target_pairs={{0,64},{32,96},{64,0},{96,32},{1,65},{33,97},{65,1},{97,33},{2,66}... | collective-permute-start | bytes 3145736 | tf_op jit(solution)/shard_map/ppermute | solution.py:178
  73.7 45.6 %collective-permute-start.11 = (bf16[4,1024,128]{2,1,0:T(8,128)(2,1)S(1)}, bf16[4,1024,128]{2,1,0:T(8,128)(2,1)S(1)}, u32[]{:S(2)}, u32[]{:S(2)}) collective-permute-start(bf16[4,1024,128]{2,1,0:T(8,128)(2,1)S(1)} %pad_maximum_fusion.1.refs_4_), channel_id=1, source_target_pairs={{0,96},{32,0},{64,32},{96,64},{1,97},{33,1},{65,33},{97,65},{2,98}... | collective-permute-start | bytes 3145736 | tf_op jit(solution)/shard_map/ppermute | solution.py:178
  75.2 44.2 %collective-permute-start.12 = (bf16[4,1024,128]{2,1,0:T(8,128)(2,1)S(1)}, bf16[4,1024,128]{2,1,0:T(8,128)(2,1)S(1)}, u32[]{:S(2)}, u32[]{:S(2)}) collective-permute-start(bf16[4,1024,128]{2,1,0:T(8,128)(2,1)S(1)} %pad_maximum_fusion.1.refs_4_), channel_id=1, source_target_pairs={{0,4},{4,0},{1,5},{5,1},{2,6},{6,2},{3,7},{7,3},{8,12},{12,8},{9,1... | collective-permute-start | bytes 3145736 | tf_op jit(solution)/shard_map/ppermute | solution.py:179
  76.3 43.6 %collective-permute-start.3 = (bf16[4,1024,128]{2,1,0:T(8,128)(2,1)S(1)}, bf16[4,1024,128]{2,1,0:T(8,128)(2,1)S(1)}, u32[]{:S(2)}, u32[]{:S(2)}) collective-permute-start(bf16[4,1024,128]{2,1,0:T(8,128)(2,1)S(1)} %pad_maximum_fusion.refs_0_), channel_id=1, source_target_pairs={{0,1},{1,2},{2,3},{3,0},{4,5},{5,6},{6,7},{7,4},{8,9},{9,10},{10,1... | collective-permute-start | bytes 3145736 | tf_op jit(solution)/shard_map/ppermute | solution.py:177
  95.8 48.0 %copy-start.9 = (bf16[4,1024,128]{2,1,0:T(8,128)(2,1)}, bf16[4,1024,128]{2,1,0:T(8,128)(2,1)S(1)}, u32[]{:S(2)}) copy-start(bf16[4,1024,128]{2,1,0:T(8,128)(2,1)S(1)} %collective-permute-done.9.refs_5_) | copy-start | bytes 3145732
  95.8 25.5 %collective-permute-start.4 = (bf16[4,1024,128]{2,1,0:T(8,128)(2,1)S(1)}, bf16[4,1024,128]{2,1,0:T(8,128)(2,1)S(1)}, u32[]{:S(2)}, u32[]{:S(2)}) collective-permute-start(bf16[4,1024,128]{2,1,0:T(8,128)(2,1)S(1)} %pad_maximum_fusion.refs_0_), channel_id=1, source_target_pairs={{0,2},{1,3},{2,0},{3,1},{4,6},{5,7},{6,4},{7,5},{8,10},{9,11},{10,... | collective-permute-start | bytes 3145736 | tf_op jit(solution)/shard_map/ppermute | solution.py:177
  119.1 24.6 %copy-start.10 = (bf16[4,1024,128]{2,1,0:T(8,128)(2,1)}, bf16[4,1024,128]{2,1,0:T(8,128)(2,1)S(1)}, u32[]{:S(2)}) copy-start(bf16[4,1024,128]{2,1,0:T(8,128)(2,1)S(1)} %collective-permute-done.10.refs_6_) | copy-start | bytes 3145732
  119.1 24.6 %collective-permute-start.5 = (bf16[4,1024,128]{2,1,0:T(8,128)(2,1)S(1)}, bf16[4,1024,128]{2,1,0:T(8,128)(2,1)S(1)}, u32[]{:S(2)}, u32[]{:S(2)}) collective-permute-start(bf16[4,1024,128]{2,1,0:T(8,128)(2,1)S(1)} %pad_maximum_fusion.refs_0_), channel_id=1, source_target_pairs={{0,3},{1,0},{2,1},{3,2},{4,7},{5,4},{6,5},{7,6},{8,11},{9,8},{10,9... | collective-permute-start | bytes 3145736 | tf_op jit(solution)/shard_map/ppermute | solution.py:177
  119.3 24.4 %copy-start.11 = (bf16[4,1024,128]{2,1,0:T(8,128)(2,1)}, bf16[4,1024,128]{2,1,0:T(8,128)(2,1)S(1)}, u32[]{:S(2)}) copy-start(bf16[4,1024,128]{2,1,0:T(8,128)(2,1)S(1)} %collective-permute-done.11.refs_7_) | copy-start | bytes 3145732
  119.3 24.4 %collective-permute-start.13 = (bf16[4,1024,128]{2,1,0:T(8,128)(2,1)S(1)}, bf16[4,1024,128]{2,1,0:T(8,128)(2,1)S(1)}, u32[]{:S(2)}, u32[]{:S(2)}) collective-permute-start(bf16[4,1024,128]{2,1,0:T(8,128)(2,1)S(1)} %collective-permute-done.9.refs_5_), channel_id=1, source_target_pairs={{0,4},{4,0},{1,5},{5,1},{2,6},{6,2},{3,7},{7,3},{8,12},{12,8},{9,1... | collective-permute-start | bytes 3145736 | tf_op jit(solution)/shard_map/ppermute | solution.py:179
  119.3 24.3 %collective-permute-start.14 = (bf16[4,1024,128]{2,1,0:T(8,128)(2,1)S(1)}, bf16[4,1024,128]{2,1,0:T(8,128)(2,1)S(1)}, u32[]{:S(2)}, u32[]{:S(2)}) collective-permute-start(bf16[4,1024,128]{2,1,0:T(8,128)(2,1)S(1)} %collective-permute-done.10.refs_6_), channel_id=1, source_target_pairs={{0,4},{4,0},{1,5},{5,1},{2,6},{6,2},{3,7},{7,3},{8,12},{12,8},{9,1... | collective-permute-start | bytes 3145736 | tf_op jit(solution)/shard_map/ppermute | solution.py:179
  119.8 23.9 %collective-permute-start.15 = (bf16[4,1024,128]{2,1,0:T(8,128)(2,1)S(1)}, bf16[4,1024,128]{2,1,0:T(8,128)(2,1)S(1)}, u32[]{:S(2)}, u32[]{:S(2)}) collective-permute-start(bf16[4,1024,128]{2,1,0:T(8,128)(2,1)S(1)} %collective-permute-done.11.refs_7_), channel_id=1, source_target_pairs={{0,4},{4,0},{1,5},{5,1},{2,6},{6,2},{3,7},{7,3},{8,12},{12,8},{9,1... | collective-permute-start | bytes 3145736 | tf_op jit(solution)/shard_map/ppermute | solution.py:179
  121.3 33.9 %copy-start = (bf16[4,1024,128]{2,1,0:T(8,128)(2,1)}, bf16[4,1024,128]{2,1,0:T(8,128)(2,1)S(1)}, u32[]{:S(2)}) copy-start(bf16[4,1024,128]{2,1,0:T(8,128)(2,1)S(1)} %collective-permute-done.4.refs_2_) | copy-start | bytes 3145732
  155.2 64.1 %reduce-scatter.7.cloned.1.call-start = ((), (), s32[]{:S(2)}) async-start(), calls=%async_computation.5 | async-start | bytes 2621440 | tf_op jit(solution)/shard_map/reduce_scatter | solution.py:186
  167.3 83.9 %reduce-scatter.9.cloned.1.call-start = ((), (), s32[]{:S(2)}) async-start(), calls=%async_computation.6 | async-start | bytes 2621440 | tf_op jit(solution)/shard_map/reduce_scatter | solution.py:186
  179.5 103.6 %reduce-scatter.11.cloned.1.call-start = ((), (), s32[]{:S(2)}) async-start(), calls=%async_computation.7 | async-start | bytes 2621440 | tf_op jit(solution)/shard_map/reduce_scatter | solution.py:186
  (12 other events, 54.5 us)
Sparse Core Ops, SparseCore 0:
  155.3 31.9 reduce-scatter.4
  189.8 29.4 reduce-scatter.6
  221.7 29.4 reduce-scatter.8
  253.6 29.4 reduce-scatter.10

commit v2 on v1

v2 whole, which is shorter than its diff:
```python
import numpy as np
import jax, jax.numpy as jnp
from jax import lax
from jax.experimental import pallas as pl
from jax.sharding import Mesh, PartitionSpec as P
from jax.experimental.pallas import tpu as pltpu

VMEM = 60*2**20


def tables():
    x = np.arange(32); e = np.arange(8); b = np.arange(4)
    ka, kx = np.meshgrid(e, x, indexing="ij")
    xx, yh = np.meshgrid(x, e, indexing="ij")
    ph = (kx.reshape(-1,1)*xx.reshape(1,-1) + 4*ka.reshape(-1,1)*yh.reshape(1,-1)) % 32
    c, s = np.cos(2*np.pi*ph/32), np.sin(2*np.pi*ph/32)
    first = np.block([[c, s], [-s, c]])
    second = []
    kb, kz = np.meshgrid(b, x, indexing="ij")
    yl, z = np.meshgrid(b, x, indexing="ij")
    for a in range(8):
        ky = a + 8*kb.reshape(-1,1)
        ph = (kz.reshape(-1,1)*z.reshape(1,-1) + ky*yl.reshape(1,-1)) % 32
        second.append(np.concatenate([np.cos(2*np.pi*ph/32), np.sin(2*np.pi*ph/32)], 1))
    return first.astype(jnp.bfloat16), np.stack(second).astype(jnp.bfloat16)

def density_kernel(pos, place, val, con, first, second, scale, *rest):
    outs, (xs, yr, yi, zt, held) = rest[:8], rest[8:]
    v = pl.program_id(0)
    vr = val[v, 0].astype(jnp.float32)
    vi = val[v, 1].astype(jnp.float32)
    for pair in range(4):
        for k in range(2):
            cr = con[2*pair+k, 0].astype(jnp.float32)
            ci = con[2*pair+k, 1].astype(jnp.float32)
            xs[0:256, k*128:(k+1)*128] = (vr*cr + vi*ci).astype(jnp.bfloat16)
            xs[256:512, k*128:(k+1)*128] = (vr*ci - vi*cr).astype(jnp.bfloat16)
        y = jnp.dot(first[...], xs[...], preferred_element_type=jnp.float32)
        for k in range(2):
            p = v*8 + 2*pair + k
            yr[pl.ds(p, 256, stride=72), :] = y[0:256, k*128:(k+1)*128]
            yi[pl.ds(p, 256, stride=72), :] = y[256:512, k*128:(k+1)*128]

    @pl.when(v == 7)
    def _():
        def side(r):
            ar = yr[pl.ds(pl.multiple_of(r*72, 8), 64), :].astype(jnp.bfloat16)
            ai = yi[pl.ds(pl.multiple_of(r*72, 8), 64), :].astype(jnp.bfloat16)
            return [jnp.concatenate([ar, ai], 1), jnp.concatenate([ai, -ar], 1)]
        @pl.loop(0, 128, unroll=8)
        def _(q):
            r = q*2
            right = jnp.concatenate(side(r) + side(r+1), 0)
            z = lax.dot_general(second[r // 32], right, (((1,), (1,)), ((), ())), preferred_element_type=jnp.float32)
            zt[pl.ds(pl.multiple_of(r*128, 128), 128), :] = z[:, 0:128]
            zt[pl.ds(pl.multiple_of(r*128+128, 128), 128), :] = z[:, 128:256]
        w = scale[...]
        @pl.loop(0, 256, unroll=2)
        def _(q):
            rows = [zt[pl.ds(pos[q*16+j], 1), :] for j in range(16)]
            t = jnp.concatenate(rows, 0) * w
            held[pl.ds(pl.multiple_of(q*16, 16), 16), :] = t.astype(jnp.bfloat16)
        for s in range(4):
            a = lax.rem(place[0]+s, 4)*1024
            for q, shift in enumerate((2, 1, 3, 0)):
                to = lax.rem(place[2]+shift, 4)
                block = lax.rem(to, 2)*2 + lax.div(to, 2)
                outs[s][q*256:(q+1)*256, :] = held[pl.ds(pl.multiple_of(a + block*256, 256), 256), :]
            b = lax.rem(place[1]+s, 4)*1024
            for q in range(4):
                outs[4+s][:, q*256:(q+1)*256] = held[pl.ds(pl.multiple_of(b + q*256, 256), 256), :].T


def densities(pos, place, val, con, scale):
    first, second = tables()
    full = lambda shape: pl.BlockSpec(shape, lambda i, *_: (0,)*len(shape))
    return pl.pallas_call(
        density_kernel,
        grid_spec=pltpu.PrefetchScalarGridSpec(
            num_scalar_prefetch=2, grid=(8,),
            in_specs=[full((8,2,256,128)), full((8,2,256,128)), full((512,512)), full((8,128,256)), full((1,128))],
            out_specs=[full((1024,128))]*4 + [full((128,1024))]*4,
            scratch_shapes=[pltpu.VMEM((512,256), jnp.bfloat16), pltpu.VMEM((256*72,128), jnp.float32),
                pltpu.VMEM((256*72,128), jnp.float32), pltpu.VMEM((32768,128), jnp.float32), pltpu.VMEM((4096,128), jnp.bfloat16)],
        ),
        out_shape=[jax.ShapeDtypeStruct((1024,128), jnp.bfloat16)]*4 + [jax.ShapeDtypeStruct((128,1024), jnp.bfloat16)]*4,
        compiler_params=pltpu.CompilerParams(vmem_limit_bytes=VMEM),
        name="densities",
    )(pos, place, val, con, jnp.asarray(first), jnp.asarray(second), scale)


def product_kernel(core, *refs):
    rows, own, other = refs[0:4], refs[4:8], refs[8:12]
    outs, (left, right) = refs[12:16], refs[16:]
    step = pl.program_id(0)

    @pl.when(step == 0)
    def _():
        for t in range(4):
            for s in range(4):
                k = (t*4 + s)*128
                left[:, k:k+128] = rows[t][s]

    def fill(cols):
        for t in range(4):
            for s in range(4):
                k = (t*4 + s)*128
                piece = cols[s][t]
                right[k:k+128, 0:256] = piece
                right[k:k+64, 256:512] = -piece[64:128]
                right[k+64:k+128, 256:512] = piece[0:64]

    @pl.when(step < 2)
    def _():
        fill(own)

    @pl.when(step >= 2)
    def _():
        fill(other)

    tile = jnp.dot(left[...], right[...], preferred_element_type=jnp.float32)
    tile = tile.astype(jnp.bfloat16)
    for h in range(2):
        @pl.when(lax.rem(step, 2) == h)
        def _(h=h):
            for b in range(2):
                for o in range(2):
                    outs[2*b + h][o] = tile[b*256:(b+1)*256, o*256:(o+1)*256]


def product(core, rows, own, other):
    full = pl.BlockSpec((4, 512, 128), lambda n, core: (0, 0, 0))
    near = pl.BlockSpec((4, 128, 256), lambda n, core: (0, 0, jnp.minimum(n, 1)))
    far = pl.BlockSpec((4, 128, 256), lambda n, core: (0, 0, jnp.maximum(n - 2, 0)))
    out = pl.BlockSpec(
        (2, 256, 256),
        lambda n, core: (0, 0, core[0] + n//2 - 2*core[0]*(n//2)))
    return pl.pallas_call(
        product_kernel,
        grid_spec=pltpu.PrefetchScalarGridSpec(
            num_scalar_prefetch=1, grid=(4,),
            in_specs=[full]*4 + [near]*4 + [far]*4,
            out_specs=[out]*4,
            scratch_shapes=[pltpu.VMEM((512, 2048), jnp.bfloat16), pltpu.VMEM((2048, 512), jnp.bfloat16)],
        ),
        out_shape=[jax.ShapeDtypeStruct((2, 256, 512), jnp.bfloat16)]*4,
        compiler_params=pltpu.CompilerParams(vmem_limit_bytes=VMEM),
        cost_estimate=pl.CostEstimate(flops=2**10, bytes_accessed=2**10, transcendentals=0),
        name="product",
    )(core, *rows, *own, *other)


def total_kernel(*refs):
    out = refs[-1]
    for h in range(2):
        t = refs[3*h][...].astype(jnp.float32) + refs[3*h+1][...].astype(jnp.float32)
        t = t + refs[3*h+2][...].astype(jnp.float32)
        out[:, 0, h*512:(h+1)*512] = t[0]
        out[:, 1, h*512:(h+1)*512] = t[1]


def total(parts, chunk, before):
    spec = pl.BlockSpec((2, 64, 512), lambda n: (0, n, 0))
    more = [] if before is None else [before]
    return pl.pallas_call(
        total_kernel,
        grid=(4,),
        in_specs=[spec]*6 + [pl.BlockSpec(memory_space=pl.ANY)]*len(more),
        out_specs=pl.BlockSpec((64, 2, 1024), lambda n: (n, 0, chunk)),
        out_shape=jax.ShapeDtypeStruct((256, 2, 2048), jnp.float32),
        input_output_aliases={6: 0} if more else {},
        compiler_params=pltpu.CompilerParams(vmem_limit_bytes=VMEM),
        cost_estimate=pl.CostEstimate(flops=2**10, bytes_accessed=2**10, transcendentals=0),
        name="total",
    )(*parts, *more)


def ring(shift):
    return [(i, (i + shift) % 4) for i in range(4)]


def along_z(block, shift):
    place = lambda z: (z % 2)*2 + z//2
    return lax.ppermute(block, ("zl", "zh"), [(place(i), place((i + shift) % 4)) for i in range(4)])


def after(arrays, *first):
    return lax.optimization_barrier((tuple(arrays), first))[0]


def spread(row, col, *first):
    rows, cols = [row] + [None]*3, [col] + [None]*3
    for s in (1, 3):
        rows[s] = lax.ppermute(row, "y", ring(s))
        cols[s] = lax.ppermute(col, "x", ring(s))
    row, col = after((row, col), rows[1], cols[1], rows[3], cols[3], *first)
    rows[2] = lax.ppermute(row, "y", ring(2))
    cols[2] = lax.ppermute(col, "x", ring(2))
    return rows, cols


def add(a, b):
    return (a.astype(jnp.float32) + b.astype(jnp.float32)).astype(jnp.bfloat16)


def begun(far):
    far0, far1, next0, next1 = far
    return next0, along_z(far0, 1), along_z(far1, -1), along_z(next1, 1)


def ended(far, near):
    next0, got0, got1, up1 = far
    last0, last1, mine0, mine1 = near
    down0 = along_z(last0, -1)
    up0, down1 = along_z(add(next0, got0), 1), along_z(add(last1, got1), -1)
    return [mine0, up0, down0, mine1, up1, down1]


def swapped(blocks):
    return [lax.ppermute(a, "core", [(0, 1), (1, 0)]) for a in blocks]


def local(valence_index, conduction_index, valence_waves, conduction_waves,
          valence_energy, conduction_energy, frequency, sphere_map):
    x, y = lax.axis_index("x"), lax.axis_index("y")
    zl, zh, core = lax.axis_index("zl"), lax.axis_index("zh"), lax.axis_index("core")
    vb, cb = (y*2 + zl)*8, (x*2 + zh)*8
    val = lax.dynamic_slice(valence_waves, (vb, 0, 0), (8, 2, 32768)).reshape(8, 2, 256, 128)
    con = lax.dynamic_slice(conduction_waves, (cb, 0, 0), (8, 2, 32768)).reshape(8, 2, 256, 128)
    gap = lax.dynamic_slice(conduction_energy, (cb,), (8,))[None, :] - lax.dynamic_slice(valence_energy, (vb,), (8,))[:, None]
    weight = 4.0 * gap / (gap*gap + frequency[0]*frequency[0]) / 4096
    scale = jnp.sqrt(weight / 32768.0).reshape(1, 64)
    scale = jnp.concatenate([scale, scale], 1)
    point = lax.dynamic_index_in_dim(sphere_map.reshape(16, 2, 256), core, 1, keepdims=False).reshape(4096)
    ky = (point >> 5) & 31
    pos = ((ky & 7)*32 + (point >> 10))*128 + (ky >> 3)*32 + (point & 31)
    place = jnp.stack([x, y, zh*2 + zl]).astype(jnp.int32)
    parts = densities(pos, place, val, con, scale)
    row = [parts[0]] + [None]*3
    col = [parts[4]] + [None]*3
    for s in (2, 1, 3):
        row[s] = lax.ppermute(parts[s], "x", ring(s))
        col[s] = lax.ppermute(parts[4 + s], "y", ring(s))
    row, col = jnp.stack(row), jnp.stack(col)
    which = core.astype(jnp.int32)[None]
    row_a, col_a = row[:, :512], col[:, :, :512]
    row_b, col_b = row[:, 512:], col[:, :, 512:]
    rows_a, own_a = spread(row_a, col_a)
    other_a = swapped(own_a)
    row_b, col_b = after((row_b, col_b), rows_a[2], own_a[2])
    aa = begun(product(which, rows_a, own_a, other_a))
    rows_b, own_b = spread(row_b, col_b, aa[0])
    other_b = swapped(after(own_b, aa[1], aa[2]))
    ba = product(which, rows_b, own_a, other_a)
    ab = begun(product(which, rows_a, own_b, other_b))
    bb = product(which, rows_b, own_b, other_b)
    return total(ended(ab, bb), 1, total(ended(aa, ba), 0, None))


def solution(mesh):
    shaped = Mesh(mesh.devices.reshape(4, 2, 2, 2, 4), ("x", "zl", "zh", "core", "y"))
    split = P(("x", "zl", "zh", "core", "y"))
    return jax.shard_map(
        local,
        mesh=shaped,
        in_specs=(split, split, P(), P(), P(), P(), P(), P()),
        out_specs=P(("x", "zl", "zh", "core"), None, "y"),
        check_vma=False,
    )
```

time: 299 us -> 210 us (0.70)
  waiting for transfers between devices: 158 us -> 58.6 us
  starting transfers between devices: 22 us -> 49.1 us
  between operations: 14 us -> 1.01 us
  local copies, waits for them, and re-layouts: 23.7 us -> 15.7 us
  other arithmetic: 5.57 us -> 9.48 us
    reduce_scatter x4 -> x0, waiting for transfers between devices: 91.2 us -> none  [local(): lax.psum_scatter(tile, ('zh', 'zl'), scatter_dimension=0, tiled=True)]
    ppermute x10 -> x32, starting transfers between devices: 10.4 us -> 37.2 us  [the longest x12 16 us: along_z(): lax.ppermute(block, ('zl', 'zh'), [(place(i), place((i + shift) % 4)) for...]
    pallas_call x1, Pallas kernels: 34.9 us -> 25 us  [densities(): pl.pallas_call(density_kernel, grid_spec=pltpu.PrefetchScalarGridSpec(num...]
    ppermute x10 -> x32, waiting for transfers between devices: 62.7 us -> 54.1 us  [the longest x12 21.6 us: along_z(): lax.ppermute(block, ('zl', 'zh'), [(place(i), place((i + shift) % 4)) for...]
    pallas_call x0 -> x2, Pallas kernels: none -> 8.62 us  [total(): pl.pallas_call(total_kernel, grid=(4,), in_specs=[spec] * 6 + [pl.BlockSp...]
    convert_element_type x1 -> x0, local copies, waits for them, and re-layouts: 5.25 us -> none  [local(): return jnp.transpose(whole, (1, 0, 2)).astype(jnp.float32)]
    convert_element_type x1 -> x4, other arithmetic: 2.06 us -> 6.04 us  [add(): return (a.astype(jnp.float32) + b.astype(jnp.float32)).astype(jnp.bfloat16)]
    unnamed x33 -> x55, local copies, waits for them, and re-layouts: 9.7 us -> 6.09 us
  transfers between devices with their start and end apart: 20 -> 38, of which waited for: 10 -> 21; matrix products, arithmetic and copies ran while one was open for 1% -> 4% of each run, Pallas kernels for 10% -> 22%
where the time goes in v2:
time: 210 us; the launch traced here: 209 us
  Pallas kernels  74.6 us (36%)
  waiting for transfers between devices  58.6 us (28%)
  starting transfers between devices  49.1 us (23%)
  local copies, waits for them, and re-layouts  15.7 us (7%)
  other arithmetic  9.48 us (5%)
    pallas_call x4, Pallas kernels, product(): pl.pallas_call(product_kernel, grid_spec=pltpu.PrefetchScalarGridSpec(num...  41 us
    pallas_call x1, Pallas kernels, densities(): pl.pallas_call(density_kernel, grid_spec=pltpu.PrefetchScalarGridSpec(num...  25 us
    ppermute x12, waiting for transfers between devices, along_z(): lax.ppermute(block, ('zl', 'zh'), [(place(i), place((i + shift) % 4)) for...  21.6 us
    ppermute x12, starting transfers between devices, along_z(): lax.ppermute(block, ('zl', 'zh'), [(place(i), place((i + shift) % 4)) for...  16 us
    ppermute x4, waiting for transfers between devices, spread(): cols[s] = lax.ppermute(col, 'x', ring(s))  11.3 us
    ppermute x2, waiting for transfers between devices, spread(): cols[2] = lax.ppermute(col, 'x', ring(2))  9.94 us
    ppermute x2, waiting for transfers between devices, spread(): rows[2] = lax.ppermute(row, 'y', ring(2))  9.35 us
    pallas_call x2, Pallas kernels, total(): pl.pallas_call(total_kernel, grid=(4,), in_specs=[spec] * 6 + [pl.BlockSp...  8.62 us
  transfers between devices with their start and end apart: 38, of which 21 were waited for; matrix products, arithmetic and copies ran while one was open for 4% of the time, Pallas kernels for 22%

profile of v2, /device:TPU:8, one launch (start us, length us, event | category | flops | bytes accessed | tf_op | source)
XLA Modules:
  0.0 208.5 jit_solution(8358845442703103481)
XLA Ops:
  12.0 25.0 %densities.1 = (bf16[1024,128]{1,0:T(8,128)(2,1)}, bf16[1024,128]{1,0:T(8,128)(2,1)}, bf16[1024,128]{1,0:T(8,128)(2,1)}, bf16[1024,128]{1,0:T(8,128)(2,1)}, bf16...) custom-call(s32[4096]{0:T(1024)} %bitcast.25, ...), custom_call_target="tpu_custom_call" | custom-call | tf_op jit(solution)/shard_map/densities/pallas_call | solution.py:77
  43.5 2.7 %collective-permute-start.1 = (bf16[1024,128]{1,0:T(8,128)(2,1)}, bf16[1024,128]{1,0:T(8,128)(2,1)S(1)}, u32[]{:S(2)}, u32[]{:S(2)}) collective-permute-start(bf16[1024,128]{1,0:T(8,128)(2,1)} %get-tuple-element.41), channel_id=1, source_target_pairs={{0,64},{32,96},{64,0},{96,32},{1,65},{33,97},{65,1},{97,33},{2,66}... | collective-permute-start | bytes 786440 | tf_op jit(solution)/shard_map/ppermute | solution.py:242
  46.5 2.8 %collective-permute-start.2 = (bf16[1024,128]{1,0:T(8,128)(2,1)}, bf16[1024,128]{1,0:T(8,128)(2,1)S(1)}, u32[]{:S(2)}, u32[]{:S(2)}) collective-permute-start(bf16[1024,128]{1,0:T(8,128)(2,1)} %get-tuple-element.42), channel_id=1, source_target_pairs={{0,96},{32,0},{64,32},{96,64},{1,97},{33,1},{65,33},{97,65},{2,98}... | collective-permute-start | bytes 786440 | tf_op jit(solution)/shard_map/ppermute | solution.py:242
  49.6 3.4 %collective-permute-done.5 = bf16[128,1024]{1,0:T(8,128)(2,1)S(1)} collective-permute-done((bf16[128,1024]{1,0:T(8,128)(2,1)}, bf16[128,1024]{1,0:T(8,128)(2,1)S(1)}, u32[]{:S(2)}, u32[]{:S(2)}) %collective-permute-start.5) | collective-permute-done | bytes 262176 | tf_op jit(solution)/shard_map/ppermute | solution.py:243
  54.2 2.8 %collective-permute-start.9 = (bf16[4,128,512]{2,1,0:T(8,128)(2,1)S(1)}, bf16[4,128,512]{2,1,0:T(8,128)(2,1)S(1)}, u32[]{:S(2)}, u32[]{:S(2)}) collective-permute-start(bf16[4,128,512]{2,1,0:T(8,128)(2,1)S(1)} %get-tuple-element.48.refs_4_), channel_id=1, source_target_pairs={{0,96},{32,0},{64,32},{96,64},{1,97},{33,1},{65,33},{97,65},{2,98}... | collective-permute-start | bytes 1572872 | tf_op jit(solution)/shard_map/ppermute | solution.py:195
  63.1 5.0 %collective-permute-done.9.refs_7_ = bf16[4,128,512]{2,1,0:T(8,128)(2,1)S(1)} collective-permute-done((bf16[4,128,512]{2,1,0:T(8,128)(2,1)S(1)}, bf16[4,128,512]{2,1,0:T(8,128)(2,1)S(1)}, u32[]{:S(2)}, u32[]{:S(2)}) %collective-permute-start.9) | collective-permute-done | bytes 524320 | tf_op jit(solution)/shard_map/ppermute | solution.py:195
  68.0 2.9 %collective-permute-done.7.refs_5_ = bf16[4,128,512]{2,1,0:T(8,128)(2,1)S(1)} collective-permute-done((bf16[4,128,512]{2,1,0:T(8,128)(2,1)S(1)}, bf16[4,128,512]{2,1,0:T(8,128)(2,1)S(1)}, u32[]{:S(2)}, u32[]{:S(2)}) %collective-permute-start.7) | collective-permute-done | bytes 524320 | tf_op jit(solution)/shard_map/ppermute | solution.py:195
  77.4 8.4 %collective-permute-done.10.refs_2_ = bf16[4,512,128]{2,1,0:T(8,128)(2,1)S(1)} collective-permute-done((bf16[4,512,128]{2,1,0:T(8,128)(2,1)S(1)}, bf16[4,512,128]{2,1,0:T(8,128)(2,1)S(1)}, u32[]{:S(2)}, u32[]{:S(2)}) %collective-permute-start.10) | collective-permute-done | bytes 524320 | tf_op jit(solution)/shard_map/ppermute | solution.py:197
  85.9 3.0 %collective-permute-done.11.refs_6_ = bf16[4,128,512]{2,1,0:T(8,128)(2,1)S(1)} collective-permute-done((bf16[4,128,512]{2,1,0:T(8,128)(2,1)S(1)}, bf16[4,128,512]{2,1,0:T(8,128)(2,1)S(1)}, u32[]{:S(2)}, u32[]{:S(2)}) %collective-permute-start.11) | collective-permute-done | bytes 524320 | tf_op jit(solution)/shard_map/ppermute | solution.py:198
  90.9 2.6 %collective-permute-start.15 = (bf16[4,128,512]{2,1,0:T(8,128)(2,1)S(1)}, bf16[4,128,512]{2,1,0:T(8,128)(2,1)}, u32[]{:S(2)}, u32[]{:S(2)}) collective-permute-start(bf16[4,128,512]{2,1,0:T(8,128)(2,1)S(1)} %get-tuple-element.56.refs_4_), channel_id=1, source_target_pairs={{0,96},{32,0},{64,32},{96,64},{1,97},{33,1},{65,33},{97,65},{2,98}... | collective-permute-start | bytes 1572872 | tf_op jit(solution)/shard_map/ppermute | solution.py:195
  95.2 10.2 %product.4 = (bf16[2,256,512]{2,1,0:T(8,128)(2,1)}, bf16[2,256,512]{2,1,0:T(8,128)(2,1)}, bf16[2,256,512]{2,1,0:T(8,128)(2,1)}, bf16[2,256,512]{2,1,0:T(8,128)(2,1)}) custom-call(s32[1]{0:T(128)} %bitcast.core, bf16[4,512,128]{2,1,0:T(8,128)(2,1)} %copy-done.3, bf16[4,512,128]{2,1,0:T(8,128)(2,1)} %copy-done.7, bf16[4,512,128]{2,1,0:T(8,128)(2,1)} %copy-done.8, ...), custom_call_target="tpu_custom_call" | custom-call | flops 1024 | bytes 1024 | tf_op jit(solution)/shard_map/product/pallas_call | solution.py:138
  105.4 3.4 %collective-permute-done.13.refs_5_ = bf16[4,128,512]{2,1,0:T(8,128)(2,1)} collective-permute-done((bf16[4,128,512]{2,1,0:T(8,128)(2,1)S(1)}, bf16[4,128,512]{2,1,0:T(8,128)(2,1)}, u32[]{:S(2)}, u32[]{:S(2)}) %collective-permute-start.13) | collective-permute-done | bytes 524320 | tf_op jit(solution)/shard_map/ppermute | solution.py:195
  112.9 3.3 %collective-permute-start.20 = (bf16[4,512,128]{2,1,0:T(8,128)(2,1)S(1)}, bf16[4,512,128]{2,1,0:T(8,128)(2,1)S(1)}, u32[]{:S(2)}, u32[]{:S(2)}) collective-permute-start(bf16[4,512,128]{2,1,0:T(8,128)(2,1)S(1)} %get-tuple-element.52.refs_0_), channel_id=1, source_target_pairs={{0,2},{1,3},{2,0},{3,1},{4,6},{5,7},{6,4},{7,5},{8,10},{9,11},{10,... | collective-permute-start | bytes 1572872 | tf_op jit(solution)/shard_map/ppermute | solution.py:197
  116.2 7.0 %collective-permute-done.21.refs_6_ = bf16[4,128,512]{2,1,0:T(8,128)(2,1)S(1)} collective-permute-done((bf16[4,128,512]{2,1,0:T(8,128)(2,1)S(1)}, bf16[4,128,512]{2,1,0:T(8,128)(2,1)S(1)}, u32[]{:S(2)}, u32[]{:S(2)}) %collective-permute-start.21) | collective-permute-done | bytes 524320 | tf_op jit(solution)/shard_map/ppermute | solution.py:198
  127.8 10.3 %product.7 = (bf16[2,256,512]{2,1,0:T(8,128)(2,1)}, bf16[2,256,512]{2,1,0:T(8,128)(2,1)}, bf16[2,256,512]{2,1,0:T(8,128)(2,1)}, bf16[2,256,512]{2,1,0:T(8,128)(2,1)}) custom-call(s32[1]{0:T(128)} %bitcast.core, bf16[4,512,128]{2,1,0:T(8,128)(2,1)} %copy-done.1, bf16[4,512,128]{2,1,0:T(8,128)(2,1)} %collective-permute-done.12.refs_1_, ...), custom_call_target="tpu_custom_call" | custom-call | flops 1024 | bytes 1024 | tf_op jit(solution)/shard_map/product/pallas_call | solution.py:138
  141.7 10.2 %product.6 = (bf16[2,256,512]{2,1,0:T(8,128)(2,1)}, bf16[2,256,512]{2,1,0:T(8,128)(2,1)}, bf16[2,256,512]{2,1,0:T(8,128)(2,1)}, bf16[2,256,512]{2,1,0:T(8,128)(2,1)}) custom-call(s32[1]{0:T(128)} %bitcast.core, bf16[4,512,128]{2,1,0:T(8,128)(2,1)} %copy-done.3, bf16[4,512,128]{2,1,0:T(8,128)(2,1)} %copy-done.7, bf16[4,512,128]{2,1,0:T(8,128)(2,1)} %copy-done.8, ...), custom_call_target="tpu_custom_call" | custom-call | flops 1024 | bytes 1024 | tf_op jit(solution)/shard_map/product/pallas_call | solution.py:138
  158.0 10.2 %product.5 = (bf16[2,256,512]{2,1,0:T(8,128)(2,1)}, bf16[2,256,512]{2,1,0:T(8,128)(2,1)}, bf16[2,256,512]{2,1,0:T(8,128)(2,1)}, bf16[2,256,512]{2,1,0:T(8,128)(2,1)}) custom-call(s32[1]{0:T(128)} %bitcast.core, bf16[4,512,128]{2,1,0:T(8,128)(2,1)} %copy-done.1, bf16[4,512,128]{2,1,0:T(8,128)(2,1)} %collective-permute-done.12.refs_1_, ...), custom_call_target="tpu_custom_call" | custom-call | flops 1024 | bytes 1024 | tf_op jit(solution)/shard_map/product/pallas_call | solution.py:138
  173.8 3.2 %collective-permute-start.30 = (bf16[2,256,512]{2,1,0:T(8,128)(2,1)}, bf16[2,256,512]{2,1,0:T(8,128)(2,1)}, u32[]{:S(2)}, u32[]{:S(2)}) collective-permute-start(bf16[2,256,512]{2,1,0:T(8,128)(2,1)} %get-tuple-element.63), channel_id=1, source_target_pairs={{0,24},{16,0},{8,16},{24,8},{1,25},{17,1},{9,17},{25,9},{2,26},{18... | collective-permute-start | bytes 1572872 | tf_op jit(solution)/shard_map/ppermute | solution.py:184
  180.2 3.0 %collective-permute-done.37.refs_5_ = bf16[2,256,512]{2,1,0:T(8,128)(2,1)S(1)} collective-permute-done((bf16[2,256,512]{2,1,0:T(8,128)(2,1)S(1)}, bf16[2,256,512]{2,1,0:T(8,128)(2,1)S(1)}, u32[]{:S(2)}, u32[]{:S(2)}) %collective-permute-start.37) | collective-permute-done | bytes 524320 | tf_op jit(solution)/shard_map/ppermute | solution.py:184
  184.0 4.3 %total.2.refs_6_ = f32[256,2,2048]{2,1,0:T(2,128)} custom-call(bf16[2,256,512]{2,1,0:T(8,128)(2,1)} %get-tuple-element.68.refs_0_, bf16[2,256,512]{2,1,0:T(8,128)(2,1)} %copy-done.20, bf16[2,256,512]{2,1,0:T(8,128)(2,1)} %copy-done.19, bf16[2,256,512]{2,1,0:T(8,128)(2,1)} %get-tuple-element.70.refs_3_, bf16[2,256,512]{2,1,0:T(8,128)(2,1)} %collective-permute-done.36.refs_4_, ...), custom_call_target="tpu_custom_call" | custom-call | flops 1024 | bytes 1024 | tf_op jit(solution)/shard_map/total/pallas_call | solution.py:165
  190.7 3.8 %collective-permute-done.30.refs_2_ = bf16[2,256,512]{2,1,0:T(8,128)(2,1)} collective-permute-done((bf16[2,256,512]{2,1,0:T(8,128)(2,1)}, bf16[2,256,512]{2,1,0:T(8,128)(2,1)}, u32[]{:S(2)}, u32[]{:S(2)}) %collective-permute-start.30) | collective-permute-done | bytes 524320 | tf_op jit(solution)/shard_map/ppermute | solution.py:184
  194.5 5.7 %collective-permute-done.29.refs_1_ = bf16[2,256,512]{2,1,0:T(8,128)(2,1)} collective-permute-done((bf16[2,256,512]{2,1,0:T(8,128)(2,1)S(1)}, bf16[2,256,512]{2,1,0:T(8,128)(2,1)}, u32[]{:S(2)}, u32[]{:S(2)}) %collective-permute-start.29) | collective-permute-done | bytes 524320 | tf_op jit(solution)/shard_map/ppermute | solution.py:184
  200.3 3.1 %collective-permute-done.33.refs_5_ = bf16[2,256,512]{2,1,0:T(8,128)(2,1)S(1)} collective-permute-done((bf16[2,256,512]{2,1,0:T(8,128)(2,1)}, bf16[2,256,512]{2,1,0:T(8,128)(2,1)S(1)}, u32[]{:S(2)}, u32[]{:S(2)}) %collective-permute-start.33) | collective-permute-done | bytes 524320 | tf_op jit(solution)/shard_map/ppermute | solution.py:184
  204.2 4.3 %total.3 = f32[256,2,2048]{2,1,0:T(2,128)} custom-call(bf16[2,256,512]{2,1,0:T(8,128)(2,1)} %get-tuple-element.60.refs_0_, bf16[2,256,512]{2,1,0:T(8,128)(2,1)} %collective-permute-done.29.refs_1_, bf16[2,256,512]{2,1,0:T(8,128)(2,1)} %collective-permute-done.30.refs_2_, ...), custom_call_target="tpu_custom_call", output_to_operand_aliasing={{}: (6, {})} | custom-call | flops 1024 | bytes 1024 | tf_op jit(solution)/shard_map/total/pallas_call | solution.py:165
  (135 shorter events, 66.7 us)
Async XLA Ops:
  42.0 15.0 %collective-permute-start = (bf16[1024,128]{1,0:T(8,128)(2,1)}, bf16[1024,128]{1,0:T(8,128)(2,1)S(1)}, u32[]{:S(2)}, u32[]{:S(2)}) collective-permute-start(bf16[1024,128]{1,0:T(8,128)(2,1)} %get-tuple-element.40), channel_id=1, source_target_pairs={{0,32},{32,64},{64,96},{96,0},{1,33},{33,65},{65,97},{97,1},{2,34}... | collective-permute-start | bytes 786440 | tf_op jit(solution)/shard_map/ppermute | solution.py:242
  76.9 14.0 %collective-permute-start.19 = (bf16[4,128,512]{2,1,0:T(8,128)(2,1)S(1)}, bf16[4,128,512]{2,1,0:T(8,128)(2,1)S(1)}, u32[]{:S(2)}, u32[]{:S(2)}) collective-permute-start(bf16[4,128,512]{2,1,0:T(8,128)(2,1)S(1)} %collective-permute-done.9.refs_7_), channel_id=1, source_target_pairs={{0,4},{4,0},{1,5},{5,1},{2,6},{6,2},{3,7},{7,3},{8,12},{12,8},{9,1... | collective-permute-start | bytes 1572872 | tf_op jit(solution)/shard_map/ppermute | solution.py:220
  77.4 16.1 %collective-permute-start.17 = (bf16[4,128,512]{2,1,0:T(8,128)(2,1)S(1)}, bf16[4,128,512]{2,1,0:T(8,128)(2,1)S(1)}, u32[]{:S(2)}, u32[]{:S(2)}) collective-permute-start(bf16[4,128,512]{2,1,0:T(8,128)(2,1)S(1)} %collective-permute-done.7.refs_5_), channel_id=1, source_target_pairs={{0,4},{4,0},{1,5},{5,1},{2,6},{6,2},{3,7},{7,3},{8,12},{12,8},{9,1... | collective-permute-start | bytes 1572872 | tf_op jit(solution)/shard_map/ppermute | solution.py:220
  88.8 16.6 %collective-permute-start.14 = (bf16[4,512,128]{2,1,0:T(8,128)(2,1)S(1)}, bf16[4,512,128]{2,1,0:T(8,128)(2,1)}, u32[]{:S(2)}, u32[]{:S(2)}) collective-permute-start(bf16[4,512,128]{2,1,0:T(8,128)(2,1)S(1)} %get-tuple-element.52.refs_0_), channel_id=1, source_target_pairs={{0,3},{1,0},{2,1},{3,2},{4,7},{5,4},{6,5},{7,6},{8,11},{9,8},{10,9... | collective-permute-start | bytes 1572872 | tf_op jit(solution)/shard_map/ppermute | solution.py:194
  88.9 16.6 %collective-permute-start.12 = (bf16[4,512,128]{2,1,0:T(8,128)(2,1)S(1)}, bf16[4,512,128]{2,1,0:T(8,128)(2,1)}, u32[]{:S(2)}, u32[]{:S(2)}) collective-permute-start(bf16[4,512,128]{2,1,0:T(8,128)(2,1)S(1)} %get-tuple-element.52.refs_0_), channel_id=1, source_target_pairs={{0,1},{1,2},{2,3},{3,0},{4,5},{5,6},{6,7},{7,4},{8,9},{9,10},{10,1... | collective-permute-start | bytes 1572872 | tf_op jit(solution)/shard_map/ppermute | solution.py:194
  90.9 14.5 %collective-permute-start.15 = (bf16[4,128,512]{2,1,0:T(8,128)(2,1)S(1)}, bf16[4,128,512]{2,1,0:T(8,128)(2,1)}, u32[]{:S(2)}, u32[]{:S(2)}) collective-permute-start(bf16[4,128,512]{2,1,0:T(8,128)(2,1)S(1)} %get-tuple-element.56.refs_4_), channel_id=1, source_target_pairs={{0,96},{32,0},{64,32},{96,64},{1,97},{33,1},{65,33},{97,65},{2,98}... | collective-permute-start | bytes 1572872 | tf_op jit(solution)/shard_map/ppermute | solution.py:195
  93.6 15.3 %collective-permute-start.13 = (bf16[4,128,512]{2,1,0:T(8,128)(2,1)S(1)}, bf16[4,128,512]{2,1,0:T(8,128)(2,1)}, u32[]{:S(2)}, u32[]{:S(2)}) collective-permute-start(bf16[4,128,512]{2,1,0:T(8,128)(2,1)S(1)} %get-tuple-element.56.refs_4_), channel_id=1, source_target_pairs={{0,32},{32,64},{64,96},{96,0},{1,33},{33,65},{65,97},{97,1},{2,34}... | collective-permute-start | bytes 1572872 | tf_op jit(solution)/shard_map/ppermute | solution.py:195
  108.9 14.3 %collective-permute-start.21 = (bf16[4,128,512]{2,1,0:T(8,128)(2,1)S(1)}, bf16[4,128,512]{2,1,0:T(8,128)(2,1)S(1)}, u32[]{:S(2)}, u32[]{:S(2)}) collective-permute-start(bf16[4,128,512]{2,1,0:T(8,128)(2,1)S(1)} %get-tuple-element.56.refs_4_), channel_id=1, source_target_pairs={{0,64},{32,96},{64,0},{96,32},{1,65},{33,97},{65,1},{97,33},{2,66}... | collective-permute-start | bytes 1572872 | tf_op jit(solution)/shard_map/ppermute | solution.py:198
  108.9 15.3 %collective-permute-start.22 = (bf16[2,256,512]{2,1,0:T(8,128)(2,1)}, bf16[2,256,512]{2,1,0:T(8,128)(2,1)S(1)}, u32[]{:S(2)}, u32[]{:S(2)}) collective-permute-start(bf16[2,256,512]{2,1,0:T(8,128)(2,1)} %get-tuple-element.54), channel_id=1, source_target_pairs={{0,16},{16,8},{8,24},{24,0},{1,17},{17,9},{9,25},{25,1},{2,18},{18... | collective-permute-start | bytes 1572872 | tf_op jit(solution)/shard_map/ppermute | solution.py:184
  110.8 14.2 %collective-permute-start.23 = (bf16[2,256,512]{2,1,0:T(8,128)(2,1)}, bf16[2,256,512]{2,1,0:T(8,128)(2,1)}, u32[]{:S(2)}, u32[]{:S(2)}) collective-permute-start(bf16[2,256,512]{2,1,0:T(8,128)(2,1)} %get-tuple-element.55), channel_id=1, source_target_pairs={{0,24},{16,0},{8,16},{24,8},{1,25},{17,1},{9,17},{25,9},{2,26},{18... | collective-permute-start | bytes 1572872 | tf_op jit(solution)/shard_map/ppermute | solution.py:184
  112.9 14.1 %collective-permute-start.20 = (bf16[4,512,128]{2,1,0:T(8,128)(2,1)S(1)}, bf16[4,512,128]{2,1,0:T(8,128)(2,1)S(1)}, u32[]{:S(2)}, u32[]{:S(2)}) collective-permute-start(bf16[4,512,128]{2,1,0:T(8,128)(2,1)S(1)} %get-tuple-element.52.refs_0_), channel_id=1, source_target_pairs={{0,2},{1,3},{2,0},{3,1},{4,6},{5,7},{6,4},{7,5},{8,10},{9,11},{10,... | collective-permute-start | bytes 1572872 | tf_op jit(solution)/shard_map/ppermute | solution.py:197
  125.0 15.6 %collective-permute-start.25 = (bf16[4,128,512]{2,1,0:T(8,128)(2,1)}, bf16[4,128,512]{2,1,0:T(8,128)(2,1)S(1)}, u32[]{:S(2)}, u32[]{:S(2)}) collective-permute-start(bf16[4,128,512]{2,1,0:T(8,128)(2,1)} %collective-permute-done.13.refs_5_), channel_id=1, source_target_pairs={{0,4},{4,0},{1,5},{5,1},{2,6},{6,2},{3,7},{7,3},{8,12},{12,8},{9,1... | collective-permute-start | bytes 1572872 | tf_op jit(solution)/shard_map/ppermute | solution.py:220
  125.5 15.1 %collective-permute-start.26 = (bf16[4,128,512]{2,1,0:T(8,128)(2,1)S(1)}, bf16[4,128,512]{2,1,0:T(8,128)(2,1)S(1)}, u32[]{:S(2)}, u32[]{:S(2)}) collective-permute-start(bf16[4,128,512]{2,1,0:T(8,128)(2,1)S(1)} %collective-permute-done.21.refs_6_), channel_id=1, source_target_pairs={{0,4},{4,0},{1,5},{5,1},{2,6},{6,2},{3,7},{7,3},{8,12},{12,8},{9,1... | collective-permute-start | bytes 1572872 | tf_op jit(solution)/shard_map/ppermute | solution.py:220
  125.5 15.1 %collective-permute-start.27 = (bf16[4,128,512]{2,1,0:T(8,128)(2,1)}, bf16[4,128,512]{2,1,0:T(8,128)(2,1)}, u32[]{:S(2)}, u32[]{:S(2)}) collective-permute-start(bf16[4,128,512]{2,1,0:T(8,128)(2,1)} %collective-permute-done.15.refs_7_), channel_id=1, source_target_pairs={{0,4},{4,0},{1,5},{5,1},{2,6},{6,2},{3,7},{7,3},{8,12},{12,8},{9,1... | collective-permute-start | bytes 1572872 | tf_op jit(solution)/shard_map/ppermute | solution.py:220
  127.0 46.8 %collective-permute-start.36 = (bf16[2,256,512]{2,1,0:T(8,128)(2,1)}, bf16[2,256,512]{2,1,0:T(8,128)(2,1)}, u32[]{:S(2)}, u32[]{:S(2)}) collective-permute-start(bf16[2,256,512]{2,1,0:T(8,128)(2,1)} %get-tuple-element.71), channel_id=1, source_target_pairs={{0,16},{16,8},{8,24},{24,0},{1,17},{17,9},{9,25},{25,1},{2,18},{18... | collective-permute-start | bytes 1572872 | tf_op jit(solution)/shard_map/ppermute | solution.py:184
  138.1 38.8 %collective-permute-start.35 = (bf16[2,256,512]{2,1,0:T(8,128)(2,1)}, bf16[2,256,512]{2,1,0:T(8,128)(2,1)S(1)}, u32[]{:S(2)}, u32[]{:S(2)}) collective-permute-start(bf16[2,256,512]{2,1,0:T(8,128)(2,1)} %get-tuple-element.69), channel_id=1, source_target_pairs={{0,24},{16,0},{8,16},{24,8},{1,25},{17,1},{9,17},{25,9},{2,26},{18... | collective-permute-start | bytes 1572872 | tf_op jit(solution)/shard_map/ppermute | solution.py:184
  151.9 16.4 %collective-permute-start.28 = (bf16[2,256,512]{2,1,0:T(8,128)(2,1)}, bf16[2,256,512]{2,1,0:T(8,128)(2,1)S(1)}, u32[]{:S(2)}, u32[]{:S(2)}) collective-permute-start(bf16[2,256,512]{2,1,0:T(8,128)(2,1)} %get-tuple-element.62), channel_id=1, source_target_pairs={{0,16},{16,8},{8,24},{24,0},{1,17},{17,9},{9,25},{25,1},{2,18},{18... | collective-permute-start | bytes 1572872 | tf_op jit(solution)/shard_map/ppermute | solution.py:184
  153.3 26.1 %collective-permute-start.34 = (bf16[2,256,512]{2,1,0:T(8,128)(2,1)S(1)}, bf16[2,256,512]{2,1,0:T(8,128)(2,1)S(1)}, u32[]{:S(2)}, u32[]{:S(2)}) collective-permute-start(bf16[2,256,512]{2,1,0:T(8,128)(2,1)S(1)} %add_convert_fusion.1), channel_id=1, source_target_pairs={{0,16},{16,8},{8,24},{24,0},{1,17},{17,9},{9,25},{25,1},{2,18},{18... | collective-permute-start | bytes 1572872 | tf_op jit(solution)/shard_map/ppermute | solution.py:184
  154.1 17.4 %collective-permute-start.32 = (bf16[2,256,512]{2,1,0:T(8,128)(2,1)}, bf16[2,256,512]{2,1,0:T(8,128)(2,1)}, u32[]{:S(2)}, u32[]{:S(2)}) collective-permute-start(bf16[2,256,512]{2,1,0:T(8,128)(2,1)} %get-tuple-element.67), channel_id=1, source_target_pairs={{0,24},{16,0},{8,16},{24,8},{1,25},{17,1},{9,17},{25,9},{2,26},{18... | collective-permute-start | bytes 1572872 | tf_op jit(solution)/shard_map/ppermute | solution.py:184
  168.3 14.9 %collective-permute-start.37 = (bf16[2,256,512]{2,1,0:T(8,128)(2,1)S(1)}, bf16[2,256,512]{2,1,0:T(8,128)(2,1)S(1)}, u32[]{:S(2)}, u32[]{:S(2)}) collective-permute-start(bf16[2,256,512]{2,1,0:T(8,128)(2,1)S(1)} %add_convert_fusion), channel_id=1, source_target_pairs={{0,24},{16,0},{8,16},{24,8},{1,25},{17,1},{9,17},{25,9},{2,26},{18... | collective-permute-start | bytes 1572872 | tf_op jit(solution)/shard_map/ppermute | solution.py:184
  171.5 19.2 %collective-permute-start.31 = (bf16[2,256,512]{2,1,0:T(8,128)(2,1)}, bf16[2,256,512]{2,1,0:T(8,128)(2,1)S(1)}, u32[]{:S(2)}, u32[]{:S(2)}) collective-permute-start(bf16[2,256,512]{2,1,0:T(8,128)(2,1)} %get-tuple-element.65), channel_id=1, source_target_pairs={{0,16},{16,8},{8,24},{24,0},{1,17},{17,9},{9,25},{25,1},{2,18},{18... | collective-permute-start | bytes 1572872 | tf_op jit(solution)/shard_map/ppermute | solution.py:184
  173.8 20.8 %collective-permute-start.30 = (bf16[2,256,512]{2,1,0:T(8,128)(2,1)}, bf16[2,256,512]{2,1,0:T(8,128)(2,1)}, u32[]{:S(2)}, u32[]{:S(2)}) collective-permute-start(bf16[2,256,512]{2,1,0:T(8,128)(2,1)} %get-tuple-element.63), channel_id=1, source_target_pairs={{0,24},{16,0},{8,16},{24,8},{1,25},{17,1},{9,17},{25,9},{2,26},{18... | collective-permute-start | bytes 1572872 | tf_op jit(solution)/shard_map/ppermute | solution.py:184
  176.9 23.3 %collective-permute-start.29 = (bf16[2,256,512]{2,1,0:T(8,128)(2,1)S(1)}, bf16[2,256,512]{2,1,0:T(8,128)(2,1)}, u32[]{:S(2)}, u32[]{:S(2)}) collective-permute-start(bf16[2,256,512]{2,1,0:T(8,128)(2,1)S(1)} %add_convert_fusion.3), channel_id=1, source_target_pairs={{0,16},{16,8},{8,24},{24,0},{1,17},{17,9},{9,25},{25,1},{2,18},{18... | collective-permute-start | bytes 1572872 | tf_op jit(solution)/shard_map/ppermute | solution.py:184
  179.5 23.9 %collective-permute-start.33 = (bf16[2,256,512]{2,1,0:T(8,128)(2,1)}, bf16[2,256,512]{2,1,0:T(8,128)(2,1)S(1)}, u32[]{:S(2)}, u32[]{:S(2)}) collective-permute-start(bf16[2,256,512]{2,1,0:T(8,128)(2,1)} %add_convert_fusion.2), channel_id=1, source_target_pairs={{0,24},{16,0},{8,16},{24,8},{1,25},{17,1},{9,17},{25,9},{2,26},{18... | collective-permute-start | bytes 1572872 | tf_op jit(solution)/shard_map/ppermute | solution.py:184
  (41 other events, 584.5 us)

commit v3 on v2

--- a/solution.py
+++ b/solution.py
@@ -5,7 +5,7 @@
 from jax.sharding import Mesh, PartitionSpec as P
 from jax.experimental.pallas import tpu as pltpu
 
-VMEM = 60*2**20
+VMEM = 63*2**20
 
 
 def tables():
@@ -62,7 +62,7 @@
             held[pl.ds(pl.multiple_of(q*16, 16), 16), :] = t.astype(jnp.bfloat16)
         for s in range(4):
             a = lax.rem(place[0]+s, 4)*1024
-            for q, shift in enumerate((2, 1, 3, 0)):
+            for q, shift in enumerate((2, 0, 1, 3)):
                 to = lax.rem(place[2]+shift, 4)
                 block = lax.rem(to, 2)*2 + lax.div(to, 2)
                 outs[s][q*256:(q+1)*256, :] = held[pl.ds(pl.multiple_of(a + block*256, 256), 256), :]
@@ -89,86 +89,120 @@
     )(pos, place, val, con, jnp.asarray(first), jnp.asarray(second), scale)
 
 
-def product_kernel(core, *refs):
-    rows, own, other = refs[0:4], refs[4:8], refs[8:12]
-    outs, (left, right) = refs[12:16], refs[16:]
-    step = pl.program_id(0)
-
-    @pl.when(step == 0)
-    def _():
+def product_kernel(place, *refs):
+    rows, cols, refs = refs[0:4], refs[4:12], refs[12:]
+    got, refs = (refs[:2], refs[2:]) if len(refs) == 14 else ((), refs)
+    outs = refs[:-10]
+    left, panel, come, ready, right0, right1, row_sem, col_sem, got_sem, out_sem = refs[-10:]
+    right = (right0, right1)
+    row_copies = [
+        pltpu.make_async_copy(
+            rows[t].at[s], left.at[:, pl.ds((t*4 + s)*128, 128)], row_sem.at[t, s])
+        for t in range(4) for s in range(4)]
+    col_copies = [
+        pltpu.make_async_copy(cols[q], panel.at[q], col_sem.at[q]) for q in range(8)]
+    got_copies = [pltpu.make_async_copy(got[h], come.at[h], got_sem.at[h]) for h in range(len(got))]
+    for copy in col_copies[:4] + row_copies + col_copies[4:] + got_copies:
+        copy.start()
+
+    def fill(n):
+        into, h = right[n % 2], n % 2
         for t in range(4):
             for s in range(4):
                 k = (t*4 + s)*128
-                left[:, k:k+128] = rows[t][s]
-
-    def fill(cols):
-        for t in range(4):
-            for s in range(4):
-                k = (t*4 + s)*128
-                piece = cols[s][t]
-                right[k:k+128, 0:256] = piece
-                right[k:k+64, 256:512] = -piece[64:128]
-                right[k+64:k+128, 256:512] = piece[0:64]
-
-    @pl.when(step < 2)
-    def _():
-        fill(own)
-
-    @pl.when(step >= 2)
-    def _():
-        fill(other)
-
-    tile = jnp.dot(left[...], right[...], preferred_element_type=jnp.float32)
-    tile = tile.astype(jnp.bfloat16)
-    for h in range(2):
-        @pl.when(lax.rem(step, 2) == h)
-        def _(h=h):
-            for b in range(2):
-                for o in range(2):
-                    outs[2*b + h][o] = tile[b*256:(b+1)*256, o*256:(o+1)*256]
-
-
-def product(core, rows, own, other):
-    full = pl.BlockSpec((4, 512, 128), lambda n, core: (0, 0, 0))
-    near = pl.BlockSpec((4, 128, 256), lambda n, core: (0, 0, jnp.minimum(n, 1)))
-    far = pl.BlockSpec((4, 128, 256), lambda n, core: (0, 0, jnp.maximum(n - 2, 0)))
-    out = pl.BlockSpec(
-        (2, 256, 256),
-        lambda n, core: (0, 0, core[0] + n//2 - 2*core[0]*(n//2)))
+                piece = panel[4*(n//2) + s, t, :, h*256:(h+1)*256]
+                into[k:k+128, 0:256] = piece
+                into[k:k+64, 256:512] = -piece[64:128]
+                into[k+64:k+128, 256:512] = piece[0:64]
+
+    for copy in col_copies[:4]:
+        copy.wait()
+    fill(0)
+    for copy in row_copies:
+        copy.wait()
+    leaving = []
+    for n in range(4):
+        if n == 1:
+            for copy in col_copies[4:]:
+                copy.wait()
+        if n < 3:
+            fill(n + 1)
+        tile = jnp.dot(left[...], right[n % 2][...], preferred_element_type=jnp.float32)
+        if n == 0:
+            for copy in got_copies:
+                copy.wait()
+        h = n % 2
+        side = place[0] + n//2 - 2*place[0]*(n//2)
+        at = pl.multiple_of(side*256, 256)
+        for o in range(2):
+            one = tile[0:256, o*256:(o+1)*256]
+            two = tile[256:512, o*256:(o+1)*256]
+            if got:
+                more = come[h, o, :, pl.ds(at, 256)].astype(jnp.float32)
+                one, two = (one + more, two) if h == 0 else (one, two + more)
+            ready[n, 0, o] = one.astype(jnp.bfloat16)
+            ready[n, 1, o] = two.astype(jnp.bfloat16)
+        wide = pl.ds(pl.multiple_of(h*512 + at, 256), 256)
+        if got:
+            first = outs[0].at[:, :, wide]
+        else:
+            first = outs[h].at[:, :, pl.ds(at, 256)]
+        for b, to in enumerate((first, outs[-1].at[:, :, wide])):
+            copy = pltpu.make_async_copy(ready.at[n, b], to, out_sem.at[n, b])
+            copy.start()
+            leaving.append(copy)
+    for copy in leaving:
+        copy.wait()
+
+
+def product(place, rows, own, other, got):
+    wide = jax.ShapeDtypeStruct((2, 256, 1024), jnp.bfloat16)
+    slim = jax.ShapeDtypeStruct((2, 256, 512), jnp.bfloat16)
+    shapes = [wide, wide] if got else [slim, slim, wide]
+    anywhere = pl.BlockSpec(memory_space=pl.ANY)
     return pl.pallas_call(
         product_kernel,
         grid_spec=pltpu.PrefetchScalarGridSpec(
-            num_scalar_prefetch=1, grid=(4,),
-            in_specs=[full]*4 + [near]*4 + [far]*4,
-            out_specs=[out]*4,
-            scratch_shapes=[pltpu.VMEM((512, 2048), jnp.bfloat16), pltpu.VMEM((2048, 512), jnp.bfloat16)],
+            num_scalar_prefetch=1, grid=(1,),
+            in_specs=[anywhere]*(12 + len(got)),
+            out_specs=[anywhere]*len(shapes),
+            scratch_shapes=[
+                pltpu.VMEM((512, 2048), jnp.bfloat16),
+                pltpu.VMEM((8, 4, 128, 512), jnp.bfloat16),
+                pltpu.VMEM((2, 2, 256, 512), jnp.bfloat16),
+                pltpu.VMEM((4, 2, 2, 256, 256), jnp.bfloat16),
+                pltpu.VMEM((2048, 512), jnp.bfloat16),
+                pltpu.VMEM((2048, 512), jnp.bfloat16),
+                pltpu.SemaphoreType.DMA((4, 4)),
+                pltpu.SemaphoreType.DMA((8,)),
+                pltpu.SemaphoreType.DMA((2,)),
+                pltpu.SemaphoreType.DMA((4, 2)),
+            ],
         ),
-        out_shape=[jax.ShapeDtypeStruct((2, 256, 512), jnp.bfloat16)]*4,
+        out_shape=shapes,
         compiler_params=pltpu.CompilerParams(vmem_limit_bytes=VMEM),
         cost_estimate=pl.CostEstimate(flops=2**10, bytes_accessed=2**10, transcendentals=0),
         name="product",
-    )(core, *rows, *own, *other)
-
-
-def total_kernel(*refs):
-    out = refs[-1]
-    for h in range(2):
-        t = refs[3*h][...].astype(jnp.float32) + refs[3*h+1][...].astype(jnp.float32)
-        t = t + refs[3*h+2][...].astype(jnp.float32)
-        out[:, 0, h*512:(h+1)*512] = t[0]
-        out[:, 1, h*512:(h+1)*512] = t[1]
+    )(place, *rows, *own, *other, *got)
+
+
+def total_kernel(a, b, c, *rest):
+    out = rest[-1]
+    t = a[...].astype(jnp.float32) + b[...].astype(jnp.float32) + c[...].astype(jnp.float32)
+    out[:, 0, :] = t[0]
+    out[:, 1, :] = t[1]
 
 
 def total(parts, chunk, before):
-    spec = pl.BlockSpec((2, 64, 512), lambda n: (0, n, 0))
+    spec = pl.BlockSpec((2, 64, 1024), lambda n: (0, n, 0))
     more = [] if before is None else [before]
     return pl.pallas_call(
         total_kernel,
         grid=(4,),
-        in_specs=[spec]*6 + [pl.BlockSpec(memory_space=pl.ANY)]*len(more),
+        in_specs=[spec]*3 + [pl.BlockSpec(memory_space=pl.ANY)]*len(more),
         out_specs=pl.BlockSpec((64, 2, 1024), lambda n: (n, 0, chunk)),
         out_shape=jax.ShapeDtypeStruct((256, 2, 2048), jnp.float32),
-        input_output_aliases={6: 0} if more else {},
+        input_output_aliases={3: 0} if more else {},
         compiler_params=pltpu.CompilerParams(vmem_limit_bytes=VMEM),
         cost_estimate=pl.CostEstimate(flops=2**10, bytes_accessed=2**10, transcendentals=0),
         name="total",
@@ -186,34 +220,6 @@
 
 def after(arrays, *first):
     return lax.optimization_barrier((tuple(arrays), first))[0]
-
-
-def spread(row, col, *first):
-    rows, cols = [row] + [None]*3, [col] + [None]*3
-    for s in (1, 3):
-        rows[s] = lax.ppermute(row, "y", ring(s))
-        cols[s] = lax.ppermute(col, "x", ring(s))
-    row, col = after((row, col), rows[1], cols[1], rows[3], cols[3], *first)
-    rows[2] = lax.ppermute(row, "y", ring(2))
-    cols[2] = lax.ppermute(col, "x", ring(2))
-    return rows, cols
-
-
-def add(a, b):
-    return (a.astype(jnp.float32) + b.astype(jnp.float32)).astype(jnp.bfloat16)
-
-
-def begun(far):
-    far0, far1, next0, next1 = far
-    return next0, along_z(far0, 1), along_z(far1, -1), along_z(next1, 1)
-
-
-def ended(far, near):
-    next0, got0, got1, up1 = far
-    last0, last1, mine0, mine1 = near
-    down0 = along_z(last0, -1)
-    up0, down1 = along_z(add(next0, got0), 1), along_z(add(last1, got1), -1)
-    return [mine0, up0, down0, mine1, up1, down1]
 
 
 def swapped(blocks):
@@ -227,14 +233,18 @@
     vb, cb = (y*2 + zl)*8, (x*2 + zh)*8
     val = lax.dynamic_slice(valence_waves, (vb, 0, 0), (8, 2, 32768)).reshape(8, 2, 256, 128)
     con = lax.dynamic_slice(conduction_waves, (cb, 0, 0), (8, 2, 32768)).reshape(8, 2, 256, 128)
-    gap = lax.dynamic_slice(conduction_energy, (cb,), (8,))[None, :] - lax.dynamic_slice(valence_energy, (vb,), (8,))[:, None]
+    channel = lax.iota(jnp.int32, 128)[:, None] % 64
+    band = lax.iota(jnp.int32, 64)[None, :]
+    gap = jnp.sum(
+        jnp.where(band == cb + channel % 8, conduction_energy[None, :], 0.0)
+        - jnp.where(band == vb + channel//8, valence_energy[None, :], 0.0), axis=1)
     weight = 4.0 * gap / (gap*gap + frequency[0]*frequency[0]) / 4096
-    scale = jnp.sqrt(weight / 32768.0).reshape(1, 64)
-    scale = jnp.concatenate([scale, scale], 1)
+    scale = jnp.sqrt(weight / 32768.0)[None, :]
     point = lax.dynamic_index_in_dim(sphere_map.reshape(16, 2, 256), core, 1, keepdims=False).reshape(4096)
     ky = (point >> 5) & 31
     pos = ((ky & 7)*32 + (point >> 10))*128 + (ky >> 3)*32 + (point & 31)
     place = jnp.stack([x, y, zh*2 + zl]).astype(jnp.int32)
+    where = jnp.stack([core, x]).astype(jnp.int32)
     parts = densities(pos, place, val, con, scale)
     row = [parts[0]] + [None]*3
     col = [parts[4]] + [None]*3
@@ -242,19 +252,33 @@
         row[s] = lax.ppermute(parts[s], "x", ring(s))
         col[s] = lax.ppermute(parts[4 + s], "y", ring(s))
     row, col = jnp.stack(row), jnp.stack(col)
-    which = core.astype(jnp.int32)[None]
     row_a, col_a = row[:, :512], col[:, :, :512]
     row_b, col_b = row[:, 512:], col[:, :, 512:]
-    rows_a, own_a = spread(row_a, col_a)
+    rows_a, own_a = [row_a] + [None]*3, [col_a] + [None]*3
+    for s in (1, 3):
+        rows_a[s] = lax.ppermute(row_a, "y", ring(s))
+        own_a[s] = lax.ppermute(col_a, "x", ring(s))
+    rows_a[2] = lax.ppermute(row_a, "y", ring(2))
+    col_a = after((col_a,), own_a[1], own_a[3])[0]
+    own_a[2] = lax.ppermute(col_a, "x", ring(2))
     other_a = swapped(own_a)
-    row_b, col_b = after((row_b, col_b), rows_a[2], own_a[2])
-    aa = begun(product(which, rows_a, own_a, other_a))
-    rows_b, own_b = spread(row_b, col_b, aa[0])
-    other_b = swapped(after(own_b, aa[1], aa[2]))
-    ba = product(which, rows_b, own_a, other_a)
-    ab = begun(product(which, rows_a, own_b, other_b))
-    bb = product(which, rows_b, own_b, other_b)
-    return total(ended(ab, bb), 1, total(ended(aa, ba), 0, None))
+    row_b, col_b = after((row_b, col_b), rows_a[2], own_a[2], other_a[0], other_a[1], other_a[3])
+    rows_b, own_b = [row_b] + [None]*3, [col_b] + [None]*3
+    for s in (1, 3):
+        rows_b[s] = lax.ppermute(row_b, "y", ring(s))
+        own_b[s] = lax.ppermute(col_b, "x", ring(s))
+    own_b[2] = lax.ppermute(col_b, "x", ring(2))
+    far0, far1, mine_a = product(where, rows_a, own_a, other_a, [])
+    got_a = [along_z(far0, 1), along_z(far1, -1)]
+    rows_b[2] = lax.ppermute(after((row_b,), far0, rows_b[1], rows_b[3])[0], "y", ring(2))
+    other_b = swapped(after(own_b, far0))
+    far0, far1, mine_b = product(where, rows_a, own_b, other_b, [])
+    got_b = [along_z(far0, 1), along_z(far1, -1)]
+    up_a, down_a = product(where, rows_b, own_a, other_a, got_a)
+    done_a = [mine_a, along_z(up_a, 1), along_z(down_a, -1)]
+    up_b, down_b = product(where, rows_b, own_b, other_b, got_b)
+    done_b = [mine_b, along_z(up_b, 1), along_z(down_b, -1)]
+    return total(done_b, 1, total(done_a, 0, None))
 
 
 def solution(mesh):

time: 210 us -> 196 us (0.933)
  other arithmetic: 9.48 us -> 4.06 us
  local copies, waits for them, and re-layouts: 15.7 us -> 11.3 us
  Pallas kernels: 74.6 us -> 70.7 us
  waiting for transfers between devices: 58.6 us -> 61.6 us
  starting transfers between devices: 49.1 us -> 47 us
    convert_element_type x4 -> x0, other arithmetic: 6.04 us -> none  [add(): return (a.astype(jnp.float32) + b.astype(jnp.float32)).astype(jnp.bfloat16)]
    ppermute x12 -> x8, waiting for transfers between devices: 21.6 us -> 27.1 us  [along_z(): lax.ppermute(block, ('zl', 'zh'), [(place(i), place((i + shift) % 4)) for...]
    unnamed x55 -> x35, local copies, waits for them, and re-layouts: 6.09 us -> 2.26 us
    pallas_call x4, Pallas kernels: 41 us -> 37.2 us  [product(): pl.pallas_call(product_kernel, grid_spec=pltpu.PrefetchScalarGridSpec(num...]
    ppermute x12, starting transfers between devices: 19.7 us -> 17.5 us  [the longest x1 3.47 us: local(): lax.ppermute(after((row_b,), far0, rows_b[1], rows_b[3])[0], 'y', ring(2))]
    ppermute x12 -> x8, starting transfers between devices: 16 us -> 16 us  [along_z(): lax.ppermute(block, ('zl', 'zh'), [(place(i), place((i + shift) % 4)) for...]
  transfers between devices with their start and end apart: 38 -> 34, of which waited for: 21 -> 11; matrix products, arithmetic and copies ran while one was open for 4% -> 2% of each run, Pallas kernels for 22% -> 21%
where the time goes in v3:
time: 196 us
  Pallas kernels  70.7 us (36%)
  waiting for transfers between devices  61.6 us (31%)
  starting transfers between devices  47 us (24%)
  local copies, waits for them, and re-layouts  11.3 us (6%)
  other arithmetic  4.06 us (2%)
    pallas_call x4, Pallas kernels, product(): pl.pallas_call(product_kernel, grid_spec=pltpu.PrefetchScalarGridSpec(num...  37.2 us
    ppermute x8, waiting for transfers between devices, along_z(): lax.ppermute(block, ('zl', 'zh'), [(place(i), place((i + shift) % 4)) for...  27.1 us
    pallas_call x1, Pallas kernels, densities(): pl.pallas_call(density_kernel, grid_spec=pltpu.PrefetchScalarGridSpec(num...  25.1 us
    ppermute x8, starting transfers between devices, along_z(): lax.ppermute(block, ('zl', 'zh'), [(place(i), place((i + shift) % 4)) for...  16 us
    ppermute x2, waiting for transfers between devices, local(): own_a[s] = lax.ppermute(col_a, 'x', ring(s))  10.1 us
    ppermute x2, waiting for transfers between devices, local(): own_b[s] = lax.ppermute(col_b, 'x', ring(s))  10.1 us
    ppermute x1, waiting for transfers between devices, local(): own_a[2] = lax.ppermute(col_a, 'x', ring(2))  8.54 us
    pallas_call x2, Pallas kernels, total(): pl.pallas_call(total_kernel, grid=(4,), in_specs=[spec] * 3 + [pl.BlockSp...  8.41 us
  transfers between devices with their start and end apart: 34, of which 11 were waited for; matrix products, arithmetic and copies ran while one was open for 2% of the time, Pallas kernels for 21%

profile of v3, /device:TPU:8, one launch (start us, length us, event | category | flops | bytes accessed | tf_op | source)
XLA Modules:
  0.0 195.5 jit_solution(230470879995741056)
XLA Ops:
  9.8 25.1 %densities.1 = (bf16[1024,128]{1,0:T(8,128)(2,1)}, bf16[1024,128]{1,0:T(8,128)(2,1)}, bf16[1024,128]{1,0:T(8,128)(2,1)}, bf16[1024,128]{1,0:T(8,128)(2,1)}, bf16...) custom-call(s32[4096]{0:T(1024)} %bitcast.27, ...), custom_call_target="tpu_custom_call" | custom-call | tf_op jit(solution)/shard_map/densities/pallas_call | solution.py:77
  37.3 2.5 %collective-permute-start.8 = (bf16[128,1024]{1,0:T(8,128)(2,1)}, bf16[128,1024]{1,0:T(8,128)(2,1)S(1)}, u32[]{:S(2)}, u32[]{:S(2)}) collective-permute-start(bf16[128,1024]{1,0:T(8,128)(2,1)} %get-tuple-element.38), channel_id=1, source_target_pairs={{0,3},{1,0},{2,1},{3,2},{4,7},{5,4},{6,5},{7,6},{8,11},{9,8},{10,9... | collective-permute-start | bytes 786440 | tf_op jit(solution)/shard_map/ppermute | solution.py:253
  41.3 2.7 %collective-permute-start.1 = (bf16[1024,128]{1,0:T(8,128)(2,1)}, bf16[1024,128]{1,0:T(8,128)(2,1)S(1)}, u32[]{:S(2)}, u32[]{:S(2)}) collective-permute-start(bf16[1024,128]{1,0:T(8,128)(2,1)} %get-tuple-element.33), channel_id=1, source_target_pairs={{0,64},{32,96},{64,0},{96,32},{1,65},{33,97},{65,1},{97,33},{2,66}... | collective-permute-start | bytes 786440 | tf_op jit(solution)/shard_map/ppermute | solution.py:252
  44.2 2.8 %collective-permute-start.2 = (bf16[1024,128]{1,0:T(8,128)(2,1)}, bf16[1024,128]{1,0:T(8,128)(2,1)S(1)}, u32[]{:S(2)}, u32[]{:S(2)}) collective-permute-start(bf16[1024,128]{1,0:T(8,128)(2,1)} %get-tuple-element.34), channel_id=1, source_target_pairs={{0,96},{32,0},{64,32},{96,64},{1,97},{33,1},{65,33},{97,65},{2,98}... | collective-permute-start | bytes 786440 | tf_op jit(solution)/shard_map/ppermute | solution.py:252
  47.4 3.4 %collective-permute-done.8 = bf16[128,1024]{1,0:T(8,128)(2,1)S(1)} collective-permute-done((bf16[128,1024]{1,0:T(8,128)(2,1)}, bf16[128,1024]{1,0:T(8,128)(2,1)S(1)}, u32[]{:S(2)}, u32[]{:S(2)}) %collective-permute-start.8) | collective-permute-done | bytes 262176 | tf_op jit(solution)/shard_map/ppermute | solution.py:253
  52.8 2.8 %collective-permute-start.10 = (bf16[4,128,512]{2,1,0:T(8,128)(2,1)S(1)}, bf16[4,128,512]{2,1,0:T(8,128)(2,1)S(1)}, u32[]{:S(2)}, u32[]{:S(2)}) collective-permute-start(bf16[4,128,512]{2,1,0:T(8,128)(2,1)S(1)} %get-tuple-element.39.refs_4_), channel_id=1, source_target_pairs={{0,96},{32,0},{64,32},{96,64},{1,97},{33,1},{65,33},{97,65},{2,98}... | collective-permute-start | bytes 1572872 | tf_op jit(solution)/shard_map/ppermute | solution.py:260
  59.4 6.7 %collective-permute-done.10.refs_7_ = bf16[4,128,512]{2,1,0:T(8,128)(2,1)S(1)} collective-permute-done((bf16[4,128,512]{2,1,0:T(8,128)(2,1)S(1)}, bf16[4,128,512]{2,1,0:T(8,128)(2,1)S(1)}, u32[]{:S(2)}, u32[]{:S(2)}) %collective-permute-start.10) | collective-permute-done | bytes 524320 | tf_op jit(solution)/shard_map/ppermute | solution.py:260
  66.1 3.4 %collective-permute-done.9.refs_5_ = bf16[4,128,512]{2,1,0:T(8,128)(2,1)S(1)} collective-permute-done((bf16[4,128,512]{2,1,0:T(8,128)(2,1)S(1)}, bf16[4,128,512]{2,1,0:T(8,128)(2,1)S(1)}, u32[]{:S(2)}, u32[]{:S(2)}) %collective-permute-start.9) | collective-permute-done | bytes 524320 | tf_op jit(solution)/shard_map/ppermute | solution.py:260
  74.3 8.5 %collective-permute-done.11.refs_6_ = bf16[4,128,512]{2,1,0:T(8,128)(2,1)S(1)} collective-permute-done((bf16[4,128,512]{2,1,0:T(8,128)(2,1)S(1)}, bf16[4,128,512]{2,1,0:T(8,128)(2,1)S(1)}, u32[]{:S(2)}, u32[]{:S(2)}) %collective-permute-start.11) | collective-permute-done | bytes 524320 | tf_op jit(solution)/shard_map/ppermute | solution.py:263
  85.1 2.7 %collective-permute-start.17 = (bf16[4,128,512]{2,1,0:T(8,128)(2,1)}, bf16[4,128,512]{2,1,0:T(8,128)(2,1)}, u32[]{:S(2)}, u32[]{:S(2)}) collective-permute-start(bf16[4,128,512]{2,1,0:T(8,128)(2,1)} %get-tuple-element.42.refs_4_), channel_id=1, source_target_pairs={{0,96},{32,0},{64,32},{96,64},{1,97},{33,1},{65,33},{97,65},{2,98}... | collective-permute-start | bytes 1572872 | tf_op jit(solution)/shard_map/ppermute | solution.py:269
  91.4 9.2 %product.4 = (bf16[2,256,512]{2,1,0:T(8,128)(2,1)}, bf16[2,256,512]{2,1,0:T(8,128)(2,1)}, bf16[2,256,1024]{2,1,0:T(8,128)(2,1)}) custom-call(s32[2]{0:T(128)} %pad_add_fusion.place, bf16[4,512,128]{2,1,0:T(8,128)(2,1)} %copy-done, bf16[4,512,128]{2,1,0:T(8,128)(2,1)} %copy-done.3, bf16[4,512,128]{2,1,0:T(8,128)(2,1)} %copy-done.2, ...), custom_call_target="tpu_custom_call" | custom-call | flops 1024 | bytes 1024 | tf_op jit(solution)/shard_map/product/pallas_call | solution.py:163
  100.6 9.5 %collective-permute-done.15.refs_5_ = bf16[4,128,512]{2,1,0:T(8,128)(2,1)} collective-permute-done((bf16[4,128,512]{2,1,0:T(8,128)(2,1)}, bf16[4,128,512]{2,1,0:T(8,128)(2,1)}, u32[]{:S(2)}, u32[]{:S(2)}) %collective-permute-start.15) | collective-permute-done | bytes 524320 | tf_op jit(solution)/shard_map/ppermute | solution.py:269
  113.6 3.5 %collective-permute-start.25 = (bf16[4,512,128]{2,1,0:T(8,128)(2,1)}, bf16[4,512,128]{2,1,0:T(8,128)(2,1)}, u32[]{:S(2)}, u32[]{:S(2)}) collective-permute-start(bf16[4,512,128]{2,1,0:T(8,128)(2,1)} %get-tuple-element.48.refs_0_), channel_id=1, source_target_pairs={{0,2},{1,3},{2,0},{3,1},{4,6},{5,7},{6,4},{7,5},{8,10},{9,11},{10,... | collective-permute-start | bytes 1572872 | tf_op jit(solution)/shard_map/ppermute | solution.py:273
  117.1 3.9 %collective-permute-start.31 = (bf16[2,256,512]{2,1,0:T(8,128)(2,1)}, bf16[2,256,512]{2,1,0:T(8,128)(2,1)}, u32[]{:S(2)}, u32[]{:S(2)}) collective-permute-start(bf16[2,256,512]{2,1,0:T(8,128)(2,1)} %get-tuple-element.54), channel_id=1, source_target_pairs={{0,24},{16,0},{8,16},{24,8},{1,25},{17,1},{9,17},{25,9},{2,26},{18... | collective-permute-start | bytes 1572872 | tf_op jit(solution)/shard_map/ppermute | solution.py:218
  121.0 9.2 %product.5 = (bf16[2,256,512]{2,1,0:T(8,128)(2,1)}, bf16[2,256,512]{2,1,0:T(8,128)(2,1)}, bf16[2,256,1024]{2,1,0:T(8,128)(2,1)}) custom-call(s32[2]{0:T(128)} %pad_add_fusion.place, bf16[4,512,128]{2,1,0:T(8,128)(2,1)} %copy-done, bf16[4,512,128]{2,1,0:T(8,128)(2,1)} %copy-done.3, bf16[4,512,128]{2,1,0:T(8,128)(2,1)} %copy-done.2, ...), custom_call_target="tpu_custom_call" | custom-call | flops 1024 | bytes 1024 | tf_op jit(solution)/shard_map/product/pallas_call | solution.py:163
  130.3 3.2 %collective-permute-start.27 = (bf16[2,256,512]{2,1,0:T(8,128)(2,1)}, bf16[2,256,512]{2,1,0:T(8,128)(2,1)}, u32[]{:S(2)}, u32[]{:S(2)}) collective-permute-start(bf16[2,256,512]{2,1,0:T(8,128)(2,1)} %get-tuple-element.50), channel_id=1, source_target_pairs={{0,24},{16,0},{8,16},{24,8},{1,25},{17,1},{9,17},{25,9},{2,26},{18... | collective-permute-start | bytes 1572872 | tf_op jit(solution)/shard_map/ppermute | solution.py:218
  133.6 9.4 %product.7 = (bf16[2,256,1024]{2,1,0:T(8,128)(2,1)}, bf16[2,256,1024]{2,1,0:T(8,128)(2,1)}) custom-call(s32[2]{0:T(128)} %pad_add_fusion.place, bf16[4,512,128]{2,1,0:T(8,128)(2,1)} %get-tuple-element.48.refs_0_, bf16[4,512,128]{2,1,0:T(8,128)(2,1)} %collective-permute-done.23.refs_1_, bf16[4,512,128]{2,1,0:T(8,128)(2,1)} %collective-permute-done.25.refs_2_, ...), custom_call_target="tpu_custom_call" | custom-call | flops 1024 | bytes 1024 | tf_op jit(solution)/shard_map/product/pallas_call | solution.py:163
  143.3 3.2 %collective-permute-start.33 = (bf16[2,256,1024]{2,1,0:T(8,128)(2,1)}, bf16[2,256,1024]{2,1,0:T(8,128)(2,1)}, u32[]{:S(2)}, u32[]{:S(2)}) collective-permute-start(bf16[2,256,1024]{2,1,0:T(8,128)(2,1)} %get-tuple-element.56), channel_id=1, source_target_pairs={{0,24},{16,0},{8,16},{24,8},{1,25},{17,1},{9,17},{25,9},{2,26},{18... | collective-permute-start | bytes 3145736 | tf_op jit(solution)/shard_map/ppermute | solution.py:218
  147.3 9.4 %product.6 = (bf16[2,256,1024]{2,1,0:T(8,128)(2,1)}, bf16[2,256,1024]{2,1,0:T(8,128)(2,1)}) custom-call(s32[2]{0:T(128)} %pad_add_fusion.place, bf16[4,512,128]{2,1,0:T(8,128)(2,1)} %get-tuple-element.48.refs_0_, bf16[4,512,128]{2,1,0:T(8,128)(2,1)} %collective-permute-done.23.refs_1_, bf16[4,512,128]{2,1,0:T(8,128)(2,1)} %collective-permute-done.25.refs_2_, ...), custom_call_target="tpu_custom_call" | custom-call | flops 1024 | bytes 1024 | tf_op jit(solution)/shard_map/product/pallas_call | solution.py:163
  156.8 3.2 %collective-permute-start.29 = (bf16[2,256,1024]{2,1,0:T(8,128)(2,1)}, bf16[2,256,1024]{2,1,0:T(8,128)(2,1)}, u32[]{:S(2)}, u32[]{:S(2)}) collective-permute-start(bf16[2,256,1024]{2,1,0:T(8,128)(2,1)} %get-tuple-element.52), channel_id=1, source_target_pairs={{0,24},{16,0},{8,16},{24,8},{1,25},{17,1},{9,17},{25,9},{2,26},{18... | collective-permute-start | bytes 3145736 | tf_op jit(solution)/shard_map/ppermute | solution.py:218
  160.1 10.8 %collective-permute-done.32.b = bf16[2,256,1024]{2,1,0:T(8,128)(2,1)} collective-permute-done((bf16[2,256,1024]{2,1,0:T(8,128)(2,1)}, bf16[2,256,1024]{2,1,0:T(8,128)(2,1)}, u32[]{:S(2)}, u32[]{:S(2)}) %collective-permute-start.32) | collective-permute-done | bytes 1048608 | tf_op jit(solution)/shard_map/ppermute | solution.py:218
  170.9 4.2 %total.2.rest_0_ = f32[256,2,2048]{2,1,0:T(2,128)} custom-call(bf16[2,256,1024]{2,1,0:T(8,128)(2,1)} %get-tuple-element.53.a, bf16[2,256,1024]{2,1,0:T(8,128)(2,1)} %collective-permute-done.32.b, bf16[2,256,1024]{2,1,0:T(8,128)(2,1)} %collective-permute-done.33.c), custom_call_target="tpu_custom_call" | custom-call | flops 1024 | bytes 1024 | tf_op jit(solution)/shard_map/total/pallas_call | solution.py:199
  175.1 16.2 %collective-permute-done.28.b = bf16[2,256,1024]{2,1,0:T(8,128)(2,1)} collective-permute-done((bf16[2,256,1024]{2,1,0:T(8,128)(2,1)}, bf16[2,256,1024]{2,1,0:T(8,128)(2,1)}, u32[]{:S(2)}, u32[]{:S(2)}) %collective-permute-start.28) | collective-permute-done | bytes 1048608 | tf_op jit(solution)/shard_map/ppermute | solution.py:218
  191.3 4.2 %total.3 = f32[256,2,2048]{2,1,0:T(2,128)} custom-call(bf16[2,256,1024]{2,1,0:T(8,128)(2,1)} %get-tuple-element.46.a, bf16[2,256,1024]{2,1,0:T(8,128)(2,1)} %collective-permute-done.28.b, bf16[2,256,1024]{2,1,0:T(8,128)(2,1)} %collective-permute-done.29.c, f32[256,2,2048]{2,1,0:T(2,128)} %total.2.rest_0_), custom_call_target="tpu_custom_call", output_to_operand_aliasing={{}: (3, {})} | custom-call | flops 1024 | bytes 1024 | tf_op jit(solution)/shard_map/total/pallas_call | solution.py:199
  (102 shorter events, 34.9 us)
Async XLA Ops:
  37.3 13.5 %collective-permute-start.8 = (bf16[128,1024]{1,0:T(8,128)(2,1)}, bf16[128,1024]{1,0:T(8,128)(2,1)S(1)}, u32[]{:S(2)}, u32[]{:S(2)}) collective-permute-start(bf16[128,1024]{1,0:T(8,128)(2,1)} %get-tuple-element.38), channel_id=1, source_target_pairs={{0,3},{1,0},{2,1},{3,2},{4,7},{5,4},{6,5},{7,6},{8,11},{9,8},{10,9... | collective-permute-start | bytes 786440 | tf_op jit(solution)/shard_map/ppermute | solution.py:253
  39.8 15.8 %collective-permute-start = (bf16[1024,128]{1,0:T(8,128)(2,1)}, bf16[1024,128]{1,0:T(8,128)(2,1)S(1)}, u32[]{:S(2)}, u32[]{:S(2)}) collective-permute-start(bf16[1024,128]{1,0:T(8,128)(2,1)} %get-tuple-element.32), channel_id=1, source_target_pairs={{0,32},{32,64},{64,96},{96,0},{1,33},{33,65},{65,97},{97,1},{2,34}... | collective-permute-start | bytes 786440 | tf_op jit(solution)/shard_map/ppermute | solution.py:252
  41.3 14.3 %collective-permute-start.1 = (bf16[1024,128]{1,0:T(8,128)(2,1)}, bf16[1024,128]{1,0:T(8,128)(2,1)S(1)}, u32[]{:S(2)}, u32[]{:S(2)}) collective-permute-start(bf16[1024,128]{1,0:T(8,128)(2,1)} %get-tuple-element.33), channel_id=1, source_target_pairs={{0,64},{32,96},{64,0},{96,32},{1,65},{33,97},{65,1},{97,33},{2,66}... | collective-permute-start | bytes 786440 | tf_op jit(solution)/shard_map/ppermute | solution.py:252
  55.5 14.0 %collective-permute-start.9 = (bf16[4,128,512]{2,1,0:T(8,128)(2,1)S(1)}, bf16[4,128,512]{2,1,0:T(8,128)(2,1)S(1)}, u32[]{:S(2)}, u32[]{:S(2)}) collective-permute-start(bf16[4,128,512]{2,1,0:T(8,128)(2,1)S(1)} %get-tuple-element.39.refs_4_), channel_id=1, source_target_pairs={{0,32},{32,64},{64,96},{96,0},{1,33},{33,65},{65,97},{97,1},{2,34}... | collective-permute-start | bytes 1572872 | tf_op jit(solution)/shard_map/ppermute | solution.py:260
  55.5 14.5 %collective-permute-start.12 = (bf16[4,128,512]{2,1,0:T(8,128)(2,1)S(1)}, bf16[4,128,512]{2,1,0:T(8,128)(2,1)S(1)}, u32[]{:S(2)}, u32[]{:S(2)}) collective-permute-start(bf16[4,128,512]{2,1,0:T(8,128)(2,1)S(1)} %get-tuple-element.39.refs_4_), channel_id=1, source_target_pairs={{0,4},{4,0},{1,5},{5,1},{2,6},{6,2},{3,7},{7,3},{8,12},{12,8},{9,1... | collective-permute-start | bytes 1572872 | tf_op jit(solution)/shard_map/ppermute | solution.py:226
  57.6 15.8 %collective-permute-start.4 = (bf16[4,512,128]{2,1,0:T(8,128)(2,1)S(1)}, bf16[4,512,128]{2,1,0:T(8,128)(2,1)S(1)}, u32[]{:S(2)}, u32[]{:S(2)}) collective-permute-start(bf16[4,512,128]{2,1,0:T(8,128)(2,1)S(1)} %get-tuple-element.60.refs_0_), channel_id=1, source_target_pairs={{0,2},{1,3},{2,0},{3,1},{4,6},{5,7},{6,4},{7,5},{8,10},{9,11},{10,... | collective-permute-start | bytes 1572872 | tf_op jit(solution)/shard_map/ppermute | solution.py:261
  69.5 13.3 %collective-permute-start.13 = (bf16[4,128,512]{2,1,0:T(8,128)(2,1)S(1)}, bf16[4,128,512]{2,1,0:T(8,128)(2,1)S(1)}, u32[]{:S(2)}, u32[]{:S(2)}) collective-permute-start(bf16[4,128,512]{2,1,0:T(8,128)(2,1)S(1)} %collective-permute-done.9.refs_5_), channel_id=1, source_target_pairs={{0,4},{4,0},{1,5},{5,1},{2,6},{6,2},{3,7},{7,3},{8,12},{12,8},{9,1... | collective-permute-start | bytes 1572872 | tf_op jit(solution)/shard_map/ppermute | solution.py:226
  69.5 13.3 %collective-permute-start.14 = (bf16[4,128,512]{2,1,0:T(8,128)(2,1)S(1)}, bf16[4,128,512]{2,1,0:T(8,128)(2,1)S(1)}, u32[]{:S(2)}, u32[]{:S(2)}) collective-permute-start(bf16[4,128,512]{2,1,0:T(8,128)(2,1)S(1)} %collective-permute-done.10.refs_7_), channel_id=1, source_target_pairs={{0,4},{4,0},{1,5},{5,1},{2,6},{6,2},{3,7},{7,3},{8,12},{12,8},{9,1... | collective-permute-start | bytes 1572872 | tf_op jit(solution)/shard_map/ppermute | solution.py:226
  70.0 15.1 %collective-permute-start.3 = (bf16[4,512,128]{2,1,0:T(8,128)(2,1)S(1)}, bf16[4,512,128]{2,1,0:T(8,128)(2,1)S(1)}, u32[]{:S(2)}, u32[]{:S(2)}) collective-permute-start(bf16[4,512,128]{2,1,0:T(8,128)(2,1)S(1)} %get-tuple-element.60.refs_0_), channel_id=1, source_target_pairs={{0,1},{1,2},{2,3},{3,0},{4,5},{5,6},{6,7},{7,4},{8,9},{9,10},{10,1... | collective-permute-start | bytes 1572872 | tf_op jit(solution)/shard_map/ppermute | solution.py:259
  73.4 14.4 %collective-permute-start.5 = (bf16[4,512,128]{2,1,0:T(8,128)(2,1)S(1)}, bf16[4,512,128]{2,1,0:T(8,128)(2,1)S(1)}, u32[]{:S(2)}, u32[]{:S(2)}) collective-permute-start(bf16[4,512,128]{2,1,0:T(8,128)(2,1)S(1)} %get-tuple-element.60.refs_0_), channel_id=1, source_target_pairs={{0,3},{1,0},{2,1},{3,2},{4,7},{5,4},{6,5},{7,6},{8,11},{9,8},{10,9... | collective-permute-start | bytes 1572872 | tf_op jit(solution)/shard_map/ppermute | solution.py:259
  82.9 27.1 %collective-permute-start.15 = (bf16[4,128,512]{2,1,0:T(8,128)(2,1)}, bf16[4,128,512]{2,1,0:T(8,128)(2,1)}, u32[]{:S(2)}, u32[]{:S(2)}) collective-permute-start(bf16[4,128,512]{2,1,0:T(8,128)(2,1)} %get-tuple-element.42.refs_4_), channel_id=1, source_target_pairs={{0,32},{32,64},{64,96},{96,0},{1,33},{33,65},{65,97},{97,1},{2,34}... | collective-permute-start | bytes 1572872 | tf_op jit(solution)/shard_map/ppermute | solution.py:269
  83.0 27.0 %collective-permute-start.16 = (bf16[4,128,512]{2,1,0:T(8,128)(2,1)}, bf16[4,128,512]{2,1,0:T(8,128)(2,1)}, u32[]{:S(2)}, u32[]{:S(2)}) collective-permute-start(bf16[4,128,512]{2,1,0:T(8,128)(2,1)} %get-tuple-element.42.refs_4_), channel_id=1, source_target_pairs={{0,64},{32,96},{64,0},{96,32},{1,65},{33,97},{65,1},{97,33},{2,66}... | collective-permute-start | bytes 1572872 | tf_op jit(solution)/shard_map/ppermute | solution.py:270
  85.1 25.5 %collective-permute-start.17 = (bf16[4,128,512]{2,1,0:T(8,128)(2,1)}, bf16[4,128,512]{2,1,0:T(8,128)(2,1)}, u32[]{:S(2)}, u32[]{:S(2)}) collective-permute-start(bf16[4,128,512]{2,1,0:T(8,128)(2,1)} %get-tuple-element.42.refs_4_), channel_id=1, source_target_pairs={{0,96},{32,0},{64,32},{96,64},{1,97},{33,1},{65,33},{97,65},{2,98}... | collective-permute-start | bytes 1572872 | tf_op jit(solution)/shard_map/ppermute | solution.py:269
  87.8 23.4 %collective-permute-start.23 = (bf16[4,512,128]{2,1,0:T(8,128)(2,1)}, bf16[4,512,128]{2,1,0:T(8,128)(2,1)}, u32[]{:S(2)}, u32[]{:S(2)}) collective-permute-start(bf16[4,512,128]{2,1,0:T(8,128)(2,1)} %get-tuple-element.48.refs_0_), channel_id=1, source_target_pairs={{0,1},{1,2},{2,3},{3,0},{4,5},{5,6},{6,7},{7,4},{8,9},{9,10},{10,1... | collective-permute-start | bytes 1572872 | tf_op jit(solution)/shard_map/ppermute | solution.py:268
  90.8 20.9 %collective-permute-start.24 = (bf16[4,512,128]{2,1,0:T(8,128)(2,1)}, bf16[4,512,128]{2,1,0:T(8,128)(2,1)}, u32[]{:S(2)}, u32[]{:S(2)}) collective-permute-start(bf16[4,512,128]{2,1,0:T(8,128)(2,1)} %get-tuple-element.48.refs_0_), channel_id=1, source_target_pairs={{0,3},{1,0},{2,1},{3,2},{4,7},{5,4},{6,5},{7,6},{8,11},{9,8},{10,9... | collective-permute-start | bytes 1572872 | tf_op jit(solution)/shard_map/ppermute | solution.py:268
  111.7 21.9 %collective-permute-start.30 = (bf16[2,256,512]{2,1,0:T(8,128)(2,1)}, bf16[2,256,512]{2,1,0:T(8,128)(2,1)}, u32[]{:S(2)}, u32[]{:S(2)}) collective-permute-start(bf16[2,256,512]{2,1,0:T(8,128)(2,1)} %get-tuple-element.41), channel_id=1, source_target_pairs={{0,16},{16,8},{8,24},{24,0},{1,17},{17,9},{9,25},{25,1},{2,18},{18... | collective-permute-start | bytes 1572872 | tf_op jit(solution)/shard_map/ppermute | solution.py:218
  113.6 19.9 %collective-permute-start.25 = (bf16[4,512,128]{2,1,0:T(8,128)(2,1)}, bf16[4,512,128]{2,1,0:T(8,128)(2,1)}, u32[]{:S(2)}, u32[]{:S(2)}) collective-permute-start(bf16[4,512,128]{2,1,0:T(8,128)(2,1)} %get-tuple-element.48.refs_0_), channel_id=1, source_target_pairs={{0,2},{1,3},{2,0},{3,1},{4,6},{5,7},{6,4},{7,5},{8,10},{9,11},{10,... | collective-permute-start | bytes 1572872 | tf_op jit(solution)/shard_map/ppermute | solution.py:273
  117.1 16.5 %collective-permute-start.31 = (bf16[2,256,512]{2,1,0:T(8,128)(2,1)}, bf16[2,256,512]{2,1,0:T(8,128)(2,1)}, u32[]{:S(2)}, u32[]{:S(2)}) collective-permute-start(bf16[2,256,512]{2,1,0:T(8,128)(2,1)} %get-tuple-element.54), channel_id=1, source_target_pairs={{0,24},{16,0},{8,16},{24,8},{1,25},{17,1},{9,17},{25,9},{2,26},{18... | collective-permute-start | bytes 1572872 | tf_op jit(solution)/shard_map/ppermute | solution.py:218
  130.3 16.3 %collective-permute-start.26 = (bf16[2,256,512]{2,1,0:T(8,128)(2,1)}, bf16[2,256,512]{2,1,0:T(8,128)(2,1)S(1)}, u32[]{:S(2)}, u32[]{:S(2)}) collective-permute-start(bf16[2,256,512]{2,1,0:T(8,128)(2,1)} %get-tuple-element.49), channel_id=1, source_target_pairs={{0,16},{16,8},{8,24},{24,0},{1,17},{17,9},{9,25},{25,1},{2,18},{18... | collective-permute-start | bytes 1572872 | tf_op jit(solution)/shard_map/ppermute | solution.py:218
  130.3 16.2 %collective-permute-start.27 = (bf16[2,256,512]{2,1,0:T(8,128)(2,1)}, bf16[2,256,512]{2,1,0:T(8,128)(2,1)}, u32[]{:S(2)}, u32[]{:S(2)}) collective-permute-start(bf16[2,256,512]{2,1,0:T(8,128)(2,1)} %get-tuple-element.50), channel_id=1, source_target_pairs={{0,24},{16,0},{8,16},{24,8},{1,25},{17,1},{9,17},{25,9},{2,26},{18... | collective-permute-start | bytes 1572872 | tf_op jit(solution)/shard_map/ppermute | solution.py:218
  143.0 27.9 %collective-permute-start.32 = (bf16[2,256,1024]{2,1,0:T(8,128)(2,1)}, bf16[2,256,1024]{2,1,0:T(8,128)(2,1)}, u32[]{:S(2)}, u32[]{:S(2)}) collective-permute-start(bf16[2,256,1024]{2,1,0:T(8,128)(2,1)} %get-tuple-element.55), channel_id=1, source_target_pairs={{0,16},{16,8},{8,24},{24,0},{1,17},{17,9},{9,25},{25,1},{2,18},{18... | collective-permute-start | bytes 3145736 | tf_op jit(solution)/shard_map/ppermute | solution.py:218
  143.3 27.6 %collective-permute-start.33 = (bf16[2,256,1024]{2,1,0:T(8,128)(2,1)}, bf16[2,256,1024]{2,1,0:T(8,128)(2,1)}, u32[]{:S(2)}, u32[]{:S(2)}) collective-permute-start(bf16[2,256,1024]{2,1,0:T(8,128)(2,1)} %get-tuple-element.56), channel_id=1, source_target_pairs={{0,24},{16,0},{8,16},{24,8},{1,25},{17,1},{9,17},{25,9},{2,26},{18... | collective-permute-start | bytes 3145736 | tf_op jit(solution)/shard_map/ppermute | solution.py:218
  156.8 34.6 %collective-permute-start.28 = (bf16[2,256,1024]{2,1,0:T(8,128)(2,1)}, bf16[2,256,1024]{2,1,0:T(8,128)(2,1)}, u32[]{:S(2)}, u32[]{:S(2)}) collective-permute-start(bf16[2,256,1024]{2,1,0:T(8,128)(2,1)} %get-tuple-element.51), channel_id=1, source_target_pairs={{0,16},{16,8},{8,24},{24,0},{1,17},{17,9},{9,25},{25,1},{2,18},{18... | collective-permute-start | bytes 3145736 | tf_op jit(solution)/shard_map/ppermute | solution.py:218
  156.8 34.5 %collective-permute-start.29 = (bf16[2,256,1024]{2,1,0:T(8,128)(2,1)}, bf16[2,256,1024]{2,1,0:T(8,128)(2,1)}, u32[]{:S(2)}, u32[]{:S(2)}) collective-permute-start(bf16[2,256,1024]{2,1,0:T(8,128)(2,1)} %get-tuple-element.52), channel_id=1, source_target_pairs={{0,24},{16,0},{8,16},{24,8},{1,25},{17,1},{9,17},{25,9},{2,26},{18... | collective-permute-start | bytes 3145736 | tf_op jit(solution)/shard_map/ppermute | solution.py:218
  (27 other events, 303.3 us)

commit v4 on v3

--- a/solution.py
+++ b/solution.py
@@ -25,7 +25,7 @@
     return first.astype(jnp.bfloat16), np.stack(second).astype(jnp.bfloat16)
 
 def density_kernel(pos, place, val, con, first, second, scale, *rest):
-    outs, (xs, yr, yi, zt, held) = rest[:8], rest[8:]
+    outs, (xs, yr, yi, zt, held, turned, row_sem, col_sem) = rest[:8], rest[8:]
     v = pl.program_id(0)
     vr = val[v, 0].astype(jnp.float32)
     vi = val[v, 1].astype(jnp.float32)
@@ -47,7 +47,7 @@
             ar = yr[pl.ds(pl.multiple_of(r*72, 8), 64), :].astype(jnp.bfloat16)
             ai = yi[pl.ds(pl.multiple_of(r*72, 8), 64), :].astype(jnp.bfloat16)
             return [jnp.concatenate([ar, ai], 1), jnp.concatenate([ai, -ar], 1)]
-        @pl.loop(0, 128, unroll=8)
+        @pl.loop(0, 128, unroll=32)
         def _(q):
             r = q*2
             right = jnp.concatenate(side(r) + side(r+1), 0)
@@ -55,20 +55,36 @@
             zt[pl.ds(pl.multiple_of(r*128, 128), 128), :] = z[:, 0:128]
             zt[pl.ds(pl.multiple_of(r*128+128, 128), 128), :] = z[:, 128:256]
         w = scale[...]
-        @pl.loop(0, 256, unroll=2)
-        def _(q):
-            rows = [zt[pl.ds(pos[q*16+j], 1), :] for j in range(16)]
-            t = jnp.concatenate(rows, 0) * w
-            held[pl.ds(pl.multiple_of(q*16, 16), 16), :] = t.astype(jnp.bfloat16)
+        @pl.loop(0, 16)
+        def _(block):
+            base = (block*2 + place[3])*256
+
+            @pl.loop(0, 16, unroll=4)
+            def _(q):
+                rows = [zt[pl.ds(pos[base + q*16 + j], 1), :] for j in range(16)]
+                t = jnp.concatenate(rows, 0) * w
+                held[pl.ds(pl.multiple_of(block*256 + q*16, 16), 16), :] = t.astype(jnp.bfloat16)
+
+        leaving = []
         for s in range(4):
             a = lax.rem(place[0]+s, 4)*1024
             for q, shift in enumerate((2, 0, 1, 3)):
                 to = lax.rem(place[2]+shift, 4)
                 block = lax.rem(to, 2)*2 + lax.div(to, 2)
-                outs[s][q*256:(q+1)*256, :] = held[pl.ds(pl.multiple_of(a + block*256, 256), 256), :]
+                copy = pltpu.make_async_copy(
+                    held.at[pl.ds(pl.multiple_of(a + block*256, 256), 256), :],
+                    outs[s].at[q*256:(q+1)*256, :], row_sem.at[s, q])
+                copy.start()
+                leaving.append(copy)
+        for s in range(4):
             b = lax.rem(place[1]+s, 4)*1024
             for q in range(4):
-                outs[4+s][:, q*256:(q+1)*256] = held[pl.ds(pl.multiple_of(b + q*256, 256), 256), :].T
+                turned[s, :, q*256:(q+1)*256] = held[pl.ds(pl.multiple_of(b + q*256, 256), 256), :].T
+            copy = pltpu.make_async_copy(turned.at[s], outs[4+s], col_sem.at[s])
+            copy.start()
+            leaving.append(copy)
+        for copy in leaving:
+            copy.wait()
 
 
 def densities(pos, place, val, con, scale):
@@ -79,9 +95,10 @@
         grid_spec=pltpu.PrefetchScalarGridSpec(
             num_scalar_prefetch=2, grid=(8,),
             in_specs=[full((8,2,256,128)), full((8,2,256,128)), full((512,512)), full((8,128,256)), full((1,128))],
-            out_specs=[full((1024,128))]*4 + [full((128,1024))]*4,
+            out_specs=[pl.BlockSpec(memory_space=pl.ANY)]*8,
             scratch_shapes=[pltpu.VMEM((512,256), jnp.bfloat16), pltpu.VMEM((256*72,128), jnp.float32),
-                pltpu.VMEM((256*72,128), jnp.float32), pltpu.VMEM((32768,128), jnp.float32), pltpu.VMEM((4096,128), jnp.bfloat16)],
+                pltpu.VMEM((256*72,128), jnp.float32), pltpu.VMEM((32768,128), jnp.float32), pltpu.VMEM((4096,128), jnp.bfloat16),
+                pltpu.VMEM((4,128,1024), jnp.bfloat16), pltpu.SemaphoreType.DMA((4,4)), pltpu.SemaphoreType.DMA((4,))],
         ),
         out_shape=[jax.ShapeDtypeStruct((1024,128), jnp.bfloat16)]*4 + [jax.ShapeDtypeStruct((128,1024), jnp.bfloat16)]*4,
         compiler_params=pltpu.CompilerParams(vmem_limit_bytes=VMEM),
@@ -132,7 +149,7 @@
             for copy in got_copies:
                 copy.wait()
         h = n % 2
-        side = place[0] + n//2 - 2*place[0]*(n//2)
+        side = place[3] + n//2 - 2*place[3]*(n//2)
         at = pl.multiple_of(side*256, 256)
         for o in range(2):
             one = tile[0:256, o*256:(o+1)*256]
@@ -194,13 +211,13 @@
 
 
 def total(parts, chunk, before):
-    spec = pl.BlockSpec((2, 64, 1024), lambda n: (0, n, 0))
+    spec = pl.BlockSpec((2, 128, 1024), lambda n: (0, n, 0))
     more = [] if before is None else [before]
     return pl.pallas_call(
         total_kernel,
-        grid=(4,),
+        grid=(2,),
         in_specs=[spec]*3 + [pl.BlockSpec(memory_space=pl.ANY)]*len(more),
-        out_specs=pl.BlockSpec((64, 2, 1024), lambda n: (n, 0, chunk)),
+        out_specs=pl.BlockSpec((128, 2, 1024), lambda n: (n, 0, chunk)),
         out_shape=jax.ShapeDtypeStruct((256, 2, 2048), jnp.float32),
         input_output_aliases={3: 0} if more else {},
         compiler_params=pltpu.CompilerParams(vmem_limit_bytes=VMEM),
@@ -240,20 +257,17 @@
         - jnp.where(band == vb + channel//8, valence_energy[None, :], 0.0), axis=1)
     weight = 4.0 * gap / (gap*gap + frequency[0]*frequency[0]) / 4096
     scale = jnp.sqrt(weight / 32768.0)[None, :]
-    point = lax.dynamic_index_in_dim(sphere_map.reshape(16, 2, 256), core, 1, keepdims=False).reshape(4096)
-    ky = (point >> 5) & 31
-    pos = ((ky & 7)*32 + (point >> 10))*128 + (ky >> 3)*32 + (point & 31)
-    place = jnp.stack([x, y, zh*2 + zl]).astype(jnp.int32)
-    where = jnp.stack([core, x]).astype(jnp.int32)
-    parts = densities(pos, place, val, con, scale)
+    ky = (sphere_map >> 5) & 31
+    pos = ((ky & 7)*32 + (sphere_map >> 10))*128 + (ky >> 3)*32 + (sphere_map & 31)
+    where = jnp.stack([x, y, zh*2 + zl, core]).astype(jnp.int32)
+    parts = densities(pos, where, val, con, scale)
     row = [parts[0]] + [None]*3
     col = [parts[4]] + [None]*3
     for s in (2, 1, 3):
         row[s] = lax.ppermute(parts[s], "x", ring(s))
         col[s] = lax.ppermute(parts[4 + s], "y", ring(s))
-    row, col = jnp.stack(row), jnp.stack(col)
-    row_a, col_a = row[:, :512], col[:, :, :512]
-    row_b, col_b = row[:, 512:], col[:, :, 512:]
+    row_a, col_a = jnp.stack([r[:512] for r in row]), jnp.stack([c[:, :512] for c in col])
+    row_b, col_b = jnp.stack([r[512:] for r in row]), jnp.stack([c[:, 512:] for c in col])
     rows_a, own_a = [row_a] + [None]*3, [col_a] + [None]*3
     for s in (1, 3):
         rows_a[s] = lax.ppermute(row_a, "y", ring(s))

time: 196 us -> 191 us (0.974)
  Pallas kernels: 70.7 us -> 66.8 us
  starting transfers between devices: 47 us -> 44.4 us
    ppermute x1, waiting for transfers between devices: 0.01 us -> 9.61 us  [local(): own_b[2] = lax.ppermute(col_b, 'x', ring(2))]
    ppermute x2, waiting for transfers between devices: 10.1 us -> 0.62 us  [local(): own_b[s] = lax.ppermute(col_b, 'x', ring(s))]
    ppermute x3, waiting for transfers between devices: 0.01 us -> 2.38 us  [local(): row[s] = lax.ppermute(parts[s], 'x', ring(s))]
    pallas_call x2, Pallas kernels: 8.41 us -> 6.31 us  [total(): pl.pallas_call(total_kernel, grid=(2,), in_specs=[spec] * 3 + [pl.BlockSp...]
    another operation x0 -> x8, local copies, waits for them, and re-layouts: none -> 2.08 us  [the longest x4 1.04 us: local(): jnp.stack([r[512:] for r in row])]
  transfers between devices with their start and end apart: 34 -> 34, of which waited for: 11 -> 10; matrix products, arithmetic and copies ran while one was open for 2% -> 2% of each run, Pallas kernels for 21% -> 21%
where the time goes in v4:
time: 191 us
  Pallas kernels  66.8 us (35%)
  waiting for transfers between devices  62.4 us (33%)
  starting transfers between devices  44.4 us (23%)
  local copies, waits for them, and re-layouts  12.1 us (6%)
  other arithmetic  3.83 us (2%)
    pallas_call x4, Pallas kernels, product(): pl.pallas_call(product_kernel, grid_spec=pltpu.PrefetchScalarGridSpec(num...  37.2 us
    ppermute x8, waiting for transfers between devices, along_z(): lax.ppermute(block, ('zl', 'zh'), [(place(i), place((i + shift) % 4)) for...  28.2 us
    pallas_call x1, Pallas kernels, densities(): pl.pallas_call(density_kernel, grid_spec=pltpu.PrefetchScalarGridSpec(num...  23.2 us
    ppermute x8, starting transfers between devices, along_z(): lax.ppermute(block, ('zl', 'zh'), [(place(i), place((i + shift) % 4)) for...  15.7 us
    ppermute x2, waiting for transfers between devices, local(): own_a[s] = lax.ppermute(col_a, 'x', ring(s))  11.4 us
    ppermute x1, waiting for transfers between devices, local(): own_b[2] = lax.ppermute(col_b, 'x', ring(2))  9.61 us
    ppermute x1, waiting for transfers between devices, local(): own_a[2] = lax.ppermute(col_a, 'x', ring(2))  6.99 us
    pallas_call x2, Pallas kernels, total(): pl.pallas_call(total_kernel, grid=(2,), in_specs=[spec] * 3 + [pl.BlockSp...  6.31 us
  transfers between devices with their start and end apart: 34, of which 10 were waited for; matrix products, arithmetic and copies ran while one was open for 2% of the time, Pallas kernels for 21%

profile of v4, /device:TPU:8, one launch (start us, length us, event | category | flops | bytes accessed | tf_op | source)
XLA Modules:
  0.0 190.6 jit_solution(8856712167613651967)
XLA Ops:
  0.7 2.0 %constant_dynamic-slice_fusion = bf16[8,2,32768]{2,1,0:T(2,128)(2,1)S(1)} fusion(bf16[64,2,32768]{2,1,0:T(2,128)(2,1)} %param.11, s32[]{:T(128)S(6)} %select_n.50), kind=kLoop, calls=%fused_computation.34 | loop fusion | bytes 2097156 | tf_op jit(solution)/shard_map/dynamic_slice | solution.py:252
  9.7 23.2 %densities.1 = (bf16[1024,128]{1,0:T(8,128)(2,1)}, bf16[1024,128]{1,0:T(8,128)(2,1)}, bf16[1024,128]{1,0:T(8,128)(2,1)}, bf16[1024,128]{1,0:T(8,128)(2,1)}, bf16...) custom-call(s32[8192]{0:T(1024)} %and_add_fusion.pos, ...), custom_call_target="tpu_custom_call" | custom-call | tf_op jit(solution)/shard_map/densities/pallas_call | solution.py:93
  35.4 2.5 %collective-permute-start.8 = (bf16[128,1024]{1,0:T(8,128)(2,1)}, bf16[128,1024]{1,0:T(8,128)(2,1)S(1)}, u32[]{:S(2)}, u32[]{:S(2)}) collective-permute-start(bf16[128,1024]{1,0:T(8,128)(2,1)} %get-tuple-element.38), channel_id=1, source_target_pairs={{0,3},{1,0},{2,1},{3,2},{4,7},{5,4},{6,5},{7,6},{8,11},{9,8},{10,9... | collective-permute-start | bytes 786440 | tf_op jit(solution)/shard_map/ppermute | solution.py:268
  39.4 2.7 %collective-permute-start.1 = (bf16[1024,128]{1,0:T(8,128)(2,1)}, bf16[1024,128]{1,0:T(8,128)(2,1)S(1)}, u32[]{:S(2)}, u32[]{:S(2)}) collective-permute-start(bf16[1024,128]{1,0:T(8,128)(2,1)} %get-tuple-element.33), channel_id=1, source_target_pairs={{0,64},{32,96},{64,0},{96,32},{1,65},{33,97},{65,1},{97,33},{2,66}... | collective-permute-start | bytes 786440 | tf_op jit(solution)/shard_map/ppermute | solution.py:267
  45.7 3.3 %collective-permute-done.8 = bf16[128,1024]{1,0:T(8,128)(2,1)S(1)} collective-permute-done((bf16[128,1024]{1,0:T(8,128)(2,1)}, bf16[128,1024]{1,0:T(8,128)(2,1)S(1)}, u32[]{:S(2)}, u32[]{:S(2)}) %collective-permute-start.8) | collective-permute-done | bytes 262176 | tf_op jit(solution)/shard_map/ppermute | solution.py:268
  49.1 2.8 %collective-permute-start.10 = (bf16[4,128,512]{2,1,0:T(8,128)(2,1)S(1)}, bf16[4,128,512]{2,1,0:T(8,128)(2,1)S(1)}, u32[]{:S(2)}, u32[]{:S(2)}) collective-permute-start(bf16[4,128,512]{2,1,0:T(8,128)(2,1)S(1)} %pad_maximum_fusion.3.refs_4_), channel_id=1, source_target_pairs={{0,96},{32,0},{64,32},{96,64},{1,97},{33,1},{65,33},{97,65},{2,98}... | collective-permute-start | bytes 1572872 | tf_op jit(solution)/shard_map/ppermute | solution.py:274
  54.5 9.4 %collective-permute-done.10.refs_7_ = bf16[4,128,512]{2,1,0:T(8,128)(2,1)S(1)} collective-permute-done((bf16[4,128,512]{2,1,0:T(8,128)(2,1)S(1)}, bf16[4,128,512]{2,1,0:T(8,128)(2,1)S(1)}, u32[]{:S(2)}, u32[]{:S(2)}) %collective-permute-start.10) | collective-permute-done | bytes 524320 | tf_op jit(solution)/shard_map/ppermute | solution.py:274
  64.0 1.9 %collective-permute-done.9.refs_5_ = bf16[4,128,512]{2,1,0:T(8,128)(2,1)S(1)} collective-permute-done((bf16[4,128,512]{2,1,0:T(8,128)(2,1)S(1)}, bf16[4,128,512]{2,1,0:T(8,128)(2,1)S(1)}, u32[]{:S(2)}, u32[]{:S(2)}) %collective-permute-start.9) | collective-permute-done | bytes 524320 | tf_op jit(solution)/shard_map/ppermute | solution.py:274
  72.3 7.0 %collective-permute-done.11.refs_6_ = bf16[4,128,512]{2,1,0:T(8,128)(2,1)S(1)} collective-permute-done((bf16[4,128,512]{2,1,0:T(8,128)(2,1)S(1)}, bf16[4,128,512]{2,1,0:T(8,128)(2,1)S(1)}, u32[]{:S(2)}, u32[]{:S(2)}) %collective-permute-start.11) | collective-permute-done | bytes 524320 | tf_op jit(solution)/shard_map/ppermute | solution.py:277
  79.4 2.4 %collective-permute-start.15 = (bf16[4,128,512]{2,1,0:T(8,128)(2,1)}, bf16[4,128,512]{2,1,0:T(8,128)(2,1)}, u32[]{:S(2)}, u32[]{:S(2)}) collective-permute-start(bf16[4,128,512]{2,1,0:T(8,128)(2,1)} %pad_maximum_fusion.2.refs_4_), channel_id=1, source_target_pairs={{0,32},{32,64},{64,96},{96,0},{1,33},{33,65},{65,97},{97,1},{2,34}... | collective-permute-start | bytes 1572872 | tf_op jit(solution)/shard_map/ppermute | solution.py:283
  87.7 9.2 %product.4 = (bf16[2,256,512]{2,1,0:T(8,128)(2,1)}, bf16[2,256,512]{2,1,0:T(8,128)(2,1)}, bf16[2,256,1024]{2,1,0:T(8,128)(2,1)}) custom-call(s32[4]{0:T(128)} %pad_add_fusion.place, bf16[4,512,128]{2,1,0:T(8,128)(2,1)} %copy-done, bf16[4,512,128]{2,1,0:T(8,128)(2,1)} %copy-done.3, bf16[4,512,128]{2,1,0:T(8,128)(2,1)} %copy-done.2, ...), custom_call_target="tpu_custom_call" | custom-call | flops 1024 | bytes 1024 | tf_op jit(solution)/shard_map/product/pallas_call | solution.py:180
  96.9 9.6 %collective-permute-done.16.refs_6_ = bf16[4,128,512]{2,1,0:T(8,128)(2,1)} collective-permute-done((bf16[4,128,512]{2,1,0:T(8,128)(2,1)}, bf16[4,128,512]{2,1,0:T(8,128)(2,1)}, u32[]{:S(2)}, u32[]{:S(2)}) %collective-permute-start.16) | collective-permute-done | bytes 524320 | tf_op jit(solution)/shard_map/ppermute | solution.py:284
  110.1 3.3 %collective-permute-start.25 = (bf16[4,512,128]{2,1,0:T(8,128)(2,1)}, bf16[4,512,128]{2,1,0:T(8,128)(2,1)}, u32[]{:S(2)}, u32[]{:S(2)}) collective-permute-start(bf16[4,512,128]{2,1,0:T(8,128)(2,1)} %pad_maximum_fusion.1.refs_0_), channel_id=1, source_target_pairs={{0,2},{1,3},{2,0},{3,1},{4,6},{5,7},{6,4},{7,5},{8,10},{9,11},{10,... | collective-permute-start | bytes 1572872 | tf_op jit(solution)/shard_map/ppermute | solution.py:287
  113.4 3.9 %collective-permute-start.31 = (bf16[2,256,512]{2,1,0:T(8,128)(2,1)}, bf16[2,256,512]{2,1,0:T(8,128)(2,1)}, u32[]{:S(2)}, u32[]{:S(2)}) collective-permute-start(bf16[2,256,512]{2,1,0:T(8,128)(2,1)} %get-tuple-element.54), channel_id=1, source_target_pairs={{0,24},{16,0},{8,16},{24,8},{1,25},{17,1},{9,17},{25,9},{2,26},{18... | collective-permute-start | bytes 1572872 | tf_op jit(solution)/shard_map/ppermute | solution.py:235
  117.4 9.2 %product.5 = (bf16[2,256,512]{2,1,0:T(8,128)(2,1)}, bf16[2,256,512]{2,1,0:T(8,128)(2,1)}, bf16[2,256,1024]{2,1,0:T(8,128)(2,1)}) custom-call(s32[4]{0:T(128)} %pad_add_fusion.place, bf16[4,512,128]{2,1,0:T(8,128)(2,1)} %copy-done, bf16[4,512,128]{2,1,0:T(8,128)(2,1)} %copy-done.3, bf16[4,512,128]{2,1,0:T(8,128)(2,1)} %copy-done.2, ...), custom_call_target="tpu_custom_call" | custom-call | flops 1024 | bytes 1024 | tf_op jit(solution)/shard_map/product/pallas_call | solution.py:180
  126.7 3.2 %collective-permute-start.27 = (bf16[2,256,512]{2,1,0:T(8,128)(2,1)}, bf16[2,256,512]{2,1,0:T(8,128)(2,1)}, u32[]{:S(2)}, u32[]{:S(2)}) collective-permute-start(bf16[2,256,512]{2,1,0:T(8,128)(2,1)} %get-tuple-element.50), channel_id=1, source_target_pairs={{0,24},{16,0},{8,16},{24,8},{1,25},{17,1},{9,17},{25,9},{2,26},{18... | collective-permute-start | bytes 1572872 | tf_op jit(solution)/shard_map/ppermute | solution.py:235
  129.9 9.4 %product.7 = (bf16[2,256,1024]{2,1,0:T(8,128)(2,1)}, bf16[2,256,1024]{2,1,0:T(8,128)(2,1)}) custom-call(s32[4]{0:T(128)} %pad_add_fusion.place, bf16[4,512,128]{2,1,0:T(8,128)(2,1)} %pad_maximum_fusion.1.refs_0_, bf16[4,512,128]{2,1,0:T(8,128)(2,1)} %collective-permute-done.23.refs_1_, bf16[4,512,128]{2,1,0:T(8,128)(2,1)} %collective-permute-done.25.refs_2_, ...), custom_call_target="tpu_custom_call" | custom-call | flops 1024 | bytes 1024 | tf_op jit(solution)/shard_map/product/pallas_call | solution.py:180
  139.4 3.2 %collective-permute-start.33 = (bf16[2,256,1024]{2,1,0:T(8,128)(2,1)}, bf16[2,256,1024]{2,1,0:T(8,128)(2,1)}, u32[]{:S(2)}, u32[]{:S(2)}) collective-permute-start(bf16[2,256,1024]{2,1,0:T(8,128)(2,1)} %get-tuple-element.56), channel_id=1, source_target_pairs={{0,24},{16,0},{8,16},{24,8},{1,25},{17,1},{9,17},{25,9},{2,26},{18... | collective-permute-start | bytes 3145736 | tf_op jit(solution)/shard_map/ppermute | solution.py:235
  143.4 9.4 %product.6 = (bf16[2,256,1024]{2,1,0:T(8,128)(2,1)}, bf16[2,256,1024]{2,1,0:T(8,128)(2,1)}) custom-call(s32[4]{0:T(128)} %pad_add_fusion.place, bf16[4,512,128]{2,1,0:T(8,128)(2,1)} %pad_maximum_fusion.1.refs_0_, bf16[4,512,128]{2,1,0:T(8,128)(2,1)} %collective-permute-done.23.refs_1_, bf16[4,512,128]{2,1,0:T(8,128)(2,1)} %collective-permute-done.25.refs_2_, ...), custom_call_target="tpu_custom_call" | custom-call | flops 1024 | bytes 1024 | tf_op jit(solution)/shard_map/product/pallas_call | solution.py:180
  152.9 3.2 %collective-permute-start.29 = (bf16[2,256,1024]{2,1,0:T(8,128)(2,1)}, bf16[2,256,1024]{2,1,0:T(8,128)(2,1)}, u32[]{:S(2)}, u32[]{:S(2)}) collective-permute-start(bf16[2,256,1024]{2,1,0:T(8,128)(2,1)} %get-tuple-element.52), channel_id=1, source_target_pairs={{0,24},{16,0},{8,16},{24,8},{1,25},{17,1},{9,17},{25,9},{2,26},{18... | collective-permute-start | bytes 3145736 | tf_op jit(solution)/shard_map/ppermute | solution.py:235
  156.1 10.9 %collective-permute-done.32.b = bf16[2,256,1024]{2,1,0:T(8,128)(2,1)} collective-permute-done((bf16[2,256,1024]{2,1,0:T(8,128)(2,1)}, bf16[2,256,1024]{2,1,0:T(8,128)(2,1)}, u32[]{:S(2)}, u32[]{:S(2)}) %collective-permute-start.32) | collective-permute-done | bytes 1048608 | tf_op jit(solution)/shard_map/ppermute | solution.py:235
  167.0 3.2 %total.2.rest_0_ = f32[256,2,2048]{2,1,0:T(2,128)} custom-call(bf16[2,256,1024]{2,1,0:T(8,128)(2,1)} %get-tuple-element.53.a, bf16[2,256,1024]{2,1,0:T(8,128)(2,1)} %collective-permute-done.32.b, bf16[2,256,1024]{2,1,0:T(8,128)(2,1)} %collective-permute-done.33.c), custom_call_target="tpu_custom_call" | custom-call | flops 1024 | bytes 1024 | tf_op jit(solution)/shard_map/total/pallas_call | solution.py:216
  170.2 17.3 %collective-permute-done.28.b = bf16[2,256,1024]{2,1,0:T(8,128)(2,1)} collective-permute-done((bf16[2,256,1024]{2,1,0:T(8,128)(2,1)}, bf16[2,256,1024]{2,1,0:T(8,128)(2,1)}, u32[]{:S(2)}, u32[]{:S(2)}) %collective-permute-start.28) | collective-permute-done | bytes 1048608 | tf_op jit(solution)/shard_map/ppermute | solution.py:235
  187.5 3.2 %total.3 = f32[256,2,2048]{2,1,0:T(2,128)} custom-call(bf16[2,256,1024]{2,1,0:T(8,128)(2,1)} %get-tuple-element.46.a, bf16[2,256,1024]{2,1,0:T(8,128)(2,1)} %collective-permute-done.28.b, bf16[2,256,1024]{2,1,0:T(8,128)(2,1)} %collective-permute-done.29.c, f32[256,2,2048]{2,1,0:T(2,128)} %total.2.rest_0_), custom_call_target="tpu_custom_call", output_to_operand_aliasing={{}: (3, {})} | custom-call | flops 1024 | bytes 1024 | tf_op jit(solution)/shard_map/total/pallas_call | solution.py:216
  (104 shorter events, 34.2 us)
Async XLA Ops:
  35.4 13.5 %collective-permute-start.8 = (bf16[128,1024]{1,0:T(8,128)(2,1)}, bf16[128,1024]{1,0:T(8,128)(2,1)S(1)}, u32[]{:S(2)}, u32[]{:S(2)}) collective-permute-start(bf16[128,1024]{1,0:T(8,128)(2,1)} %get-tuple-element.38), channel_id=1, source_target_pairs={{0,3},{1,0},{2,1},{3,2},{4,7},{5,4},{6,5},{7,6},{8,11},{9,8},{10,9... | collective-permute-start | bytes 786440 | tf_op jit(solution)/shard_map/ppermute | solution.py:268
  37.9 14.0 %collective-permute-start = (bf16[1024,128]{1,0:T(8,128)(2,1)}, bf16[1024,128]{1,0:T(8,128)(2,1)S(1)}, u32[]{:S(2)}, u32[]{:S(2)}) collective-permute-start(bf16[1024,128]{1,0:T(8,128)(2,1)} %get-tuple-element.32), channel_id=1, source_target_pairs={{0,32},{32,64},{64,96},{96,0},{1,33},{33,65},{65,97},{97,1},{2,34}... | collective-permute-start | bytes 786440 | tf_op jit(solution)/shard_map/ppermute | solution.py:267
  39.4 13.7 %collective-permute-start.1 = (bf16[1024,128]{1,0:T(8,128)(2,1)}, bf16[1024,128]{1,0:T(8,128)(2,1)S(1)}, u32[]{:S(2)}, u32[]{:S(2)}) collective-permute-start(bf16[1024,128]{1,0:T(8,128)(2,1)} %get-tuple-element.33), channel_id=1, source_target_pairs={{0,64},{32,96},{64,0},{96,32},{1,65},{33,97},{65,1},{97,33},{2,66}... | collective-permute-start | bytes 786440 | tf_op jit(solution)/shard_map/ppermute | solution.py:267
  49.1 14.9 %collective-permute-start.10 = (bf16[4,128,512]{2,1,0:T(8,128)(2,1)S(1)}, bf16[4,128,512]{2,1,0:T(8,128)(2,1)S(1)}, u32[]{:S(2)}, u32[]{:S(2)}) collective-permute-start(bf16[4,128,512]{2,1,0:T(8,128)(2,1)S(1)} %pad_maximum_fusion.3.refs_4_), channel_id=1, source_target_pairs={{0,96},{32,0},{64,32},{96,64},{1,97},{33,1},{65,33},{97,65},{2,98}... | collective-permute-start | bytes 1572872 | tf_op jit(solution)/shard_map/ppermute | solution.py:274
  51.9 14.0 %collective-permute-start.9 = (bf16[4,128,512]{2,1,0:T(8,128)(2,1)S(1)}, bf16[4,128,512]{2,1,0:T(8,128)(2,1)S(1)}, u32[]{:S(2)}, u32[]{:S(2)}) collective-permute-start(bf16[4,128,512]{2,1,0:T(8,128)(2,1)S(1)} %pad_maximum_fusion.3.refs_4_), channel_id=1, source_target_pairs={{0,32},{32,64},{64,96},{96,0},{1,33},{33,65},{65,97},{97,1},{2,34}... | collective-permute-start | bytes 1572872 | tf_op jit(solution)/shard_map/ppermute | solution.py:274
  51.9 15.7 %collective-permute-start.12 = (bf16[4,128,512]{2,1,0:T(8,128)(2,1)S(1)}, bf16[4,128,512]{2,1,0:T(8,128)(2,1)}, u32[]{:S(2)}, u32[]{:S(2)}) collective-permute-start(bf16[4,128,512]{2,1,0:T(8,128)(2,1)S(1)} %pad_maximum_fusion.3.refs_4_), channel_id=1, source_target_pairs={{0,4},{4,0},{1,5},{5,1},{2,6},{6,2},{3,7},{7,3},{8,12},{12,8},{9,1... | collective-permute-start | bytes 1572872 | tf_op jit(solution)/shard_map/ppermute | solution.py:243
  54.5 14.9 %collective-permute-start.4 = (bf16[4,512,128]{2,1,0:T(8,128)(2,1)S(1)}, bf16[4,512,128]{2,1,0:T(8,128)(2,1)S(1)}, u32[]{:S(2)}, u32[]{:S(2)}) collective-permute-start(bf16[4,512,128]{2,1,0:T(8,128)(2,1)S(1)} %pad_maximum_fusion.refs_0_), channel_id=1, source_target_pairs={{0,2},{1,3},{2,0},{3,1},{4,6},{5,7},{6,4},{7,5},{8,10},{9,11},{10,... | collective-permute-start | bytes 1572872 | tf_op jit(solution)/shard_map/ppermute | solution.py:275
  65.9 13.4 %collective-permute-start.11 = (bf16[4,128,512]{2,1,0:T(8,128)(2,1)S(1)}, bf16[4,128,512]{2,1,0:T(8,128)(2,1)S(1)}, u32[]{:S(2)}, u32[]{:S(2)}) collective-permute-start(bf16[4,128,512]{2,1,0:T(8,128)(2,1)S(1)} %pad_maximum_fusion.3.refs_4_), channel_id=1, source_target_pairs={{0,64},{32,96},{64,0},{96,32},{1,65},{33,97},{65,1},{97,33},{2,66}... | collective-permute-start | bytes 1572872 | tf_op jit(solution)/shard_map/ppermute | solution.py:277
  67.6 15.0 %collective-permute-start.3 = (bf16[4,512,128]{2,1,0:T(8,128)(2,1)S(1)}, bf16[4,512,128]{2,1,0:T(8,128)(2,1)S(1)}, u32[]{:S(2)}, u32[]{:S(2)}) collective-permute-start(bf16[4,512,128]{2,1,0:T(8,128)(2,1)S(1)} %pad_maximum_fusion.refs_0_), channel_id=1, source_target_pairs={{0,1},{1,2},{2,3},{3,0},{4,5},{5,6},{6,7},{7,4},{8,9},{9,10},{10,1... | collective-permute-start | bytes 1572872 | tf_op jit(solution)/shard_map/ppermute | solution.py:273
  70.2 14.4 %collective-permute-start.5 = (bf16[4,512,128]{2,1,0:T(8,128)(2,1)S(1)}, bf16[4,512,128]{2,1,0:T(8,128)(2,1)S(1)}, u32[]{:S(2)}, u32[]{:S(2)}) collective-permute-start(bf16[4,512,128]{2,1,0:T(8,128)(2,1)S(1)} %pad_maximum_fusion.refs_0_), channel_id=1, source_target_pairs={{0,3},{1,0},{2,1},{3,2},{4,7},{5,4},{6,5},{7,6},{8,11},{9,8},{10,9... | collective-permute-start | bytes 1572872 | tf_op jit(solution)/shard_map/ppermute | solution.py:273
  79.4 17.5 %collective-permute-start.15 = (bf16[4,128,512]{2,1,0:T(8,128)(2,1)}, bf16[4,128,512]{2,1,0:T(8,128)(2,1)}, u32[]{:S(2)}, u32[]{:S(2)}) collective-permute-start(bf16[4,128,512]{2,1,0:T(8,128)(2,1)} %pad_maximum_fusion.2.refs_4_), channel_id=1, source_target_pairs={{0,32},{32,64},{64,96},{96,0},{1,33},{33,65},{65,97},{97,1},{2,34}... | collective-permute-start | bytes 1572872 | tf_op jit(solution)/shard_map/ppermute | solution.py:283
  81.8 24.8 %collective-permute-start.16 = (bf16[4,128,512]{2,1,0:T(8,128)(2,1)}, bf16[4,128,512]{2,1,0:T(8,128)(2,1)}, u32[]{:S(2)}, u32[]{:S(2)}) collective-permute-start(bf16[4,128,512]{2,1,0:T(8,128)(2,1)} %pad_maximum_fusion.2.refs_4_), channel_id=1, source_target_pairs={{0,64},{32,96},{64,0},{96,32},{1,65},{33,97},{65,1},{97,33},{2,66}... | collective-permute-start | bytes 1572872 | tf_op jit(solution)/shard_map/ppermute | solution.py:284
  82.7 24.5 %collective-permute-start.17 = (bf16[4,128,512]{2,1,0:T(8,128)(2,1)}, bf16[4,128,512]{2,1,0:T(8,128)(2,1)}, u32[]{:S(2)}, u32[]{:S(2)}) collective-permute-start(bf16[4,128,512]{2,1,0:T(8,128)(2,1)} %pad_maximum_fusion.2.refs_4_), channel_id=1, source_target_pairs={{0,96},{32,0},{64,32},{96,64},{1,97},{33,1},{65,33},{97,65},{2,98}... | collective-permute-start | bytes 1572872 | tf_op jit(solution)/shard_map/ppermute | solution.py:283
  84.5 23.1 %collective-permute-start.23 = (bf16[4,512,128]{2,1,0:T(8,128)(2,1)}, bf16[4,512,128]{2,1,0:T(8,128)(2,1)}, u32[]{:S(2)}, u32[]{:S(2)}) collective-permute-start(bf16[4,512,128]{2,1,0:T(8,128)(2,1)} %pad_maximum_fusion.1.refs_0_), channel_id=1, source_target_pairs={{0,1},{1,2},{2,3},{3,0},{4,5},{5,6},{6,7},{7,4},{8,9},{9,10},{10,1... | collective-permute-start | bytes 1572872 | tf_op jit(solution)/shard_map/ppermute | solution.py:282
  86.2 22.0 %collective-permute-start.24 = (bf16[4,512,128]{2,1,0:T(8,128)(2,1)}, bf16[4,512,128]{2,1,0:T(8,128)(2,1)}, u32[]{:S(2)}, u32[]{:S(2)}) collective-permute-start(bf16[4,512,128]{2,1,0:T(8,128)(2,1)} %pad_maximum_fusion.1.refs_0_), channel_id=1, source_target_pairs={{0,3},{1,0},{2,1},{3,2},{4,7},{5,4},{6,5},{7,6},{8,11},{9,8},{10,9... | collective-permute-start | bytes 1572872 | tf_op jit(solution)/shard_map/ppermute | solution.py:282
  108.2 21.8 %collective-permute-start.30 = (bf16[2,256,512]{2,1,0:T(8,128)(2,1)}, bf16[2,256,512]{2,1,0:T(8,128)(2,1)}, u32[]{:S(2)}, u32[]{:S(2)}) collective-permute-start(bf16[2,256,512]{2,1,0:T(8,128)(2,1)} %get-tuple-element.41), channel_id=1, source_target_pairs={{0,16},{16,8},{8,24},{24,0},{1,17},{17,9},{9,25},{25,1},{2,18},{18... | collective-permute-start | bytes 1572872 | tf_op jit(solution)/shard_map/ppermute | solution.py:235
  110.1 19.8 %collective-permute-start.25 = (bf16[4,512,128]{2,1,0:T(8,128)(2,1)}, bf16[4,512,128]{2,1,0:T(8,128)(2,1)}, u32[]{:S(2)}, u32[]{:S(2)}) collective-permute-start(bf16[4,512,128]{2,1,0:T(8,128)(2,1)} %pad_maximum_fusion.1.refs_0_), channel_id=1, source_target_pairs={{0,2},{1,3},{2,0},{3,1},{4,6},{5,7},{6,4},{7,5},{8,10},{9,11},{10,... | collective-permute-start | bytes 1572872 | tf_op jit(solution)/shard_map/ppermute | solution.py:287
  113.4 16.5 %collective-permute-start.31 = (bf16[2,256,512]{2,1,0:T(8,128)(2,1)}, bf16[2,256,512]{2,1,0:T(8,128)(2,1)}, u32[]{:S(2)}, u32[]{:S(2)}) collective-permute-start(bf16[2,256,512]{2,1,0:T(8,128)(2,1)} %get-tuple-element.54), channel_id=1, source_target_pairs={{0,24},{16,0},{8,16},{24,8},{1,25},{17,1},{9,17},{25,9},{2,26},{18... | collective-permute-start | bytes 1572872 | tf_op jit(solution)/shard_map/ppermute | solution.py:235
  126.6 16.0 %collective-permute-start.26 = (bf16[2,256,512]{2,1,0:T(8,128)(2,1)}, bf16[2,256,512]{2,1,0:T(8,128)(2,1)S(1)}, u32[]{:S(2)}, u32[]{:S(2)}) collective-permute-start(bf16[2,256,512]{2,1,0:T(8,128)(2,1)} %get-tuple-element.49), channel_id=1, source_target_pairs={{0,16},{16,8},{8,24},{24,0},{1,17},{17,9},{9,25},{25,1},{2,18},{18... | collective-permute-start | bytes 1572872 | tf_op jit(solution)/shard_map/ppermute | solution.py:235
  126.7 15.9 %collective-permute-start.27 = (bf16[2,256,512]{2,1,0:T(8,128)(2,1)}, bf16[2,256,512]{2,1,0:T(8,128)(2,1)}, u32[]{:S(2)}, u32[]{:S(2)}) collective-permute-start(bf16[2,256,512]{2,1,0:T(8,128)(2,1)} %get-tuple-element.50), channel_id=1, source_target_pairs={{0,24},{16,0},{8,16},{24,8},{1,25},{17,1},{9,17},{25,9},{2,26},{18... | collective-permute-start | bytes 1572872 | tf_op jit(solution)/shard_map/ppermute | solution.py:235
  139.3 27.7 %collective-permute-start.32 = (bf16[2,256,1024]{2,1,0:T(8,128)(2,1)}, bf16[2,256,1024]{2,1,0:T(8,128)(2,1)}, u32[]{:S(2)}, u32[]{:S(2)}) collective-permute-start(bf16[2,256,1024]{2,1,0:T(8,128)(2,1)} %get-tuple-element.55), channel_id=1, source_target_pairs={{0,16},{16,8},{8,24},{24,0},{1,17},{17,9},{9,25},{25,1},{2,18},{18... | collective-permute-start | bytes 3145736 | tf_op jit(solution)/shard_map/ppermute | solution.py:235
  139.4 27.6 %collective-permute-start.33 = (bf16[2,256,1024]{2,1,0:T(8,128)(2,1)}, bf16[2,256,1024]{2,1,0:T(8,128)(2,1)}, u32[]{:S(2)}, u32[]{:S(2)}) collective-permute-start(bf16[2,256,1024]{2,1,0:T(8,128)(2,1)} %get-tuple-element.56), channel_id=1, source_target_pairs={{0,24},{16,0},{8,16},{24,8},{1,25},{17,1},{9,17},{25,9},{2,26},{18... | collective-permute-start | bytes 3145736 | tf_op jit(solution)/shard_map/ppermute | solution.py:235
  152.8 34.6 %collective-permute-start.28 = (bf16[2,256,1024]{2,1,0:T(8,128)(2,1)}, bf16[2,256,1024]{2,1,0:T(8,128)(2,1)}, u32[]{:S(2)}, u32[]{:S(2)}) collective-permute-start(bf16[2,256,1024]{2,1,0:T(8,128)(2,1)} %get-tuple-element.51), channel_id=1, source_target_pairs={{0,16},{16,8},{8,24},{24,0},{1,17},{17,9},{9,25},{25,1},{2,18},{18... | collective-permute-start | bytes 3145736 | tf_op jit(solution)/shard_map/ppermute | solution.py:235
  152.9 34.5 %collective-permute-start.29 = (bf16[2,256,1024]{2,1,0:T(8,128)(2,1)}, bf16[2,256,1024]{2,1,0:T(8,128)(2,1)}, u32[]{:S(2)}, u32[]{:S(2)}) collective-permute-start(bf16[2,256,1024]{2,1,0:T(8,128)(2,1)} %get-tuple-element.52), channel_id=1, source_target_pairs={{0,24},{16,0},{8,16},{24,8},{1,25},{17,1},{9,17},{25,9},{2,26},{18... | collective-permute-start | bytes 3145736 | tf_op jit(solution)/shard_map/ppermute | solution.py:235
  (26 other events, 253.6 us)

commit v5 on v4

--- a/solution.py
+++ b/solution.py
@@ -26,22 +26,23 @@
 
 def density_kernel(pos, place, val, con, first, second, scale, *rest):
     outs, (xs, yr, yi, zt, held, turned, row_sem, col_sem) = rest[:8], rest[8:]
-    v = pl.program_id(0)
-    vr = val[v, 0].astype(jnp.float32)
-    vi = val[v, 1].astype(jnp.float32)
-    for pair in range(4):
-        for k in range(2):
-            cr = con[2*pair+k, 0].astype(jnp.float32)
-            ci = con[2*pair+k, 1].astype(jnp.float32)
-            xs[0:256, k*128:(k+1)*128] = (vr*cr + vi*ci).astype(jnp.bfloat16)
-            xs[256:512, k*128:(k+1)*128] = (vr*ci - vi*cr).astype(jnp.bfloat16)
-        y = jnp.dot(first[...], xs[...], preferred_element_type=jnp.float32)
-        for k in range(2):
-            p = v*8 + 2*pair + k
-            yr[pl.ds(p, 256, stride=72), :] = y[0:256, k*128:(k+1)*128]
-            yi[pl.ds(p, 256, stride=72), :] = y[256:512, k*128:(k+1)*128]
-
-    @pl.when(v == 7)
+    step = pl.program_id(0)
+    for v in (2*step, 2*step + 1):
+        vr = val[v, 0].astype(jnp.float32)
+        vi = val[v, 1].astype(jnp.float32)
+        for pair in range(4):
+            for k in range(2):
+                cr = con[2*pair+k, 0].astype(jnp.float32)
+                ci = con[2*pair+k, 1].astype(jnp.float32)
+                xs[0:256, k*128:(k+1)*128] = (vr*cr + vi*ci).astype(jnp.bfloat16)
+                xs[256:512, k*128:(k+1)*128] = (vr*ci - vi*cr).astype(jnp.bfloat16)
+            y = jnp.dot(first[...], xs[...], preferred_element_type=jnp.float32)
+            for k in range(2):
+                p = v*8 + 2*pair + k
+                yr[pl.ds(p, 256, stride=72), :] = y[0:256, k*128:(k+1)*128]
+                yi[pl.ds(p, 256, stride=72), :] = y[256:512, k*128:(k+1)*128]
+
+    @pl.when(step == 3)
     def _():
         def side(r):
             ar = yr[pl.ds(pl.multiple_of(r*72, 8), 64), :].astype(jnp.bfloat16)
@@ -93,7 +94,7 @@
     return pl.pallas_call(
         density_kernel,
         grid_spec=pltpu.PrefetchScalarGridSpec(
-            num_scalar_prefetch=2, grid=(8,),
+            num_scalar_prefetch=2, grid=(4,),
             in_specs=[full((8,2,256,128)), full((8,2,256,128)), full((512,512)), full((8,128,256)), full((1,128))],
             out_specs=[pl.BlockSpec(memory_space=pl.ANY)]*8,
             scratch_shapes=[pltpu.VMEM((512,256), jnp.bfloat16), pltpu.VMEM((256*72,128), jnp.float32),
@@ -101,7 +102,7 @@
                 pltpu.VMEM((4,128,1024), jnp.bfloat16), pltpu.SemaphoreType.DMA((4,4)), pltpu.SemaphoreType.DMA((4,))],
         ),
         out_shape=[jax.ShapeDtypeStruct((1024,128), jnp.bfloat16)]*4 + [jax.ShapeDtypeStruct((128,1024), jnp.bfloat16)]*4,
-        compiler_params=pltpu.CompilerParams(vmem_limit_bytes=VMEM),
+        compiler_params=pltpu.CompilerParams(vmem_limit_bytes=50*2**20),
         name="densities",
     )(pos, place, val, con, jnp.asarray(first), jnp.asarray(second), scale)
 

time: 191 us -> 188 us (0.984)
  local copies, waits for them, and re-layouts: 12.1 us -> 9.62 us
  transfers between devices with their start and end apart: 34 -> 34, of which waited for: 10 -> 11; matrix products, arithmetic and copies ran while one was open for 2% -> 1% of each run, Pallas kernels for 21% -> 22%
where the time goes in v5:
time: 188 us
  Pallas kernels  66.1 us (35%)
  waiting for transfers between devices  63.4 us (34%)
  starting transfers between devices  45.7 us (24%)
  local copies, waits for them, and re-layouts  9.62 us (5%)
  other arithmetic  2.21 us (1%)
    pallas_call x4, Pallas kernels, product(): pl.pallas_call(product_kernel, grid_spec=pltpu.PrefetchScalarGridSpec(num...  37.3 us
    ppermute x8, waiting for transfers between devices, along_z(): lax.ppermute(block, ('zl', 'zh'), [(place(i), place((i + shift) % 4)) for...  28.1 us
    pallas_call x1, Pallas kernels, densities(): pl.pallas_call(density_kernel, grid_spec=pltpu.PrefetchScalarGridSpec(num...  22.5 us
    ppermute x8, starting transfers between devices, along_z(): lax.ppermute(block, ('zl', 'zh'), [(place(i), place((i + shift) % 4)) for...  15.7 us
    ppermute x2, waiting for transfers between devices, local(): own_a[s] = lax.ppermute(col_a, 'x', ring(s))  11.3 us
    ppermute x1, waiting for transfers between devices, local(): own_b[2] = lax.ppermute(col_b, 'x', ring(2))  9.44 us
    ppermute x1, waiting for transfers between devices, local(): own_a[2] = lax.ppermute(col_a, 'x', ring(2))  7.8 us
    ppermute x3, starting transfers between devices, local(): row[s] = lax.ppermute(parts[s], 'x', ring(s))  6.97 us
  transfers between devices with their start and end apart: 34, of which 11 were waited for; matrix products, arithmetic and copies ran while one was open for 1% of the time, Pallas kernels for 22%

profile of v5, /device:TPU:8, one launch (start us, length us, event | category | flops | bytes accessed | tf_op | source)
XLA Modules:
  0.0 188.1 jit_solution(8501393610277683238)
XLA Ops:
  0.8 2.0 %constant_dynamic-slice_fusion = bf16[8,2,32768]{2,1,0:T(2,128)(2,1)S(1)} fusion(bf16[64,2,32768]{2,1,0:T(2,128)(2,1)} %param.11, s32[]{:T(128)S(6)} %select_n.50), kind=kLoop, calls=%fused_computation.34 | loop fusion | bytes 2097156 | tf_op jit(solution)/shard_map/dynamic_slice | solution.py:253
  8.2 22.5 %densities.1 = (bf16[1024,128]{1,0:T(8,128)(2,1)S(1)}, bf16[1024,128]{1,0:T(8,128)(2,1)S(1)}, bf16[1024,128]{1,0:T(8,128)(2,1)S(1)}, bf16[1024,128]{1,0:T(8,128)...) custom-call(s32[8192]{0:T(1024)S(1)} %and_add_fusion.pos, ...), custom_call_target="tpu_custom_call" | custom-call | tf_op jit(solution)/shard_map/densities/pallas_call | solution.py:94
  33.1 2.5 %collective-permute-start.8 = (bf16[128,1024]{1,0:T(8,128)(2,1)S(1)}, bf16[128,1024]{1,0:T(8,128)(2,1)S(1)}, u32[]{:S(2)}, u32[]{:S(2)}) collective-permute-start(bf16[128,1024]{1,0:T(8,128)(2,1)S(1)} %get-tuple-element.38), channel_id=1, source_target_pairs={{0,3},{1,0},{2,1},{3,2},{4,7},{5,4},{6,5},{7,6},{8,11},{9,8},{10,9... | collective-permute-start | bytes 786440 | tf_op jit(solution)/shard_map/ppermute | solution.py:269
  37.1 2.7 %collective-permute-start.1 = (bf16[1024,128]{1,0:T(8,128)(2,1)S(1)}, bf16[1024,128]{1,0:T(8,128)(2,1)S(1)}, u32[]{:S(2)}, u32[]{:S(2)}) collective-permute-start(bf16[1024,128]{1,0:T(8,128)(2,1)S(1)} %get-tuple-element.33), channel_id=1, source_target_pairs={{0,64},{32,96},{64,0},{96,32},{1,65},{33,97},{65,1},{97,33},{2,66}... | collective-permute-start | bytes 786440 | tf_op jit(solution)/shard_map/ppermute | solution.py:268
  39.9 2.7 %collective-permute-start.2 = (bf16[1024,128]{1,0:T(8,128)(2,1)S(1)}, bf16[1024,128]{1,0:T(8,128)(2,1)S(1)}, u32[]{:S(2)}, u32[]{:S(2)}) collective-permute-start(bf16[1024,128]{1,0:T(8,128)(2,1)S(1)} %get-tuple-element.34), channel_id=1, source_target_pairs={{0,96},{32,0},{64,32},{96,64},{1,97},{33,1},{65,33},{97,65},{2,98}... | collective-permute-start | bytes 786440 | tf_op jit(solution)/shard_map/ppermute | solution.py:268
  43.1 3.4 %collective-permute-done.8 = bf16[128,1024]{1,0:T(8,128)(2,1)S(1)} collective-permute-done((bf16[128,1024]{1,0:T(8,128)(2,1)S(1)}, bf16[128,1024]{1,0:T(8,128)(2,1)S(1)}, u32[]{:S(2)}, u32[]{:S(2)}) %collective-permute-start.8) | collective-permute-done | bytes 262176 | tf_op jit(solution)/shard_map/ppermute | solution.py:269
  46.6 2.8 %collective-permute-start.10 = (bf16[4,128,512]{2,1,0:T(8,128)(2,1)S(1)}, bf16[4,128,512]{2,1,0:T(8,128)(2,1)S(1)}, u32[]{:S(2)}, u32[]{:S(2)}) collective-permute-start(bf16[4,128,512]{2,1,0:T(8,128)(2,1)S(1)} %pad_maximum_fusion.3.refs_4_), channel_id=1, source_target_pairs={{0,96},{32,0},{64,32},{96,64},{1,97},{33,1},{65,33},{97,65},{2,98}... | collective-permute-start | bytes 1572872 | tf_op jit(solution)/shard_map/ppermute | solution.py:275
  52.1 9.4 %collective-permute-done.10.refs_7_ = bf16[4,128,512]{2,1,0:T(8,128)(2,1)S(1)} collective-permute-done((bf16[4,128,512]{2,1,0:T(8,128)(2,1)S(1)}, bf16[4,128,512]{2,1,0:T(8,128)(2,1)S(1)}, u32[]{:S(2)}, u32[]{:S(2)}) %collective-permute-start.10) | collective-permute-done | bytes 524320 | tf_op jit(solution)/shard_map/ppermute | solution.py:275
  69.0 7.8 %collective-permute-done.11.refs_6_ = bf16[4,128,512]{2,1,0:T(8,128)(2,1)S(1)} collective-permute-done((bf16[4,128,512]{2,1,0:T(8,128)(2,1)S(1)}, bf16[4,128,512]{2,1,0:T(8,128)(2,1)S(1)}, u32[]{:S(2)}, u32[]{:S(2)}) %collective-permute-start.11) | collective-permute-done | bytes 524320 | tf_op jit(solution)/shard_map/ppermute | solution.py:278
  77.0 2.7 %collective-permute-start.15 = (bf16[4,128,512]{2,1,0:T(8,128)(2,1)}, bf16[4,128,512]{2,1,0:T(8,128)(2,1)}, u32[]{:S(2)}, u32[]{:S(2)}) collective-permute-start(bf16[4,128,512]{2,1,0:T(8,128)(2,1)} %pad_maximum_fusion.2.refs_4_), channel_id=1, source_target_pairs={{0,32},{32,64},{64,96},{96,0},{1,33},{33,65},{65,97},{97,1},{2,34}... | collective-permute-start | bytes 1572872 | tf_op jit(solution)/shard_map/ppermute | solution.py:284
  85.5 9.2 %product.4 = (bf16[2,256,512]{2,1,0:T(8,128)(2,1)}, bf16[2,256,512]{2,1,0:T(8,128)(2,1)}, bf16[2,256,1024]{2,1,0:T(8,128)(2,1)}) custom-call(s32[4]{0:T(128)} %copy-done.2, bf16[4,512,128]{2,1,0:T(8,128)(2,1)} %copy-done.3, bf16[4,512,128]{2,1,0:T(8,128)(2,1)} %copy-done.6, bf16[4,512,128]{2,1,0:T(8,128)(2,1)} %copy-done.5, bf16[4,512,128]{2,1,0:T(8,128)(2,1)} %copy-done.7, ...), custom_call_target="tpu_custom_call" | custom-call | flops 1024 | bytes 1024 | tf_op jit(solution)/shard_map/product/pallas_call | solution.py:181
  94.8 9.4 %collective-permute-done.16.refs_6_ = bf16[4,128,512]{2,1,0:T(8,128)(2,1)} collective-permute-done((bf16[4,128,512]{2,1,0:T(8,128)(2,1)}, bf16[4,128,512]{2,1,0:T(8,128)(2,1)}, u32[]{:S(2)}, u32[]{:S(2)}) %collective-permute-start.16) | collective-permute-done | bytes 524320 | tf_op jit(solution)/shard_map/ppermute | solution.py:285
  107.6 3.3 %collective-permute-start.25 = (bf16[4,512,128]{2,1,0:T(8,128)(2,1)}, bf16[4,512,128]{2,1,0:T(8,128)(2,1)}, u32[]{:S(2)}, u32[]{:S(2)}) collective-permute-start(bf16[4,512,128]{2,1,0:T(8,128)(2,1)} %pad_maximum_fusion.1.refs_0_), channel_id=1, source_target_pairs={{0,2},{1,3},{2,0},{3,1},{4,6},{5,7},{6,4},{7,5},{8,10},{9,11},{10,... | collective-permute-start | bytes 1572872 | tf_op jit(solution)/shard_map/ppermute | solution.py:288
  111.0 3.9 %collective-permute-start.31 = (bf16[2,256,512]{2,1,0:T(8,128)(2,1)}, bf16[2,256,512]{2,1,0:T(8,128)(2,1)}, u32[]{:S(2)}, u32[]{:S(2)}) collective-permute-start(bf16[2,256,512]{2,1,0:T(8,128)(2,1)} %get-tuple-element.54), channel_id=1, source_target_pairs={{0,24},{16,0},{8,16},{24,8},{1,25},{17,1},{9,17},{25,9},{2,26},{18... | collective-permute-start | bytes 1572872 | tf_op jit(solution)/shard_map/ppermute | solution.py:236
  114.9 9.3 %product.5 = (bf16[2,256,512]{2,1,0:T(8,128)(2,1)}, bf16[2,256,512]{2,1,0:T(8,128)(2,1)}, bf16[2,256,1024]{2,1,0:T(8,128)(2,1)}) custom-call(s32[4]{0:T(128)} %copy-done.2, bf16[4,512,128]{2,1,0:T(8,128)(2,1)} %copy-done.3, bf16[4,512,128]{2,1,0:T(8,128)(2,1)} %copy-done.6, bf16[4,512,128]{2,1,0:T(8,128)(2,1)} %copy-done.5, bf16[4,512,128]{2,1,0:T(8,128)(2,1)} %copy-done.7, ...), custom_call_target="tpu_custom_call" | custom-call | flops 1024 | bytes 1024 | tf_op jit(solution)/shard_map/product/pallas_call | solution.py:181
  124.3 3.2 %collective-permute-start.27 = (bf16[2,256,512]{2,1,0:T(8,128)(2,1)}, bf16[2,256,512]{2,1,0:T(8,128)(2,1)}, u32[]{:S(2)}, u32[]{:S(2)}) collective-permute-start(bf16[2,256,512]{2,1,0:T(8,128)(2,1)} %get-tuple-element.50), channel_id=1, source_target_pairs={{0,24},{16,0},{8,16},{24,8},{1,25},{17,1},{9,17},{25,9},{2,26},{18... | collective-permute-start | bytes 1572872 | tf_op jit(solution)/shard_map/ppermute | solution.py:236
  127.5 9.4 %product.7 = (bf16[2,256,1024]{2,1,0:T(8,128)(2,1)}, bf16[2,256,1024]{2,1,0:T(8,128)(2,1)}) custom-call(s32[4]{0:T(128)} %copy-done.2, bf16[4,512,128]{2,1,0:T(8,128)(2,1)} %pad_maximum_fusion.1.refs_0_, bf16[4,512,128]{2,1,0:T(8,128)(2,1)} %collective-permute-done.23.refs_1_, bf16[4,512,128]{2,1,0:T(8,128)(2,1)} %collective-permute-done.25.refs_2_, ...), custom_call_target="tpu_custom_call" | custom-call | flops 1024 | bytes 1024 | tf_op jit(solution)/shard_map/product/pallas_call | solution.py:181
  137.0 3.2 %collective-permute-start.33 = (bf16[2,256,1024]{2,1,0:T(8,128)(2,1)}, bf16[2,256,1024]{2,1,0:T(8,128)(2,1)}, u32[]{:S(2)}, u32[]{:S(2)}) collective-permute-start(bf16[2,256,1024]{2,1,0:T(8,128)(2,1)} %get-tuple-element.56), channel_id=1, source_target_pairs={{0,24},{16,0},{8,16},{24,8},{1,25},{17,1},{9,17},{25,9},{2,26},{18... | collective-permute-start | bytes 3145736 | tf_op jit(solution)/shard_map/ppermute | solution.py:236
  141.0 9.4 %product.6 = (bf16[2,256,1024]{2,1,0:T(8,128)(2,1)}, bf16[2,256,1024]{2,1,0:T(8,128)(2,1)}) custom-call(s32[4]{0:T(128)} %copy-done.2, bf16[4,512,128]{2,1,0:T(8,128)(2,1)} %pad_maximum_fusion.1.refs_0_, bf16[4,512,128]{2,1,0:T(8,128)(2,1)} %collective-permute-done.23.refs_1_, bf16[4,512,128]{2,1,0:T(8,128)(2,1)} %collective-permute-done.25.refs_2_, ...), custom_call_target="tpu_custom_call" | custom-call | flops 1024 | bytes 1024 | tf_op jit(solution)/shard_map/product/pallas_call | solution.py:181
  150.5 3.2 %collective-permute-start.29 = (bf16[2,256,1024]{2,1,0:T(8,128)(2,1)}, bf16[2,256,1024]{2,1,0:T(8,128)(2,1)}, u32[]{:S(2)}, u32[]{:S(2)}) collective-permute-start(bf16[2,256,1024]{2,1,0:T(8,128)(2,1)} %get-tuple-element.52), channel_id=1, source_target_pairs={{0,24},{16,0},{8,16},{24,8},{1,25},{17,1},{9,17},{25,9},{2,26},{18... | collective-permute-start | bytes 3145736 | tf_op jit(solution)/shard_map/ppermute | solution.py:236
  153.7 10.8 %collective-permute-done.32.b = bf16[2,256,1024]{2,1,0:T(8,128)(2,1)} collective-permute-done((bf16[2,256,1024]{2,1,0:T(8,128)(2,1)}, bf16[2,256,1024]{2,1,0:T(8,128)(2,1)}, u32[]{:S(2)}, u32[]{:S(2)}) %collective-permute-start.32) | collective-permute-done | bytes 1048608 | tf_op jit(solution)/shard_map/ppermute | solution.py:236
  164.6 3.2 %total.2.rest_0_ = f32[256,2,2048]{2,1,0:T(2,128)} custom-call(bf16[2,256,1024]{2,1,0:T(8,128)(2,1)} %get-tuple-element.53.a, bf16[2,256,1024]{2,1,0:T(8,128)(2,1)} %collective-permute-done.32.b, bf16[2,256,1024]{2,1,0:T(8,128)(2,1)} %collective-permute-done.33.c), custom_call_target="tpu_custom_call" | custom-call | flops 1024 | bytes 1024 | tf_op jit(solution)/shard_map/total/pallas_call | solution.py:217
  167.7 17.3 %collective-permute-done.28.b = bf16[2,256,1024]{2,1,0:T(8,128)(2,1)} collective-permute-done((bf16[2,256,1024]{2,1,0:T(8,128)(2,1)}, bf16[2,256,1024]{2,1,0:T(8,128)(2,1)}, u32[]{:S(2)}, u32[]{:S(2)}) %collective-permute-start.28) | collective-permute-done | bytes 1048608 | tf_op jit(solution)/shard_map/ppermute | solution.py:236
  185.0 3.2 %total.3 = f32[256,2,2048]{2,1,0:T(2,128)} custom-call(bf16[2,256,1024]{2,1,0:T(8,128)(2,1)} %get-tuple-element.46.a, bf16[2,256,1024]{2,1,0:T(8,128)(2,1)} %collective-permute-done.28.b, bf16[2,256,1024]{2,1,0:T(8,128)(2,1)} %collective-permute-done.29.c, f32[256,2,2048]{2,1,0:T(2,128)} %total.2.rest_0_), custom_call_target="tpu_custom_call", output_to_operand_aliasing={{}: (3, {})} | custom-call | flops 1024 | bytes 1024 | tf_op jit(solution)/shard_map/total/pallas_call | solution.py:217
  (110 shorter events, 30.4 us)
Async XLA Ops:
  33.1 13.4 %collective-permute-start.8 = (bf16[128,1024]{1,0:T(8,128)(2,1)S(1)}, bf16[128,1024]{1,0:T(8,128)(2,1)S(1)}, u32[]{:S(2)}, u32[]{:S(2)}) collective-permute-start(bf16[128,1024]{1,0:T(8,128)(2,1)S(1)} %get-tuple-element.38), channel_id=1, source_target_pairs={{0,3},{1,0},{2,1},{3,2},{4,7},{5,4},{6,5},{7,6},{8,11},{9,8},{10,9... | collective-permute-start | bytes 786440 | tf_op jit(solution)/shard_map/ppermute | solution.py:269
  35.7 13.8 %collective-permute-start = (bf16[1024,128]{1,0:T(8,128)(2,1)S(1)}, bf16[1024,128]{1,0:T(8,128)(2,1)S(1)}, u32[]{:S(2)}, u32[]{:S(2)}) collective-permute-start(bf16[1024,128]{1,0:T(8,128)(2,1)S(1)} %get-tuple-element.32), channel_id=1, source_target_pairs={{0,32},{32,64},{64,96},{96,0},{1,33},{33,65},{65,97},{97,1},{2,34}... | collective-permute-start | bytes 786440 | tf_op jit(solution)/shard_map/ppermute | solution.py:268
  37.1 13.5 %collective-permute-start.1 = (bf16[1024,128]{1,0:T(8,128)(2,1)S(1)}, bf16[1024,128]{1,0:T(8,128)(2,1)S(1)}, u32[]{:S(2)}, u32[]{:S(2)}) collective-permute-start(bf16[1024,128]{1,0:T(8,128)(2,1)S(1)} %get-tuple-element.33), channel_id=1, source_target_pairs={{0,64},{32,96},{64,0},{96,32},{1,65},{33,97},{65,1},{97,33},{2,66}... | collective-permute-start | bytes 786440 | tf_op jit(solution)/shard_map/ppermute | solution.py:268
  46.6 14.9 %collective-permute-start.10 = (bf16[4,128,512]{2,1,0:T(8,128)(2,1)S(1)}, bf16[4,128,512]{2,1,0:T(8,128)(2,1)S(1)}, u32[]{:S(2)}, u32[]{:S(2)}) collective-permute-start(bf16[4,128,512]{2,1,0:T(8,128)(2,1)S(1)} %pad_maximum_fusion.3.refs_4_), channel_id=1, source_target_pairs={{0,96},{32,0},{64,32},{96,64},{1,97},{33,1},{65,33},{97,65},{2,98}... | collective-permute-start | bytes 1572872 | tf_op jit(solution)/shard_map/ppermute | solution.py:275
  49.4 14.0 %collective-permute-start.9 = (bf16[4,128,512]{2,1,0:T(8,128)(2,1)S(1)}, bf16[4,128,512]{2,1,0:T(8,128)(2,1)S(1)}, u32[]{:S(2)}, u32[]{:S(2)}) collective-permute-start(bf16[4,128,512]{2,1,0:T(8,128)(2,1)S(1)} %pad_maximum_fusion.3.refs_4_), channel_id=1, source_target_pairs={{0,32},{32,64},{64,96},{96,0},{1,33},{33,65},{65,97},{97,1},{2,34}... | collective-permute-start | bytes 1572872 | tf_op jit(solution)/shard_map/ppermute | solution.py:275
  49.4 15.7 %collective-permute-start.12 = (bf16[4,128,512]{2,1,0:T(8,128)(2,1)S(1)}, bf16[4,128,512]{2,1,0:T(8,128)(2,1)}, u32[]{:S(2)}, u32[]{:S(2)}) collective-permute-start(bf16[4,128,512]{2,1,0:T(8,128)(2,1)S(1)} %pad_maximum_fusion.3.refs_4_), channel_id=1, source_target_pairs={{0,4},{4,0},{1,5},{5,1},{2,6},{6,2},{3,7},{7,3},{8,12},{12,8},{9,1... | collective-permute-start | bytes 1572872 | tf_op jit(solution)/shard_map/ppermute | solution.py:244
  52.0 14.9 %collective-permute-start.4 = (bf16[4,512,128]{2,1,0:T(8,128)(2,1)S(1)}, bf16[4,512,128]{2,1,0:T(8,128)(2,1)S(1)}, u32[]{:S(2)}, u32[]{:S(2)}) collective-permute-start(bf16[4,512,128]{2,1,0:T(8,128)(2,1)S(1)} %pad_maximum_fusion.refs_0_), channel_id=1, source_target_pairs={{0,2},{1,3},{2,0},{3,1},{4,6},{5,7},{6,4},{7,5},{8,10},{9,11},{10,... | collective-permute-start | bytes 1572872 | tf_op jit(solution)/shard_map/ppermute | solution.py:276
  63.5 13.4 %collective-permute-start.11 = (bf16[4,128,512]{2,1,0:T(8,128)(2,1)S(1)}, bf16[4,128,512]{2,1,0:T(8,128)(2,1)S(1)}, u32[]{:S(2)}, u32[]{:S(2)}) collective-permute-start(bf16[4,128,512]{2,1,0:T(8,128)(2,1)S(1)} %pad_maximum_fusion.3.refs_4_), channel_id=1, source_target_pairs={{0,64},{32,96},{64,0},{96,32},{1,65},{33,97},{65,1},{97,33},{2,66}... | collective-permute-start | bytes 1572872 | tf_op jit(solution)/shard_map/ppermute | solution.py:278
  65.2 15.4 %collective-permute-start.3 = (bf16[4,512,128]{2,1,0:T(8,128)(2,1)S(1)}, bf16[4,512,128]{2,1,0:T(8,128)(2,1)S(1)}, u32[]{:S(2)}, u32[]{:S(2)}) collective-permute-start(bf16[4,512,128]{2,1,0:T(8,128)(2,1)S(1)} %pad_maximum_fusion.refs_0_), channel_id=1, source_target_pairs={{0,1},{1,2},{2,3},{3,0},{4,5},{5,6},{6,7},{7,4},{8,9},{9,10},{10,1... | collective-permute-start | bytes 1572872 | tf_op jit(solution)/shard_map/ppermute | solution.py:274
  66.9 15.5 %collective-permute-start.5 = (bf16[4,512,128]{2,1,0:T(8,128)(2,1)S(1)}, bf16[4,512,128]{2,1,0:T(8,128)(2,1)S(1)}, u32[]{:S(2)}, u32[]{:S(2)}) collective-permute-start(bf16[4,512,128]{2,1,0:T(8,128)(2,1)S(1)} %pad_maximum_fusion.refs_0_), channel_id=1, source_target_pairs={{0,3},{1,0},{2,1},{3,2},{4,7},{5,4},{6,5},{7,6},{8,11},{9,8},{10,9... | collective-permute-start | bytes 1572872 | tf_op jit(solution)/shard_map/ppermute | solution.py:274
  77.0 17.8 %collective-permute-start.15 = (bf16[4,128,512]{2,1,0:T(8,128)(2,1)}, bf16[4,128,512]{2,1,0:T(8,128)(2,1)}, u32[]{:S(2)}, u32[]{:S(2)}) collective-permute-start(bf16[4,128,512]{2,1,0:T(8,128)(2,1)} %pad_maximum_fusion.2.refs_4_), channel_id=1, source_target_pairs={{0,32},{32,64},{64,96},{96,0},{1,33},{33,65},{65,97},{97,1},{2,34}... | collective-permute-start | bytes 1572872 | tf_op jit(solution)/shard_map/ppermute | solution.py:284
  79.7 24.5 %collective-permute-start.16 = (bf16[4,128,512]{2,1,0:T(8,128)(2,1)}, bf16[4,128,512]{2,1,0:T(8,128)(2,1)}, u32[]{:S(2)}, u32[]{:S(2)}) collective-permute-start(bf16[4,128,512]{2,1,0:T(8,128)(2,1)} %pad_maximum_fusion.2.refs_4_), channel_id=1, source_target_pairs={{0,64},{32,96},{64,0},{96,32},{1,65},{33,97},{65,1},{97,33},{2,66}... | collective-permute-start | bytes 1572872 | tf_op jit(solution)/shard_map/ppermute | solution.py:285
  80.6 24.1 %collective-permute-start.17 = (bf16[4,128,512]{2,1,0:T(8,128)(2,1)}, bf16[4,128,512]{2,1,0:T(8,128)(2,1)}, u32[]{:S(2)}, u32[]{:S(2)}) collective-permute-start(bf16[4,128,512]{2,1,0:T(8,128)(2,1)} %pad_maximum_fusion.2.refs_4_), channel_id=1, source_target_pairs={{0,96},{32,0},{64,32},{96,64},{1,97},{33,1},{65,33},{97,65},{2,98}... | collective-permute-start | bytes 1572872 | tf_op jit(solution)/shard_map/ppermute | solution.py:284
  82.5 22.7 %collective-permute-start.23 = (bf16[4,512,128]{2,1,0:T(8,128)(2,1)}, bf16[4,512,128]{2,1,0:T(8,128)(2,1)}, u32[]{:S(2)}, u32[]{:S(2)}) collective-permute-start(bf16[4,512,128]{2,1,0:T(8,128)(2,1)} %pad_maximum_fusion.1.refs_0_), channel_id=1, source_target_pairs={{0,1},{1,2},{2,3},{3,0},{4,5},{5,6},{6,7},{7,4},{8,9},{9,10},{10,1... | collective-permute-start | bytes 1572872 | tf_op jit(solution)/shard_map/ppermute | solution.py:283
  84.1 21.6 %collective-permute-start.24 = (bf16[4,512,128]{2,1,0:T(8,128)(2,1)}, bf16[4,512,128]{2,1,0:T(8,128)(2,1)}, u32[]{:S(2)}, u32[]{:S(2)}) collective-permute-start(bf16[4,512,128]{2,1,0:T(8,128)(2,1)} %pad_maximum_fusion.1.refs_0_), channel_id=1, source_target_pairs={{0,3},{1,0},{2,1},{3,2},{4,7},{5,4},{6,5},{7,6},{8,11},{9,8},{10,9... | collective-permute-start | bytes 1572872 | tf_op jit(solution)/shard_map/ppermute | solution.py:283
  105.7 21.8 %collective-permute-start.30 = (bf16[2,256,512]{2,1,0:T(8,128)(2,1)}, bf16[2,256,512]{2,1,0:T(8,128)(2,1)}, u32[]{:S(2)}, u32[]{:S(2)}) collective-permute-start(bf16[2,256,512]{2,1,0:T(8,128)(2,1)} %get-tuple-element.41), channel_id=1, source_target_pairs={{0,16},{16,8},{8,24},{24,0},{1,17},{17,9},{9,25},{25,1},{2,18},{18... | collective-permute-start | bytes 1572872 | tf_op jit(solution)/shard_map/ppermute | solution.py:236
  107.6 19.9 %collective-permute-start.25 = (bf16[4,512,128]{2,1,0:T(8,128)(2,1)}, bf16[4,512,128]{2,1,0:T(8,128)(2,1)}, u32[]{:S(2)}, u32[]{:S(2)}) collective-permute-start(bf16[4,512,128]{2,1,0:T(8,128)(2,1)} %pad_maximum_fusion.1.refs_0_), channel_id=1, source_target_pairs={{0,2},{1,3},{2,0},{3,1},{4,6},{5,7},{6,4},{7,5},{8,10},{9,11},{10,... | collective-permute-start | bytes 1572872 | tf_op jit(solution)/shard_map/ppermute | solution.py:288
  111.0 16.5 %collective-permute-start.31 = (bf16[2,256,512]{2,1,0:T(8,128)(2,1)}, bf16[2,256,512]{2,1,0:T(8,128)(2,1)}, u32[]{:S(2)}, u32[]{:S(2)}) collective-permute-start(bf16[2,256,512]{2,1,0:T(8,128)(2,1)} %get-tuple-element.54), channel_id=1, source_target_pairs={{0,24},{16,0},{8,16},{24,8},{1,25},{17,1},{9,17},{25,9},{2,26},{18... | collective-permute-start | bytes 1572872 | tf_op jit(solution)/shard_map/ppermute | solution.py:236
  124.2 16.0 %collective-permute-start.26 = (bf16[2,256,512]{2,1,0:T(8,128)(2,1)}, bf16[2,256,512]{2,1,0:T(8,128)(2,1)S(1)}, u32[]{:S(2)}, u32[]{:S(2)}) collective-permute-start(bf16[2,256,512]{2,1,0:T(8,128)(2,1)} %get-tuple-element.49), channel_id=1, source_target_pairs={{0,16},{16,8},{8,24},{24,0},{1,17},{17,9},{9,25},{25,1},{2,18},{18... | collective-permute-start | bytes 1572872 | tf_op jit(solution)/shard_map/ppermute | solution.py:236
  124.3 15.9 %collective-permute-start.27 = (bf16[2,256,512]{2,1,0:T(8,128)(2,1)}, bf16[2,256,512]{2,1,0:T(8,128)(2,1)}, u32[]{:S(2)}, u32[]{:S(2)}) collective-permute-start(bf16[2,256,512]{2,1,0:T(8,128)(2,1)} %get-tuple-element.50), channel_id=1, source_target_pairs={{0,24},{16,0},{8,16},{24,8},{1,25},{17,1},{9,17},{25,9},{2,26},{18... | collective-permute-start | bytes 1572872 | tf_op jit(solution)/shard_map/ppermute | solution.py:236
  136.9 27.7 %collective-permute-start.32 = (bf16[2,256,1024]{2,1,0:T(8,128)(2,1)}, bf16[2,256,1024]{2,1,0:T(8,128)(2,1)}, u32[]{:S(2)}, u32[]{:S(2)}) collective-permute-start(bf16[2,256,1024]{2,1,0:T(8,128)(2,1)} %get-tuple-element.55), channel_id=1, source_target_pairs={{0,16},{16,8},{8,24},{24,0},{1,17},{17,9},{9,25},{25,1},{2,18},{18... | collective-permute-start | bytes 3145736 | tf_op jit(solution)/shard_map/ppermute | solution.py:236
  137.0 27.6 %collective-permute-start.33 = (bf16[2,256,1024]{2,1,0:T(8,128)(2,1)}, bf16[2,256,1024]{2,1,0:T(8,128)(2,1)}, u32[]{:S(2)}, u32[]{:S(2)}) collective-permute-start(bf16[2,256,1024]{2,1,0:T(8,128)(2,1)} %get-tuple-element.56), channel_id=1, source_target_pairs={{0,24},{16,0},{8,16},{24,8},{1,25},{17,1},{9,17},{25,9},{2,26},{18... | collective-permute-start | bytes 3145736 | tf_op jit(solution)/shard_map/ppermute | solution.py:236
  150.4 34.6 %collective-permute-start.28 = (bf16[2,256,1024]{2,1,0:T(8,128)(2,1)}, bf16[2,256,1024]{2,1,0:T(8,128)(2,1)}, u32[]{:S(2)}, u32[]{:S(2)}) collective-permute-start(bf16[2,256,1024]{2,1,0:T(8,128)(2,1)} %get-tuple-element.51), channel_id=1, source_target_pairs={{0,16},{16,8},{8,24},{24,0},{1,17},{17,9},{9,25},{25,1},{2,18},{18... | collective-permute-start | bytes 3145736 | tf_op jit(solution)/shard_map/ppermute | solution.py:236
  150.5 34.5 %collective-permute-start.29 = (bf16[2,256,1024]{2,1,0:T(8,128)(2,1)}, bf16[2,256,1024]{2,1,0:T(8,128)(2,1)}, u32[]{:S(2)}, u32[]{:S(2)}) collective-permute-start(bf16[2,256,1024]{2,1,0:T(8,128)(2,1)} %get-tuple-element.52), channel_id=1, source_target_pairs={{0,24},{16,0},{8,16},{24,8},{1,25},{17,1},{9,17},{25,9},{2,26},{18... | collective-permute-start | bytes 3145736 | tf_op jit(solution)/shard_map/ppermute | solution.py:236
  (29 other events, 362.5 us)

commit v6 on v5

--- a/solution.py
+++ b/solution.py
@@ -198,7 +198,7 @@
             ],
         ),
         out_shape=shapes,
-        compiler_params=pltpu.CompilerParams(vmem_limit_bytes=VMEM),
+        compiler_params=pltpu.CompilerParams(vmem_limit_bytes=30*2**20),
         cost_estimate=pl.CostEstimate(flops=2**10, bytes_accessed=2**10, transcendentals=0),
         name="product",
     )(place, *rows, *own, *other, *got)
@@ -221,7 +221,7 @@
         out_specs=pl.BlockSpec((128, 2, 1024), lambda n: (n, 0, chunk)),
         out_shape=jax.ShapeDtypeStruct((256, 2, 2048), jnp.float32),
         input_output_aliases={3: 0} if more else {},
-        compiler_params=pltpu.CompilerParams(vmem_limit_bytes=VMEM),
+        compiler_params=pltpu.CompilerParams(vmem_limit_bytes=30*2**20),
         cost_estimate=pl.CostEstimate(flops=2**10, bytes_accessed=2**10, transcendentals=0),
         name="total",
     )(*parts, *more)

time: 188 us -> 183 us (0.973)
  Pallas kernels: 66.1 us -> 56.9 us
  waiting for transfers between devices: 63.4 us -> 71.7 us
  local copies, waits for them, and re-layouts: 9.62 us -> 7.3 us
    pallas_call x4, Pallas kernels: 37.3 us -> 30.4 us  [product(): pl.pallas_call(product_kernel, grid_spec=pltpu.PrefetchScalarGridSpec(num...]
    ppermute x8, waiting for transfers between devices: 28.1 us -> 32.2 us  [along_z(): lax.ppermute(block, ('zl', 'zh'), [(place(i), place((i + shift) % 4)) for...]
    pallas_call x2, Pallas kernels: 6.31 us -> 3.8 us  [total(): pl.pallas_call(total_kernel, grid=(2,), in_specs=[spec] * 3 + [pl.BlockSp...]
    unnamed x38 -> x10, local copies, waits for them, and re-layouts: 2.35 us -> 0.02 us
  transfers between devices with their start and end apart: 34 -> 34, of which waited for: 11 -> 13; matrix products, arithmetic and copies ran while one was open for 1% -> 0% of each run, Pallas kernels for 22% -> 18%
where the time goes in v6:
time: 183 us
  waiting for transfers between devices  71.7 us (39%)
  Pallas kernels  56.9 us (31%)
  starting transfers between devices  45.7 us (25%)
  local copies, waits for them, and re-layouts  7.3 us (4%)
    ppermute x8, waiting for transfers between devices, along_z(): lax.ppermute(block, ('zl', 'zh'), [(place(i), place((i + shift) % 4)) for...  32.2 us
    pallas_call x4, Pallas kernels, product(): pl.pallas_call(product_kernel, grid_spec=pltpu.PrefetchScalarGridSpec(num...  30.4 us
    pallas_call x1, Pallas kernels, densities(): pl.pallas_call(density_kernel, grid_spec=pltpu.PrefetchScalarGridSpec(num...  22.7 us
    ppermute x8, starting transfers between devices, along_z(): lax.ppermute(block, ('zl', 'zh'), [(place(i), place((i + shift) % 4)) for...  15.3 us
    ppermute x2, waiting for transfers between devices, local(): own_a[s] = lax.ppermute(col_a, 'x', ring(s))  11.3 us
    ppermute x1, waiting for transfers between devices, local(): own_b[2] = lax.ppermute(col_b, 'x', ring(2))  10.7 us
    ppermute x1, waiting for transfers between devices, local(): own_a[2] = lax.ppermute(col_a, 'x', ring(2))  9.56 us
    ppermute x3, starting transfers between devices, local(): row[s] = lax.ppermute(parts[s], 'x', ring(s))  6.97 us
  transfers between devices with their start and end apart: 34, of which 13 were waited for; matrix products, arithmetic and copies ran while one was open for 0% of the time, Pallas kernels for 18%

profile of v6, /device:TPU:8, one launch (start us, length us, event | category | flops | bytes accessed | tf_op | source)
XLA Modules:
  0.0 183.1 jit_solution(12254508832303006208)
XLA Ops:
  0.8 2.0 %constant_dynamic-slice_fusion = bf16[8,2,32768]{2,1,0:T(2,128)(2,1)S(1)} fusion(bf16[64,2,32768]{2,1,0:T(2,128)(2,1)} %param.11, s32[]{:T(128)S(6)} %select_n.50), kind=kLoop, calls=%fused_computation.34 | loop fusion | bytes 2097156 | tf_op jit(solution)/shard_map/dynamic_slice | solution.py:253
  4.4 1.9 %constant_dynamic-slice_fusion.1 = bf16[8,2,32768]{2,1,0:T(2,128)(2,1)S(1)} fusion(bf16[64,2,32768]{2,1,0:T(2,128)(2,1)} %param.10, s32[]{:T(128)S(6)} %select_n.49), kind=kLoop, calls=%fused_computation.35 | loop fusion | bytes 2097156 | tf_op jit(solution)/shard_map/dynamic_slice | solution.py:252
  8.2 22.7 %densities.1 = (bf16[1024,128]{1,0:T(8,128)(2,1)S(1)}, bf16[1024,128]{1,0:T(8,128)(2,1)S(1)}, bf16[1024,128]{1,0:T(8,128)(2,1)S(1)}, bf16[1024,128]{1,0:T(8,128)...) custom-call(s32[8192]{0:T(1024)S(1)} %and_add_fusion.pos, ...), custom_call_target="tpu_custom_call" | custom-call | tf_op jit(solution)/shard_map/densities/pallas_call | solution.py:94
  33.4 2.5 %collective-permute-start.8 = (bf16[128,1024]{1,0:T(8,128)(2,1)S(1)}, bf16[128,1024]{1,0:T(8,128)(2,1)S(1)}, u32[]{:S(2)}, u32[]{:S(2)}) collective-permute-start(bf16[128,1024]{1,0:T(8,128)(2,1)S(1)} %get-tuple-element.38), channel_id=1, source_target_pairs={{0,3},{1,0},{2,1},{3,2},{4,7},{5,4},{6,5},{7,6},{8,11},{9,8},{10,9... | collective-permute-start | bytes 786440 | tf_op jit(solution)/shard_map/ppermute | solution.py:269
  37.4 2.7 %collective-permute-start.1 = (bf16[1024,128]{1,0:T(8,128)(2,1)S(1)}, bf16[1024,128]{1,0:T(8,128)(2,1)S(1)}, u32[]{:S(2)}, u32[]{:S(2)}) collective-permute-start(bf16[1024,128]{1,0:T(8,128)(2,1)S(1)} %get-tuple-element.33), channel_id=1, source_target_pairs={{0,64},{32,96},{64,0},{96,32},{1,65},{33,97},{65,1},{97,33},{2,66}... | collective-permute-start | bytes 786440 | tf_op jit(solution)/shard_map/ppermute | solution.py:268
  40.2 2.7 %collective-permute-start.2 = (bf16[1024,128]{1,0:T(8,128)(2,1)S(1)}, bf16[1024,128]{1,0:T(8,128)(2,1)S(1)}, u32[]{:S(2)}, u32[]{:S(2)}) collective-permute-start(bf16[1024,128]{1,0:T(8,128)(2,1)S(1)} %get-tuple-element.34), channel_id=1, source_target_pairs={{0,96},{32,0},{64,32},{96,64},{1,97},{33,1},{65,33},{97,65},{2,98}... | collective-permute-start | bytes 786440 | tf_op jit(solution)/shard_map/ppermute | solution.py:268
  43.3 3.4 %collective-permute-done.8 = bf16[128,1024]{1,0:T(8,128)(2,1)S(1)} collective-permute-done((bf16[128,1024]{1,0:T(8,128)(2,1)S(1)}, bf16[128,1024]{1,0:T(8,128)(2,1)S(1)}, u32[]{:S(2)}, u32[]{:S(2)}) %collective-permute-start.8) | collective-permute-done | bytes 262176 | tf_op jit(solution)/shard_map/ppermute | solution.py:269
  46.8 2.8 %collective-permute-start.10 = (bf16[4,128,512]{2,1,0:T(8,128)(2,1)S(1)}, bf16[4,128,512]{2,1,0:T(8,128)(2,1)S(1)}, u32[]{:S(2)}, u32[]{:S(2)}) collective-permute-start(bf16[4,128,512]{2,1,0:T(8,128)(2,1)S(1)} %pad_maximum_fusion.3.refs_4_), channel_id=1, source_target_pairs={{0,96},{32,0},{64,32},{96,64},{1,97},{33,1},{65,33},{97,65},{2,98}... | collective-permute-start | bytes 1572872 | tf_op jit(solution)/shard_map/ppermute | solution.py:275
  52.4 9.4 %collective-permute-done.10.refs_7_ = bf16[4,128,512]{2,1,0:T(8,128)(2,1)S(1)} collective-permute-done((bf16[4,128,512]{2,1,0:T(8,128)(2,1)S(1)}, bf16[4,128,512]{2,1,0:T(8,128)(2,1)S(1)}, u32[]{:S(2)}, u32[]{:S(2)}) %collective-permute-start.10) | collective-permute-done | bytes 524320 | tf_op jit(solution)/shard_map/ppermute | solution.py:275
  67.5 9.6 %collective-permute-done.11.refs_6_ = bf16[4,128,512]{2,1,0:T(8,128)(2,1)S(1)} collective-permute-done((bf16[4,128,512]{2,1,0:T(8,128)(2,1)S(1)}, bf16[4,128,512]{2,1,0:T(8,128)(2,1)S(1)}, u32[]{:S(2)}, u32[]{:S(2)}) %collective-permute-start.11) | collective-permute-done | bytes 524320 | tf_op jit(solution)/shard_map/ppermute | solution.py:278
  77.1 2.7 %collective-permute-start.15 = (bf16[4,128,512]{2,1,0:T(8,128)(2,1)S(1)}, bf16[4,128,512]{2,1,0:T(8,128)(2,1)S(1)}, u32[]{:S(2)}, u32[]{:S(2)}) collective-permute-start(bf16[4,128,512]{2,1,0:T(8,128)(2,1)S(1)} %pad_maximum_fusion.2.refs_4_), channel_id=1, source_target_pairs={{0,32},{32,64},{64,96},{96,0},{1,33},{33,65},{65,97},{97,1},{2,34}... | collective-permute-start | bytes 1572872 | tf_op jit(solution)/shard_map/ppermute | solution.py:284
  82.5 2.0 %collective-permute-start.24 = (bf16[4,512,128]{2,1,0:T(8,128)(2,1)S(1)}, bf16[4,512,128]{2,1,0:T(8,128)(2,1)S(1)}, u32[]{:S(2)}, u32[]{:S(2)}) collective-permute-start(bf16[4,512,128]{2,1,0:T(8,128)(2,1)S(1)} %pad_maximum_fusion.1.refs_0_), channel_id=1, source_target_pairs={{0,3},{1,0},{2,1},{3,2},{4,7},{5,4},{6,5},{7,6},{8,11},{9,8},{10,9... | collective-permute-start | bytes 1572872 | tf_op jit(solution)/shard_map/ppermute | solution.py:283
  84.6 7.5 %product.4 = (bf16[2,256,512]{2,1,0:T(8,128)(2,1)S(1)}, bf16[2,256,512]{2,1,0:T(8,128)(2,1)S(1)}, bf16[2,256,1024]{2,1,0:T(8,128)(2,1)S(1)}) custom-call(s32[4]{0:T(128)S(1)} %pad_add_fusion.place, bf16[4,512,128]{2,1,0:T(8,128)(2,1)S(1)} %pad_maximum_fusion.refs_0_, bf16[4,512,128]{2,1,0:T(8,128)(2,1)S(1)} %collective-permute-done.3.refs_1_, ...), custom_call_target="tpu_custom_call" | custom-call | flops 1024 | bytes 1024 | tf_op jit(solution)/shard_map/product/pallas_call | solution.py:181
  93.2 10.7 %collective-permute-done.16.refs_6_ = bf16[4,128,512]{2,1,0:T(8,128)(2,1)S(1)} collective-permute-done((bf16[4,128,512]{2,1,0:T(8,128)(2,1)S(1)}, bf16[4,128,512]{2,1,0:T(8,128)(2,1)S(1)}, u32[]{:S(2)}, u32[]{:S(2)}) %collective-permute-start.16) | collective-permute-done | bytes 524320 | tf_op jit(solution)/shard_map/ppermute | solution.py:285
  107.4 3.3 %collective-permute-start.25 = (bf16[4,512,128]{2,1,0:T(8,128)(2,1)S(1)}, bf16[4,512,128]{2,1,0:T(8,128)(2,1)S(1)}, u32[]{:S(2)}, u32[]{:S(2)}) collective-permute-start(bf16[4,512,128]{2,1,0:T(8,128)(2,1)S(1)} %pad_maximum_fusion.1.refs_0_), channel_id=1, source_target_pairs={{0,2},{1,3},{2,0},{3,1},{4,6},{5,7},{6,4},{7,5},{8,10},{9,11},{10,... | collective-permute-start | bytes 1572872 | tf_op jit(solution)/shard_map/ppermute | solution.py:288
  110.8 3.0 %collective-permute-start.31 = (bf16[2,256,512]{2,1,0:T(8,128)(2,1)S(1)}, bf16[2,256,512]{2,1,0:T(8,128)(2,1)S(1)}, u32[]{:S(2)}, u32[]{:S(2)}) collective-permute-start(bf16[2,256,512]{2,1,0:T(8,128)(2,1)S(1)} %get-tuple-element.54), channel_id=1, source_target_pairs={{0,24},{16,0},{8,16},{24,8},{1,25},{17,1},{9,17},{25,9},{2,26},{18... | collective-permute-start | bytes 1572872 | tf_op jit(solution)/shard_map/ppermute | solution.py:236
  113.8 7.5 %product.5 = (bf16[2,256,512]{2,1,0:T(8,128)(2,1)S(1)}, bf16[2,256,512]{2,1,0:T(8,128)(2,1)S(1)}, bf16[2,256,1024]{2,1,0:T(8,128)(2,1)S(1)}) custom-call(s32[4]{0:T(128)S(1)} %pad_add_fusion.place, bf16[4,512,128]{2,1,0:T(8,128)(2,1)S(1)} %pad_maximum_fusion.refs_0_, bf16[4,512,128]{2,1,0:T(8,128)(2,1)S(1)} %collective-permute-done.3.refs_1_, ...), custom_call_target="tpu_custom_call" | custom-call | flops 1024 | bytes 1024 | tf_op jit(solution)/shard_map/product/pallas_call | solution.py:181
  121.4 3.2 %collective-permute-start.27 = (bf16[2,256,512]{2,1,0:T(8,128)(2,1)S(1)}, bf16[2,256,512]{2,1,0:T(8,128)(2,1)S(1)}, u32[]{:S(2)}, u32[]{:S(2)}) collective-permute-start(bf16[2,256,512]{2,1,0:T(8,128)(2,1)S(1)} %get-tuple-element.50), channel_id=1, source_target_pairs={{0,24},{16,0},{8,16},{24,8},{1,25},{17,1},{9,17},{25,9},{2,26},{18... | collective-permute-start | bytes 1572872 | tf_op jit(solution)/shard_map/ppermute | solution.py:236
  125.9 7.7 %product.7 = (bf16[2,256,1024]{2,1,0:T(8,128)(2,1)S(1)}, bf16[2,256,1024]{2,1,0:T(8,128)(2,1)S(1)}) custom-call(s32[4]{0:T(128)S(1)} %pad_add_fusion.place, bf16[4,512,128]{2,1,0:T(8,128)(2,1)S(1)} %pad_maximum_fusion.1.refs_0_, bf16[4,512,128]{2,1,0:T(8,128)(2,1)S(1)} %collective-permute-done.23.refs_1_, ...), custom_call_target="tpu_custom_call" | custom-call | flops 1024 | bytes 1024 | tf_op jit(solution)/shard_map/product/pallas_call | solution.py:181
  135.3 2.1 %collective-permute-start.33 = (bf16[2,256,1024]{2,1,0:T(8,128)(2,1)S(1)}, bf16[2,256,1024]{2,1,0:T(8,128)(2,1)S(1)}, u32[]{:S(2)}, u32[]{:S(2)}) collective-permute-start(bf16[2,256,1024]{2,1,0:T(8,128)(2,1)S(1)} %get-tuple-element.56), channel_id=1, source_target_pairs={{0,24},{16,0},{8,16},{24,8},{1,25},{17,1},{9,17},{25,9},{2,26},{18... | collective-permute-start | bytes 3145736 | tf_op jit(solution)/shard_map/ppermute | solution.py:236
  137.5 7.7 %product.6 = (bf16[2,256,1024]{2,1,0:T(8,128)(2,1)S(1)}, bf16[2,256,1024]{2,1,0:T(8,128)(2,1)S(1)}) custom-call(s32[4]{0:T(128)S(1)} %pad_add_fusion.place, bf16[4,512,128]{2,1,0:T(8,128)(2,1)S(1)} %pad_maximum_fusion.1.refs_0_, bf16[4,512,128]{2,1,0:T(8,128)(2,1)S(1)} %collective-permute-done.23.refs_1_, ...), custom_call_target="tpu_custom_call" | custom-call | flops 1024 | bytes 1024 | tf_op jit(solution)/shard_map/product/pallas_call | solution.py:181
  145.3 3.2 %collective-permute-start.29 = (bf16[2,256,1024]{2,1,0:T(8,128)(2,1)S(1)}, bf16[2,256,1024]{2,1,0:T(8,128)(2,1)S(1)}, u32[]{:S(2)}, u32[]{:S(2)}) collective-permute-start(bf16[2,256,1024]{2,1,0:T(8,128)(2,1)S(1)} %get-tuple-element.52), channel_id=1, source_target_pairs={{0,24},{16,0},{8,16},{24,8},{1,25},{17,1},{9,17},{25,9},{2,26},{18... | collective-permute-start | bytes 3145736 | tf_op jit(solution)/shard_map/ppermute | solution.py:236
  148.5 13.0 %collective-permute-done.32.b = bf16[2,256,1024]{2,1,0:T(8,128)(2,1)S(1)} collective-permute-done((bf16[2,256,1024]{2,1,0:T(8,128)(2,1)S(1)}, bf16[2,256,1024]{2,1,0:T(8,128)(2,1)S(1)}, u32[]{:S(2)}, u32[]{:S(2)}) %collective-permute-start.32) | collective-permute-done | bytes 1048608 | tf_op jit(solution)/shard_map/ppermute | solution.py:236
  163.4 17.9 %collective-permute-done.28.b = bf16[2,256,1024]{2,1,0:T(8,128)(2,1)S(1)} collective-permute-done((bf16[2,256,1024]{2,1,0:T(8,128)(2,1)S(1)}, bf16[2,256,1024]{2,1,0:T(8,128)(2,1)S(1)}, u32[]{:S(2)}, u32[]{:S(2)}) %collective-permute-start.28) | collective-permute-done | bytes 1048608 | tf_op jit(solution)/shard_map/ppermute | solution.py:236
  (82 shorter events, 30.8 us)
Async XLA Ops:
  33.4 13.4 %collective-permute-start.8 = (bf16[128,1024]{1,0:T(8,128)(2,1)S(1)}, bf16[128,1024]{1,0:T(8,128)(2,1)S(1)}, u32[]{:S(2)}, u32[]{:S(2)}) collective-permute-start(bf16[128,1024]{1,0:T(8,128)(2,1)S(1)} %get-tuple-element.38), channel_id=1, source_target_pairs={{0,3},{1,0},{2,1},{3,2},{4,7},{5,4},{6,5},{7,6},{8,11},{9,8},{10,9... | collective-permute-start | bytes 786440 | tf_op jit(solution)/shard_map/ppermute | solution.py:269
  35.9 13.8 %collective-permute-start = (bf16[1024,128]{1,0:T(8,128)(2,1)S(1)}, bf16[1024,128]{1,0:T(8,128)(2,1)S(1)}, u32[]{:S(2)}, u32[]{:S(2)}) collective-permute-start(bf16[1024,128]{1,0:T(8,128)(2,1)S(1)} %get-tuple-element.32), channel_id=1, source_target_pairs={{0,32},{32,64},{64,96},{96,0},{1,33},{33,65},{65,97},{97,1},{2,34}... | collective-permute-start | bytes 786440 | tf_op jit(solution)/shard_map/ppermute | solution.py:268
  37.4 13.5 %collective-permute-start.1 = (bf16[1024,128]{1,0:T(8,128)(2,1)S(1)}, bf16[1024,128]{1,0:T(8,128)(2,1)S(1)}, u32[]{:S(2)}, u32[]{:S(2)}) collective-permute-start(bf16[1024,128]{1,0:T(8,128)(2,1)S(1)} %get-tuple-element.33), channel_id=1, source_target_pairs={{0,64},{32,96},{64,0},{96,32},{1,65},{33,97},{65,1},{97,33},{2,66}... | collective-permute-start | bytes 786440 | tf_op jit(solution)/shard_map/ppermute | solution.py:268
  46.8 14.9 %collective-permute-start.10 = (bf16[4,128,512]{2,1,0:T(8,128)(2,1)S(1)}, bf16[4,128,512]{2,1,0:T(8,128)(2,1)S(1)}, u32[]{:S(2)}, u32[]{:S(2)}) collective-permute-start(bf16[4,128,512]{2,1,0:T(8,128)(2,1)S(1)} %pad_maximum_fusion.3.refs_4_), channel_id=1, source_target_pairs={{0,96},{32,0},{64,32},{96,64},{1,97},{33,1},{65,33},{97,65},{2,98}... | collective-permute-start | bytes 1572872 | tf_op jit(solution)/shard_map/ppermute | solution.py:275
  49.7 14.0 %collective-permute-start.9 = (bf16[4,128,512]{2,1,0:T(8,128)(2,1)S(1)}, bf16[4,128,512]{2,1,0:T(8,128)(2,1)S(1)}, u32[]{:S(2)}, u32[]{:S(2)}) collective-permute-start(bf16[4,128,512]{2,1,0:T(8,128)(2,1)S(1)} %pad_maximum_fusion.3.refs_4_), channel_id=1, source_target_pairs={{0,32},{32,64},{64,96},{96,0},{1,33},{33,65},{65,97},{97,1},{2,34}... | collective-permute-start | bytes 1572872 | tf_op jit(solution)/shard_map/ppermute | solution.py:275
  49.7 15.6 %collective-permute-start.12 = (bf16[4,128,512]{2,1,0:T(8,128)(2,1)S(1)}, bf16[4,128,512]{2,1,0:T(8,128)(2,1)S(1)}, u32[]{:S(2)}, u32[]{:S(2)}) collective-permute-start(bf16[4,128,512]{2,1,0:T(8,128)(2,1)S(1)} %pad_maximum_fusion.3.refs_4_), channel_id=1, source_target_pairs={{0,4},{4,0},{1,5},{5,1},{2,6},{6,2},{3,7},{7,3},{8,12},{12,8},{9,1... | collective-permute-start | bytes 1572872 | tf_op jit(solution)/shard_map/ppermute | solution.py:244
  52.3 14.8 %collective-permute-start.4 = (bf16[4,512,128]{2,1,0:T(8,128)(2,1)S(1)}, bf16[4,512,128]{2,1,0:T(8,128)(2,1)S(1)}, u32[]{:S(2)}, u32[]{:S(2)}) collective-permute-start(bf16[4,512,128]{2,1,0:T(8,128)(2,1)S(1)} %pad_maximum_fusion.refs_0_), channel_id=1, source_target_pairs={{0,2},{1,3},{2,0},{3,1},{4,6},{5,7},{6,4},{7,5},{8,10},{9,11},{10,... | collective-permute-start | bytes 1572872 | tf_op jit(solution)/shard_map/ppermute | solution.py:276
  63.7 13.4 %collective-permute-start.11 = (bf16[4,128,512]{2,1,0:T(8,128)(2,1)S(1)}, bf16[4,128,512]{2,1,0:T(8,128)(2,1)S(1)}, u32[]{:S(2)}, u32[]{:S(2)}) collective-permute-start(bf16[4,128,512]{2,1,0:T(8,128)(2,1)S(1)} %pad_maximum_fusion.3.refs_4_), channel_id=1, source_target_pairs={{0,64},{32,96},{64,0},{96,32},{1,65},{33,97},{65,1},{97,33},{2,66}... | collective-permute-start | bytes 1572872 | tf_op jit(solution)/shard_map/ppermute | solution.py:278
  65.3 15.3 %collective-permute-start.3 = (bf16[4,512,128]{2,1,0:T(8,128)(2,1)S(1)}, bf16[4,512,128]{2,1,0:T(8,128)(2,1)S(1)}, u32[]{:S(2)}, u32[]{:S(2)}) collective-permute-start(bf16[4,512,128]{2,1,0:T(8,128)(2,1)S(1)} %pad_maximum_fusion.refs_0_), channel_id=1, source_target_pairs={{0,1},{1,2},{2,3},{3,0},{4,5},{5,6},{6,7},{7,4},{8,9},{9,10},{10,1... | collective-permute-start | bytes 1572872 | tf_op jit(solution)/shard_map/ppermute | solution.py:274
  67.1 15.4 %collective-permute-start.5 = (bf16[4,512,128]{2,1,0:T(8,128)(2,1)S(1)}, bf16[4,512,128]{2,1,0:T(8,128)(2,1)S(1)}, u32[]{:S(2)}, u32[]{:S(2)}) collective-permute-start(bf16[4,512,128]{2,1,0:T(8,128)(2,1)S(1)} %pad_maximum_fusion.refs_0_), channel_id=1, source_target_pairs={{0,3},{1,0},{2,1},{3,2},{4,7},{5,4},{6,5},{7,6},{8,11},{9,8},{10,9... | collective-permute-start | bytes 1572872 | tf_op jit(solution)/shard_map/ppermute | solution.py:274
  77.1 16.1 %collective-permute-start.15 = (bf16[4,128,512]{2,1,0:T(8,128)(2,1)S(1)}, bf16[4,128,512]{2,1,0:T(8,128)(2,1)S(1)}, u32[]{:S(2)}, u32[]{:S(2)}) collective-permute-start(bf16[4,128,512]{2,1,0:T(8,128)(2,1)S(1)} %pad_maximum_fusion.2.refs_4_), channel_id=1, source_target_pairs={{0,32},{32,64},{64,96},{96,0},{1,33},{33,65},{65,97},{97,1},{2,34}... | collective-permute-start | bytes 1572872 | tf_op jit(solution)/shard_map/ppermute | solution.py:284
  79.8 24.2 %collective-permute-start.16 = (bf16[4,128,512]{2,1,0:T(8,128)(2,1)S(1)}, bf16[4,128,512]{2,1,0:T(8,128)(2,1)S(1)}, u32[]{:S(2)}, u32[]{:S(2)}) collective-permute-start(bf16[4,128,512]{2,1,0:T(8,128)(2,1)S(1)} %pad_maximum_fusion.2.refs_4_), channel_id=1, source_target_pairs={{0,64},{32,96},{64,0},{96,32},{1,65},{33,97},{65,1},{97,33},{2,66}... | collective-permute-start | bytes 1572872 | tf_op jit(solution)/shard_map/ppermute | solution.py:285
  80.7 23.8 %collective-permute-start.17 = (bf16[4,128,512]{2,1,0:T(8,128)(2,1)S(1)}, bf16[4,128,512]{2,1,0:T(8,128)(2,1)S(1)}, u32[]{:S(2)}, u32[]{:S(2)}) collective-permute-start(bf16[4,128,512]{2,1,0:T(8,128)(2,1)S(1)} %pad_maximum_fusion.2.refs_4_), channel_id=1, source_target_pairs={{0,96},{32,0},{64,32},{96,64},{1,97},{33,1},{65,33},{97,65},{2,98}... | collective-permute-start | bytes 1572872 | tf_op jit(solution)/shard_map/ppermute | solution.py:284
  82.5 22.5 %collective-permute-start.23 = (bf16[4,512,128]{2,1,0:T(8,128)(2,1)S(1)}, bf16[4,512,128]{2,1,0:T(8,128)(2,1)S(1)}, u32[]{:S(2)}, u32[]{:S(2)}) collective-permute-start(bf16[4,512,128]{2,1,0:T(8,128)(2,1)S(1)} %pad_maximum_fusion.1.refs_0_), channel_id=1, source_target_pairs={{0,1},{1,2},{2,3},{3,0},{4,5},{5,6},{6,7},{7,4},{8,9},{9,10},{10,1... | collective-permute-start | bytes 1572872 | tf_op jit(solution)/shard_map/ppermute | solution.py:283
  82.5 23.0 %collective-permute-start.24 = (bf16[4,512,128]{2,1,0:T(8,128)(2,1)S(1)}, bf16[4,512,128]{2,1,0:T(8,128)(2,1)S(1)}, u32[]{:S(2)}, u32[]{:S(2)}) collective-permute-start(bf16[4,512,128]{2,1,0:T(8,128)(2,1)S(1)} %pad_maximum_fusion.1.refs_0_), channel_id=1, source_target_pairs={{0,3},{1,0},{2,1},{3,2},{4,7},{5,4},{6,5},{7,6},{8,11},{9,8},{10,9... | collective-permute-start | bytes 1572872 | tf_op jit(solution)/shard_map/ppermute | solution.py:283
  105.5 19.1 %collective-permute-start.30 = (bf16[2,256,512]{2,1,0:T(8,128)(2,1)S(1)}, bf16[2,256,512]{2,1,0:T(8,128)(2,1)S(1)}, u32[]{:S(2)}, u32[]{:S(2)}) collective-permute-start(bf16[2,256,512]{2,1,0:T(8,128)(2,1)S(1)} %get-tuple-element.41), channel_id=1, source_target_pairs={{0,16},{16,8},{8,24},{24,0},{1,17},{17,9},{9,25},{25,1},{2,18},{18... | collective-permute-start | bytes 1572872 | tf_op jit(solution)/shard_map/ppermute | solution.py:236
  107.4 17.2 %collective-permute-start.25 = (bf16[4,512,128]{2,1,0:T(8,128)(2,1)S(1)}, bf16[4,512,128]{2,1,0:T(8,128)(2,1)S(1)}, u32[]{:S(2)}, u32[]{:S(2)}) collective-permute-start(bf16[4,512,128]{2,1,0:T(8,128)(2,1)S(1)} %pad_maximum_fusion.1.refs_0_), channel_id=1, source_target_pairs={{0,2},{1,3},{2,0},{3,1},{4,6},{5,7},{6,4},{7,5},{8,10},{9,11},{10,... | collective-permute-start | bytes 1572872 | tf_op jit(solution)/shard_map/ppermute | solution.py:288
  110.8 15.1 %collective-permute-start.31 = (bf16[2,256,512]{2,1,0:T(8,128)(2,1)S(1)}, bf16[2,256,512]{2,1,0:T(8,128)(2,1)S(1)}, u32[]{:S(2)}, u32[]{:S(2)}) collective-permute-start(bf16[2,256,512]{2,1,0:T(8,128)(2,1)S(1)} %get-tuple-element.54), channel_id=1, source_target_pairs={{0,24},{16,0},{8,16},{24,8},{1,25},{17,1},{9,17},{25,9},{2,26},{18... | collective-permute-start | bytes 1572872 | tf_op jit(solution)/shard_map/ppermute | solution.py:236
  121.3 16.2 %collective-permute-start.26 = (bf16[2,256,512]{2,1,0:T(8,128)(2,1)S(1)}, bf16[2,256,512]{2,1,0:T(8,128)(2,1)S(1)}, u32[]{:S(2)}, u32[]{:S(2)}) collective-permute-start(bf16[2,256,512]{2,1,0:T(8,128)(2,1)S(1)} %get-tuple-element.49), channel_id=1, source_target_pairs={{0,16},{16,8},{8,24},{24,0},{1,17},{17,9},{9,25},{25,1},{2,18},{18... | collective-permute-start | bytes 1572872 | tf_op jit(solution)/shard_map/ppermute | solution.py:236
  121.4 16.1 %collective-permute-start.27 = (bf16[2,256,512]{2,1,0:T(8,128)(2,1)S(1)}, bf16[2,256,512]{2,1,0:T(8,128)(2,1)S(1)}, u32[]{:S(2)}, u32[]{:S(2)}) collective-permute-start(bf16[2,256,512]{2,1,0:T(8,128)(2,1)S(1)} %get-tuple-element.50), channel_id=1, source_target_pairs={{0,24},{16,0},{8,16},{24,8},{1,25},{17,1},{9,17},{25,9},{2,26},{18... | collective-permute-start | bytes 1572872 | tf_op jit(solution)/shard_map/ppermute | solution.py:236
  133.6 27.8 %collective-permute-start.32 = (bf16[2,256,1024]{2,1,0:T(8,128)(2,1)S(1)}, bf16[2,256,1024]{2,1,0:T(8,128)(2,1)S(1)}, u32[]{:S(2)}, u32[]{:S(2)}) collective-permute-start(bf16[2,256,1024]{2,1,0:T(8,128)(2,1)S(1)} %get-tuple-element.55), channel_id=1, source_target_pairs={{0,16},{16,8},{8,24},{24,0},{1,17},{17,9},{9,25},{25,1},{2,18},{18... | collective-permute-start | bytes 3145736 | tf_op jit(solution)/shard_map/ppermute | solution.py:236
  135.3 26.1 %collective-permute-start.33 = (bf16[2,256,1024]{2,1,0:T(8,128)(2,1)S(1)}, bf16[2,256,1024]{2,1,0:T(8,128)(2,1)S(1)}, u32[]{:S(2)}, u32[]{:S(2)}) collective-permute-start(bf16[2,256,1024]{2,1,0:T(8,128)(2,1)S(1)} %get-tuple-element.56), channel_id=1, source_target_pairs={{0,24},{16,0},{8,16},{24,8},{1,25},{17,1},{9,17},{25,9},{2,26},{18... | collective-permute-start | bytes 3145736 | tf_op jit(solution)/shard_map/ppermute | solution.py:236
  145.2 36.1 %collective-permute-start.28 = (bf16[2,256,1024]{2,1,0:T(8,128)(2,1)S(1)}, bf16[2,256,1024]{2,1,0:T(8,128)(2,1)S(1)}, u32[]{:S(2)}, u32[]{:S(2)}) collective-permute-start(bf16[2,256,1024]{2,1,0:T(8,128)(2,1)S(1)} %get-tuple-element.51), channel_id=1, source_target_pairs={{0,16},{16,8},{8,24},{24,0},{1,17},{17,9},{9,25},{25,1},{2,18},{18... | collective-permute-start | bytes 3145736 | tf_op jit(solution)/shard_map/ppermute | solution.py:236
  145.3 36.0 %collective-permute-start.29 = (bf16[2,256,1024]{2,1,0:T(8,128)(2,1)S(1)}, bf16[2,256,1024]{2,1,0:T(8,128)(2,1)S(1)}, u32[]{:S(2)}, u32[]{:S(2)}) collective-permute-start(bf16[2,256,1024]{2,1,0:T(8,128)(2,1)S(1)} %get-tuple-element.52), channel_id=1, source_target_pairs={{0,24},{16,0},{8,16},{24,8},{1,25},{17,1},{9,17},{25,9},{2,26},{18... | collective-permute-start | bytes 3145736 | tf_op jit(solution)/shard_map/ppermute | solution.py:236
  (15 other events, 129.0 us)

commit v7 on v6

--- a/solution.py
+++ b/solution.py
@@ -198,7 +198,7 @@
             ],
         ),
         out_shape=shapes,
-        compiler_params=pltpu.CompilerParams(vmem_limit_bytes=30*2**20),
+        compiler_params=pltpu.CompilerParams(vmem_limit_bytes=20*2**20),
         cost_estimate=pl.CostEstimate(flops=2**10, bytes_accessed=2**10, transcendentals=0),
         name="product",
     )(place, *rows, *own, *other, *got)
@@ -221,7 +221,7 @@
         out_specs=pl.BlockSpec((128, 2, 1024), lambda n: (n, 0, chunk)),
         out_shape=jax.ShapeDtypeStruct((256, 2, 2048), jnp.float32),
         input_output_aliases={3: 0} if more else {},
-        compiler_params=pltpu.CompilerParams(vmem_limit_bytes=30*2**20),
+        compiler_params=pltpu.CompilerParams(vmem_limit_bytes=20*2**20),
         cost_estimate=pl.CostEstimate(flops=2**10, bytes_accessed=2**10, transcendentals=0),
         name="total",
     )(*parts, *more)

time: 183 us -> 183 us (level)
  no operation moved by 1% of the time
where the time goes in v7:
time: 183 us
  waiting for transfers between devices  71.7 us (39%)
  Pallas kernels  56.9 us (31%)
  starting transfers between devices  45.7 us (25%)
  local copies, waits for them, and re-layouts  7.3 us (4%)
    ppermute x8, waiting for transfers between devices, along_z(): lax.ppermute(block, ('zl', 'zh'), [(place(i), place((i + shift) % 4)) for...  32.2 us
    pallas_call x4, Pallas kernels, product(): pl.pallas_call(product_kernel, grid_spec=pltpu.PrefetchScalarGridSpec(num...  30.4 us
    pallas_call x1, Pallas kernels, densities(): pl.pallas_call(density_kernel, grid_spec=pltpu.PrefetchScalarGridSpec(num...  22.7 us
    ppermute x8, starting transfers between devices, along_z(): lax.ppermute(block, ('zl', 'zh'), [(place(i), place((i + shift) % 4)) for...  15.3 us
    ppermute x2, waiting for transfers between devices, local(): own_a[s] = lax.ppermute(col_a, 'x', ring(s))  11.3 us
    ppermute x1, waiting for transfers between devices, local(): own_b[2] = lax.ppermute(col_b, 'x', ring(2))  10.7 us
    ppermute x1, waiting for transfers between devices, local(): own_a[2] = lax.ppermute(col_a, 'x', ring(2))  9.56 us
    ppermute x3, starting transfers between devices, local(): row[s] = lax.ppermute(parts[s], 'x', ring(s))  6.97 us
  transfers between devices with their start and end apart: 34, of which 13 were waited for; matrix products, arithmetic and copies ran while one was open for 0% of the time, Pallas kernels for 18%

profile of v7, /device:TPU:8, one launch (start us, length us, event | category | flops | bytes accessed | tf_op | source)
XLA Modules:
  0.0 183.1 jit_solution(15757266682543809117)
XLA Ops:
  0.8 2.0 %constant_dynamic-slice_fusion = bf16[8,2,32768]{2,1,0:T(2,128)(2,1)S(1)} fusion(bf16[64,2,32768]{2,1,0:T(2,128)(2,1)} %param.11, s32[]{:T(128)S(6)} %select_n.50), kind=kLoop, calls=%fused_computation.34 | loop fusion | bytes 2097156 | tf_op jit(solution)/shard_map/dynamic_slice | solution.py:253
  4.4 1.9 %constant_dynamic-slice_fusion.1 = bf16[8,2,32768]{2,1,0:T(2,128)(2,1)S(1)} fusion(bf16[64,2,32768]{2,1,0:T(2,128)(2,1)} %param.10, s32[]{:T(128)S(6)} %select_n.49), kind=kLoop, calls=%fused_computation.35 | loop fusion | bytes 2097156 | tf_op jit(solution)/shard_map/dynamic_slice | solution.py:252
  8.2 22.7 %densities.1 = (bf16[1024,128]{1,0:T(8,128)(2,1)S(1)}, bf16[1024,128]{1,0:T(8,128)(2,1)S(1)}, bf16[1024,128]{1,0:T(8,128)(2,1)S(1)}, bf16[1024,128]{1,0:T(8,128)...) custom-call(s32[8192]{0:T(1024)S(1)} %and_add_fusion.pos, ...), custom_call_target="tpu_custom_call" | custom-call | tf_op jit(solution)/shard_map/densities/pallas_call | solution.py:94
  33.4 2.5 %collective-permute-start.8 = (bf16[128,1024]{1,0:T(8,128)(2,1)S(1)}, bf16[128,1024]{1,0:T(8,128)(2,1)S(1)}, u32[]{:S(2)}, u32[]{:S(2)}) collective-permute-start(bf16[128,1024]{1,0:T(8,128)(2,1)S(1)} %get-tuple-element.38), channel_id=1, source_target_pairs={{0,3},{1,0},{2,1},{3,2},{4,7},{5,4},{6,5},{7,6},{8,11},{9,8},{10,9... | collective-permute-start | bytes 786440 | tf_op jit(solution)/shard_map/ppermute | solution.py:269
  37.4 2.7 %collective-permute-start.1 = (bf16[1024,128]{1,0:T(8,128)(2,1)S(1)}, bf16[1024,128]{1,0:T(8,128)(2,1)S(1)}, u32[]{:S(2)}, u32[]{:S(2)}) collective-permute-start(bf16[1024,128]{1,0:T(8,128)(2,1)S(1)} %get-tuple-element.33), channel_id=1, source_target_pairs={{0,64},{32,96},{64,0},{96,32},{1,65},{33,97},{65,1},{97,33},{2,66}... | collective-permute-start | bytes 786440 | tf_op jit(solution)/shard_map/ppermute | solution.py:268
  40.2 2.7 %collective-permute-start.2 = (bf16[1024,128]{1,0:T(8,128)(2,1)S(1)}, bf16[1024,128]{1,0:T(8,128)(2,1)S(1)}, u32[]{:S(2)}, u32[]{:S(2)}) collective-permute-start(bf16[1024,128]{1,0:T(8,128)(2,1)S(1)} %get-tuple-element.34), channel_id=1, source_target_pairs={{0,96},{32,0},{64,32},{96,64},{1,97},{33,1},{65,33},{97,65},{2,98}... | collective-permute-start | bytes 786440 | tf_op jit(solution)/shard_map/ppermute | solution.py:268
  43.3 3.4 %collective-permute-done.8 = bf16[128,1024]{1,0:T(8,128)(2,1)S(1)} collective-permute-done((bf16[128,1024]{1,0:T(8,128)(2,1)S(1)}, bf16[128,1024]{1,0:T(8,128)(2,1)S(1)}, u32[]{:S(2)}, u32[]{:S(2)}) %collective-permute-start.8) | collective-permute-done | bytes 262176 | tf_op jit(solution)/shard_map/ppermute | solution.py:269
  46.8 2.8 %collective-permute-start.10 = (bf16[4,128,512]{2,1,0:T(8,128)(2,1)S(1)}, bf16[4,128,512]{2,1,0:T(8,128)(2,1)S(1)}, u32[]{:S(2)}, u32[]{:S(2)}) collective-permute-start(bf16[4,128,512]{2,1,0:T(8,128)(2,1)S(1)} %pad_maximum_fusion.3.refs_4_), channel_id=1, source_target_pairs={{0,96},{32,0},{64,32},{96,64},{1,97},{33,1},{65,33},{97,65},{2,98}... | collective-permute-start | bytes 1572872 | tf_op jit(solution)/shard_map/ppermute | solution.py:275
  52.4 9.4 %collective-permute-done.10.refs_7_ = bf16[4,128,512]{2,1,0:T(8,128)(2,1)S(1)} collective-permute-done((bf16[4,128,512]{2,1,0:T(8,128)(2,1)S(1)}, bf16[4,128,512]{2,1,0:T(8,128)(2,1)S(1)}, u32[]{:S(2)}, u32[]{:S(2)}) %collective-permute-start.10) | collective-permute-done | bytes 524320 | tf_op jit(solution)/shard_map/ppermute | solution.py:275
  67.5 9.6 %collective-permute-done.11.refs_6_ = bf16[4,128,512]{2,1,0:T(8,128)(2,1)S(1)} collective-permute-done((bf16[4,128,512]{2,1,0:T(8,128)(2,1)S(1)}, bf16[4,128,512]{2,1,0:T(8,128)(2,1)S(1)}, u32[]{:S(2)}, u32[]{:S(2)}) %collective-permute-start.11) | collective-permute-done | bytes 524320 | tf_op jit(solution)/shard_map/ppermute | solution.py:278
  77.1 2.7 %collective-permute-start.15 = (bf16[4,128,512]{2,1,0:T(8,128)(2,1)S(1)}, bf16[4,128,512]{2,1,0:T(8,128)(2,1)S(1)}, u32[]{:S(2)}, u32[]{:S(2)}) collective-permute-start(bf16[4,128,512]{2,1,0:T(8,128)(2,1)S(1)} %pad_maximum_fusion.2.refs_4_), channel_id=1, source_target_pairs={{0,32},{32,64},{64,96},{96,0},{1,33},{33,65},{65,97},{97,1},{2,34}... | collective-permute-start | bytes 1572872 | tf_op jit(solution)/shard_map/ppermute | solution.py:284
  82.5 2.0 %collective-permute-start.24 = (bf16[4,512,128]{2,1,0:T(8,128)(2,1)S(1)}, bf16[4,512,128]{2,1,0:T(8,128)(2,1)S(1)}, u32[]{:S(2)}, u32[]{:S(2)}) collective-permute-start(bf16[4,512,128]{2,1,0:T(8,128)(2,1)S(1)} %pad_maximum_fusion.1.refs_0_), channel_id=1, source_target_pairs={{0,3},{1,0},{2,1},{3,2},{4,7},{5,4},{6,5},{7,6},{8,11},{9,8},{10,9... | collective-permute-start | bytes 1572872 | tf_op jit(solution)/shard_map/ppermute | solution.py:283
  84.6 7.5 %product.4 = (bf16[2,256,512]{2,1,0:T(8,128)(2,1)S(1)}, bf16[2,256,512]{2,1,0:T(8,128)(2,1)S(1)}, bf16[2,256,1024]{2,1,0:T(8,128)(2,1)S(1)}) custom-call(s32[4]{0:T(128)S(1)} %pad_add_fusion.place, bf16[4,512,128]{2,1,0:T(8,128)(2,1)S(1)} %pad_maximum_fusion.refs_0_, bf16[4,512,128]{2,1,0:T(8,128)(2,1)S(1)} %collective-permute-done.3.refs_1_, ...), custom_call_target="tpu_custom_call" | custom-call | flops 1024 | bytes 1024 | tf_op jit(solution)/shard_map/product/pallas_call | solution.py:181
  93.2 10.7 %collective-permute-done.16.refs_6_ = bf16[4,128,512]{2,1,0:T(8,128)(2,1)S(1)} collective-permute-done((bf16[4,128,512]{2,1,0:T(8,128)(2,1)S(1)}, bf16[4,128,512]{2,1,0:T(8,128)(2,1)S(1)}, u32[]{:S(2)}, u32[]{:S(2)}) %collective-permute-start.16) | collective-permute-done | bytes 524320 | tf_op jit(solution)/shard_map/ppermute | solution.py:285
  107.4 3.3 %collective-permute-start.25 = (bf16[4,512,128]{2,1,0:T(8,128)(2,1)S(1)}, bf16[4,512,128]{2,1,0:T(8,128)(2,1)S(1)}, u32[]{:S(2)}, u32[]{:S(2)}) collective-permute-start(bf16[4,512,128]{2,1,0:T(8,128)(2,1)S(1)} %pad_maximum_fusion.1.refs_0_), channel_id=1, source_target_pairs={{0,2},{1,3},{2,0},{3,1},{4,6},{5,7},{6,4},{7,5},{8,10},{9,11},{10,... | collective-permute-start | bytes 1572872 | tf_op jit(solution)/shard_map/ppermute | solution.py:288
  110.8 3.0 %collective-permute-start.31 = (bf16[2,256,512]{2,1,0:T(8,128)(2,1)S(1)}, bf16[2,256,512]{2,1,0:T(8,128)(2,1)S(1)}, u32[]{:S(2)}, u32[]{:S(2)}) collective-permute-start(bf16[2,256,512]{2,1,0:T(8,128)(2,1)S(1)} %get-tuple-element.54), channel_id=1, source_target_pairs={{0,24},{16,0},{8,16},{24,8},{1,25},{17,1},{9,17},{25,9},{2,26},{18... | collective-permute-start | bytes 1572872 | tf_op jit(solution)/shard_map/ppermute | solution.py:236
  113.8 7.5 %product.5 = (bf16[2,256,512]{2,1,0:T(8,128)(2,1)S(1)}, bf16[2,256,512]{2,1,0:T(8,128)(2,1)S(1)}, bf16[2,256,1024]{2,1,0:T(8,128)(2,1)S(1)}) custom-call(s32[4]{0:T(128)S(1)} %pad_add_fusion.place, bf16[4,512,128]{2,1,0:T(8,128)(2,1)S(1)} %pad_maximum_fusion.refs_0_, bf16[4,512,128]{2,1,0:T(8,128)(2,1)S(1)} %collective-permute-done.3.refs_1_, ...), custom_call_target="tpu_custom_call" | custom-call | flops 1024 | bytes 1024 | tf_op jit(solution)/shard_map/product/pallas_call | solution.py:181
  121.4 3.2 %collective-permute-start.27 = (bf16[2,256,512]{2,1,0:T(8,128)(2,1)S(1)}, bf16[2,256,512]{2,1,0:T(8,128)(2,1)S(1)}, u32[]{:S(2)}, u32[]{:S(2)}) collective-permute-start(bf16[2,256,512]{2,1,0:T(8,128)(2,1)S(1)} %get-tuple-element.50), channel_id=1, source_target_pairs={{0,24},{16,0},{8,16},{24,8},{1,25},{17,1},{9,17},{25,9},{2,26},{18... | collective-permute-start | bytes 1572872 | tf_op jit(solution)/shard_map/ppermute | solution.py:236
  125.9 7.7 %product.7 = (bf16[2,256,1024]{2,1,0:T(8,128)(2,1)S(1)}, bf16[2,256,1024]{2,1,0:T(8,128)(2,1)S(1)}) custom-call(s32[4]{0:T(128)S(1)} %pad_add_fusion.place, bf16[4,512,128]{2,1,0:T(8,128)(2,1)S(1)} %pad_maximum_fusion.1.refs_0_, bf16[4,512,128]{2,1,0:T(8,128)(2,1)S(1)} %collective-permute-done.23.refs_1_, ...), custom_call_target="tpu_custom_call" | custom-call | flops 1024 | bytes 1024 | tf_op jit(solution)/shard_map/product/pallas_call | solution.py:181
  135.3 2.1 %collective-permute-start.33 = (bf16[2,256,1024]{2,1,0:T(8,128)(2,1)S(1)}, bf16[2,256,1024]{2,1,0:T(8,128)(2,1)S(1)}, u32[]{:S(2)}, u32[]{:S(2)}) collective-permute-start(bf16[2,256,1024]{2,1,0:T(8,128)(2,1)S(1)} %get-tuple-element.56), channel_id=1, source_target_pairs={{0,24},{16,0},{8,16},{24,8},{1,25},{17,1},{9,17},{25,9},{2,26},{18... | collective-permute-start | bytes 3145736 | tf_op jit(solution)/shard_map/ppermute | solution.py:236
  137.5 7.7 %product.6 = (bf16[2,256,1024]{2,1,0:T(8,128)(2,1)S(1)}, bf16[2,256,1024]{2,1,0:T(8,128)(2,1)S(1)}) custom-call(s32[4]{0:T(128)S(1)} %pad_add_fusion.place, bf16[4,512,128]{2,1,0:T(8,128)(2,1)S(1)} %pad_maximum_fusion.1.refs_0_, bf16[4,512,128]{2,1,0:T(8,128)(2,1)S(1)} %collective-permute-done.23.refs_1_, ...), custom_call_target="tpu_custom_call" | custom-call | flops 1024 | bytes 1024 | tf_op jit(solution)/shard_map/product/pallas_call | solution.py:181
  145.3 3.2 %collective-permute-start.29 = (bf16[2,256,1024]{2,1,0:T(8,128)(2,1)S(1)}, bf16[2,256,1024]{2,1,0:T(8,128)(2,1)S(1)}, u32[]{:S(2)}, u32[]{:S(2)}) collective-permute-start(bf16[2,256,1024]{2,1,0:T(8,128)(2,1)S(1)} %get-tuple-element.52), channel_id=1, source_target_pairs={{0,24},{16,0},{8,16},{24,8},{1,25},{17,1},{9,17},{25,9},{2,26},{18... | collective-permute-start | bytes 3145736 | tf_op jit(solution)/shard_map/ppermute | solution.py:236
  148.5 13.0 %collective-permute-done.32.b = bf16[2,256,1024]{2,1,0:T(8,128)(2,1)S(1)} collective-permute-done((bf16[2,256,1024]{2,1,0:T(8,128)(2,1)S(1)}, bf16[2,256,1024]{2,1,0:T(8,128)(2,1)S(1)}, u32[]{:S(2)}, u32[]{:S(2)}) %collective-permute-start.32) | collective-permute-done | bytes 1048608 | tf_op jit(solution)/shard_map/ppermute | solution.py:236
  163.4 17.9 %collective-permute-done.28.b = bf16[2,256,1024]{2,1,0:T(8,128)(2,1)S(1)} collective-permute-done((bf16[2,256,1024]{2,1,0:T(8,128)(2,1)S(1)}, bf16[2,256,1024]{2,1,0:T(8,128)(2,1)S(1)}, u32[]{:S(2)}, u32[]{:S(2)}) %collective-permute-start.28) | collective-permute-done | bytes 1048608 | tf_op jit(solution)/shard_map/ppermute | solution.py:236
  (82 shorter events, 30.8 us)
Async XLA Ops:
  33.4 13.4 %collective-permute-start.8 = (bf16[128,1024]{1,0:T(8,128)(2,1)S(1)}, bf16[128,1024]{1,0:T(8,128)(2,1)S(1)}, u32[]{:S(2)}, u32[]{:S(2)}) collective-permute-start(bf16[128,1024]{1,0:T(8,128)(2,1)S(1)} %get-tuple-element.38), channel_id=1, source_target_pairs={{0,3},{1,0},{2,1},{3,2},{4,7},{5,4},{6,5},{7,6},{8,11},{9,8},{10,9... | collective-permute-start | bytes 786440 | tf_op jit(solution)/shard_map/ppermute | solution.py:269
  35.9 13.8 %collective-permute-start = (bf16[1024,128]{1,0:T(8,128)(2,1)S(1)}, bf16[1024,128]{1,0:T(8,128)(2,1)S(1)}, u32[]{:S(2)}, u32[]{:S(2)}) collective-permute-start(bf16[1024,128]{1,0:T(8,128)(2,1)S(1)} %get-tuple-element.32), channel_id=1, source_target_pairs={{0,32},{32,64},{64,96},{96,0},{1,33},{33,65},{65,97},{97,1},{2,34}... | collective-permute-start | bytes 786440 | tf_op jit(solution)/shard_map/ppermute | solution.py:268
  37.4 13.5 %collective-permute-start.1 = (bf16[1024,128]{1,0:T(8,128)(2,1)S(1)}, bf16[1024,128]{1,0:T(8,128)(2,1)S(1)}, u32[]{:S(2)}, u32[]{:S(2)}) collective-permute-start(bf16[1024,128]{1,0:T(8,128)(2,1)S(1)} %get-tuple-element.33), channel_id=1, source_target_pairs={{0,64},{32,96},{64,0},{96,32},{1,65},{33,97},{65,1},{97,33},{2,66}... | collective-permute-start | bytes 786440 | tf_op jit(solution)/shard_map/ppermute | solution.py:268
  46.8 14.9 %collective-permute-start.10 = (bf16[4,128,512]{2,1,0:T(8,128)(2,1)S(1)}, bf16[4,128,512]{2,1,0:T(8,128)(2,1)S(1)}, u32[]{:S(2)}, u32[]{:S(2)}) collective-permute-start(bf16[4,128,512]{2,1,0:T(8,128)(2,1)S(1)} %pad_maximum_fusion.3.refs_4_), channel_id=1, source_target_pairs={{0,96},{32,0},{64,32},{96,64},{1,97},{33,1},{65,33},{97,65},{2,98}... | collective-permute-start | bytes 1572872 | tf_op jit(solution)/shard_map/ppermute | solution.py:275
  49.7 14.0 %collective-permute-start.9 = (bf16[4,128,512]{2,1,0:T(8,128)(2,1)S(1)}, bf16[4,128,512]{2,1,0:T(8,128)(2,1)S(1)}, u32[]{:S(2)}, u32[]{:S(2)}) collective-permute-start(bf16[4,128,512]{2,1,0:T(8,128)(2,1)S(1)} %pad_maximum_fusion.3.refs_4_), channel_id=1, source_target_pairs={{0,32},{32,64},{64,96},{96,0},{1,33},{33,65},{65,97},{97,1},{2,34}... | collective-permute-start | bytes 1572872 | tf_op jit(solution)/shard_map/ppermute | solution.py:275
  49.7 15.6 %collective-permute-start.12 = (bf16[4,128,512]{2,1,0:T(8,128)(2,1)S(1)}, bf16[4,128,512]{2,1,0:T(8,128)(2,1)S(1)}, u32[]{:S(2)}, u32[]{:S(2)}) collective-permute-start(bf16[4,128,512]{2,1,0:T(8,128)(2,1)S(1)} %pad_maximum_fusion.3.refs_4_), channel_id=1, source_target_pairs={{0,4},{4,0},{1,5},{5,1},{2,6},{6,2},{3,7},{7,3},{8,12},{12,8},{9,1... | collective-permute-start | bytes 1572872 | tf_op jit(solution)/shard_map/ppermute | solution.py:244
  52.3 14.8 %collective-permute-start.4 = (bf16[4,512,128]{2,1,0:T(8,128)(2,1)S(1)}, bf16[4,512,128]{2,1,0:T(8,128)(2,1)S(1)}, u32[]{:S(2)}, u32[]{:S(2)}) collective-permute-start(bf16[4,512,128]{2,1,0:T(8,128)(2,1)S(1)} %pad_maximum_fusion.refs_0_), channel_id=1, source_target_pairs={{0,2},{1,3},{2,0},{3,1},{4,6},{5,7},{6,4},{7,5},{8,10},{9,11},{10,... | collective-permute-start | bytes 1572872 | tf_op jit(solution)/shard_map/ppermute | solution.py:276
  63.7 13.4 %collective-permute-start.11 = (bf16[4,128,512]{2,1,0:T(8,128)(2,1)S(1)}, bf16[4,128,512]{2,1,0:T(8,128)(2,1)S(1)}, u32[]{:S(2)}, u32[]{:S(2)}) collective-permute-start(bf16[4,128,512]{2,1,0:T(8,128)(2,1)S(1)} %pad_maximum_fusion.3.refs_4_), channel_id=1, source_target_pairs={{0,64},{32,96},{64,0},{96,32},{1,65},{33,97},{65,1},{97,33},{2,66}... | collective-permute-start | bytes 1572872 | tf_op jit(solution)/shard_map/ppermute | solution.py:278
  65.3 15.3 %collective-permute-start.3 = (bf16[4,512,128]{2,1,0:T(8,128)(2,1)S(1)}, bf16[4,512,128]{2,1,0:T(8,128)(2,1)S(1)}, u32[]{:S(2)}, u32[]{:S(2)}) collective-permute-start(bf16[4,512,128]{2,1,0:T(8,128)(2,1)S(1)} %pad_maximum_fusion.refs_0_), channel_id=1, source_target_pairs={{0,1},{1,2},{2,3},{3,0},{4,5},{5,6},{6,7},{7,4},{8,9},{9,10},{10,1... | collective-permute-start | bytes 1572872 | tf_op jit(solution)/shard_map/ppermute | solution.py:274
  67.1 15.4 %collective-permute-start.5 = (bf16[4,512,128]{2,1,0:T(8,128)(2,1)S(1)}, bf16[4,512,128]{2,1,0:T(8,128)(2,1)S(1)}, u32[]{:S(2)}, u32[]{:S(2)}) collective-permute-start(bf16[4,512,128]{2,1,0:T(8,128)(2,1)S(1)} %pad_maximum_fusion.refs_0_), channel_id=1, source_target_pairs={{0,3},{1,0},{2,1},{3,2},{4,7},{5,4},{6,5},{7,6},{8,11},{9,8},{10,9... | collective-permute-start | bytes 1572872 | tf_op jit(solution)/shard_map/ppermute | solution.py:274
  77.1 16.1 %collective-permute-start.15 = (bf16[4,128,512]{2,1,0:T(8,128)(2,1)S(1)}, bf16[4,128,512]{2,1,0:T(8,128)(2,1)S(1)}, u32[]{:S(2)}, u32[]{:S(2)}) collective-permute-start(bf16[4,128,512]{2,1,0:T(8,128)(2,1)S(1)} %pad_maximum_fusion.2.refs_4_), channel_id=1, source_target_pairs={{0,32},{32,64},{64,96},{96,0},{1,33},{33,65},{65,97},{97,1},{2,34}... | collective-permute-start | bytes 1572872 | tf_op jit(solution)/shard_map/ppermute | solution.py:284
  79.8 24.2 %collective-permute-start.16 = (bf16[4,128,512]{2,1,0:T(8,128)(2,1)S(1)}, bf16[4,128,512]{2,1,0:T(8,128)(2,1)S(1)}, u32[]{:S(2)}, u32[]{:S(2)}) collective-permute-start(bf16[4,128,512]{2,1,0:T(8,128)(2,1)S(1)} %pad_maximum_fusion.2.refs_4_), channel_id=1, source_target_pairs={{0,64},{32,96},{64,0},{96,32},{1,65},{33,97},{65,1},{97,33},{2,66}... | collective-permute-start | bytes 1572872 | tf_op jit(solution)/shard_map/ppermute | solution.py:285
  80.7 23.8 %collective-permute-start.17 = (bf16[4,128,512]{2,1,0:T(8,128)(2,1)S(1)}, bf16[4,128,512]{2,1,0:T(8,128)(2,1)S(1)}, u32[]{:S(2)}, u32[]{:S(2)}) collective-permute-start(bf16[4,128,512]{2,1,0:T(8,128)(2,1)S(1)} %pad_maximum_fusion.2.refs_4_), channel_id=1, source_target_pairs={{0,96},{32,0},{64,32},{96,64},{1,97},{33,1},{65,33},{97,65},{2,98}... | collective-permute-start | bytes 1572872 | tf_op jit(solution)/shard_map/ppermute | solution.py:284
  82.5 22.5 %collective-permute-start.23 = (bf16[4,512,128]{2,1,0:T(8,128)(2,1)S(1)}, bf16[4,512,128]{2,1,0:T(8,128)(2,1)S(1)}, u32[]{:S(2)}, u32[]{:S(2)}) collective-permute-start(bf16[4,512,128]{2,1,0:T(8,128)(2,1)S(1)} %pad_maximum_fusion.1.refs_0_), channel_id=1, source_target_pairs={{0,1},{1,2},{2,3},{3,0},{4,5},{5,6},{6,7},{7,4},{8,9},{9,10},{10,1... | collective-permute-start | bytes 1572872 | tf_op jit(solution)/shard_map/ppermute | solution.py:283
  82.5 23.0 %collective-permute-start.24 = (bf16[4,512,128]{2,1,0:T(8,128)(2,1)S(1)}, bf16[4,512,128]{2,1,0:T(8,128)(2,1)S(1)}, u32[]{:S(2)}, u32[]{:S(2)}) collective-permute-start(bf16[4,512,128]{2,1,0:T(8,128)(2,1)S(1)} %pad_maximum_fusion.1.refs_0_), channel_id=1, source_target_pairs={{0,3},{1,0},{2,1},{3,2},{4,7},{5,4},{6,5},{7,6},{8,11},{9,8},{10,9... | collective-permute-start | bytes 1572872 | tf_op jit(solution)/shard_map/ppermute | solution.py:283
  105.5 19.1 %collective-permute-start.30 = (bf16[2,256,512]{2,1,0:T(8,128)(2,1)S(1)}, bf16[2,256,512]{2,1,0:T(8,128)(2,1)S(1)}, u32[]{:S(2)}, u32[]{:S(2)}) collective-permute-start(bf16[2,256,512]{2,1,0:T(8,128)(2,1)S(1)} %get-tuple-element.41), channel_id=1, source_target_pairs={{0,16},{16,8},{8,24},{24,0},{1,17},{17,9},{9,25},{25,1},{2,18},{18... | collective-permute-start | bytes 1572872 | tf_op jit(solution)/shard_map/ppermute | solution.py:236
  107.4 17.2 %collective-permute-start.25 = (bf16[4,512,128]{2,1,0:T(8,128)(2,1)S(1)}, bf16[4,512,128]{2,1,0:T(8,128)(2,1)S(1)}, u32[]{:S(2)}, u32[]{:S(2)}) collective-permute-start(bf16[4,512,128]{2,1,0:T(8,128)(2,1)S(1)} %pad_maximum_fusion.1.refs_0_), channel_id=1, source_target_pairs={{0,2},{1,3},{2,0},{3,1},{4,6},{5,7},{6,4},{7,5},{8,10},{9,11},{10,... | collective-permute-start | bytes 1572872 | tf_op jit(solution)/shard_map/ppermute | solution.py:288
  110.8 15.1 %collective-permute-start.31 = (bf16[2,256,512]{2,1,0:T(8,128)(2,1)S(1)}, bf16[2,256,512]{2,1,0:T(8,128)(2,1)S(1)}, u32[]{:S(2)}, u32[]{:S(2)}) collective-permute-start(bf16[2,256,512]{2,1,0:T(8,128)(2,1)S(1)} %get-tuple-element.54), channel_id=1, source_target_pairs={{0,24},{16,0},{8,16},{24,8},{1,25},{17,1},{9,17},{25,9},{2,26},{18... | collective-permute-start | bytes 1572872 | tf_op jit(solution)/shard_map/ppermute | solution.py:236
  121.3 16.2 %collective-permute-start.26 = (bf16[2,256,512]{2,1,0:T(8,128)(2,1)S(1)}, bf16[2,256,512]{2,1,0:T(8,128)(2,1)S(1)}, u32[]{:S(2)}, u32[]{:S(2)}) collective-permute-start(bf16[2,256,512]{2,1,0:T(8,128)(2,1)S(1)} %get-tuple-element.49), channel_id=1, source_target_pairs={{0,16},{16,8},{8,24},{24,0},{1,17},{17,9},{9,25},{25,1},{2,18},{18... | collective-permute-start | bytes 1572872 | tf_op jit(solution)/shard_map/ppermute | solution.py:236
  121.4 16.1 %collective-permute-start.27 = (bf16[2,256,512]{2,1,0:T(8,128)(2,1)S(1)}, bf16[2,256,512]{2,1,0:T(8,128)(2,1)S(1)}, u32[]{:S(2)}, u32[]{:S(2)}) collective-permute-start(bf16[2,256,512]{2,1,0:T(8,128)(2,1)S(1)} %get-tuple-element.50), channel_id=1, source_target_pairs={{0,24},{16,0},{8,16},{24,8},{1,25},{17,1},{9,17},{25,9},{2,26},{18... | collective-permute-start | bytes 1572872 | tf_op jit(solution)/shard_map/ppermute | solution.py:236
  133.6 27.8 %collective-permute-start.32 = (bf16[2,256,1024]{2,1,0:T(8,128)(2,1)S(1)}, bf16[2,256,1024]{2,1,0:T(8,128)(2,1)S(1)}, u32[]{:S(2)}, u32[]{:S(2)}) collective-permute-start(bf16[2,256,1024]{2,1,0:T(8,128)(2,1)S(1)} %get-tuple-element.55), channel_id=1, source_target_pairs={{0,16},{16,8},{8,24},{24,0},{1,17},{17,9},{9,25},{25,1},{2,18},{18... | collective-permute-start | bytes 3145736 | tf_op jit(solution)/shard_map/ppermute | solution.py:236
  135.3 26.1 %collective-permute-start.33 = (bf16[2,256,1024]{2,1,0:T(8,128)(2,1)S(1)}, bf16[2,256,1024]{2,1,0:T(8,128)(2,1)S(1)}, u32[]{:S(2)}, u32[]{:S(2)}) collective-permute-start(bf16[2,256,1024]{2,1,0:T(8,128)(2,1)S(1)} %get-tuple-element.56), channel_id=1, source_target_pairs={{0,24},{16,0},{8,16},{24,8},{1,25},{17,1},{9,17},{25,9},{2,26},{18... | collective-permute-start | bytes 3145736 | tf_op jit(solution)/shard_map/ppermute | solution.py:236
  145.2 36.1 %collective-permute-start.28 = (bf16[2,256,1024]{2,1,0:T(8,128)(2,1)S(1)}, bf16[2,256,1024]{2,1,0:T(8,128)(2,1)S(1)}, u32[]{:S(2)}, u32[]{:S(2)}) collective-permute-start(bf16[2,256,1024]{2,1,0:T(8,128)(2,1)S(1)} %get-tuple-element.51), channel_id=1, source_target_pairs={{0,16},{16,8},{8,24},{24,0},{1,17},{17,9},{9,25},{25,1},{2,18},{18... | collective-permute-start | bytes 3145736 | tf_op jit(solution)/shard_map/ppermute | solution.py:236
  145.3 36.0 %collective-permute-start.29 = (bf16[2,256,1024]{2,1,0:T(8,128)(2,1)S(1)}, bf16[2,256,1024]{2,1,0:T(8,128)(2,1)S(1)}, u32[]{:S(2)}, u32[]{:S(2)}) collective-permute-start(bf16[2,256,1024]{2,1,0:T(8,128)(2,1)S(1)} %get-tuple-element.52), channel_id=1, source_target_pairs={{0,24},{16,0},{8,16},{24,8},{1,25},{17,1},{9,17},{25,9},{2,26},{18... | collective-permute-start | bytes 3145736 | tf_op jit(solution)/shard_map/ppermute | solution.py:236
  (15 other events, 129.0 us)
